TPU v7x, 32 devices: a whole 2x2x4 slice. The times are simulated.
32 devices in a mesh: rep: 2 (over x), shard: 16 (over z, y, core).
Axes of the slice: x: 2, y: 2, z: 4, core: 2. Of those that a mesh axis runs over, the one named last changes fastest.
Arguments:
- images: bfloat16 [64, 1024, 512], P(('rep', 'shard')), may hold values from -6 to 6
- embeds: bfloat16 [64, 1024], P(('rep', 'shard')), may hold values from -6 to 6
- cotangent: bfloat16 [64, 1024, 512], P(('rep', 'shard')), may hold values from -6 to 6
- counts: int32 [32, 2], P(('rep', 'shard')), may hold values from 0 to 2, as said below
- bucket_weight: float32 [2], replicated, may hold values from 0.5 to 2
- owner: int32 [32], replicated, may hold values from 0 to 31, as said below
- master: float32 [32, 512, 512], P('shard')
- first_moment: float32 [32, 512, 512], P('shard')
- second_moment: float32 [32, 512, 512], P('shard')
- left_basis: float32 [32, 512, 512], P('shard'), as said below
- right_basis: float32 [32, 512, 512], P('shard'), as said below
- vec_master: float32 [13, 512], P(None, 'shard')
- vec_first: float32 [13, 512], P(None, 'shard')
- vec_second: float32 [13, 512], P(None, 'shard')
Outputs:
- block_out: bfloat16 [64, 1024, 512], P(('rep', 'shard'))
- grad_images: float32 [64, 1024, 512], P(('rep', 'shard'))
- grad_embeds: float32 [64, 1024], P(('rep', 'shard'))
- new_first: float32 [32, 512, 512], P('shard')
- new_second: float32 [32, 512, 512], P('shard')
- new_master: float32 [32, 512, 512], P('shard')
- master_low: bfloat16 [32, 512, 512], P('shard')
- vec_first_new: float32 [13, 512], P(None, 'shard')
- vec_second_new: float32 [13, 512], P(None, 'shard')
- vec_master_new: float32 [13, 512], P(None, 'shard')
- vec_low: bfloat16 [13, 512], P(None, 'shard')
Inputs may be any that keep to these rules, and one draw needn't show every extreme that they name: `counts`: row d gives device d's images of bucket 0 and of bucket 1; they fill its first slots in that order, the rest of its 2 slots are unused; every row sums to 1 or more and some row sums to 2. A permutation of the 32 slots; block b, for b < 26, lives in slot owner[b]; the other slots hold no block. `left_basis`: each slot's matrix is orthogonal. `right_basis`: each slot's matrix is orthogonal.
All inputs are finite; a program needn't handle non-finite values.
Results may differ from a plain program's by a relative error of at most 0.025.
Values may be sent and summed in bfloat16 or wider, within the bound.
No kernel may reach another device: no remote copies, remote signals or barrier semaphores. Data moves between devices by JAX's collectives and lax.ppermute only.
A program may use at most 320 MiB of HBM per device.

v0:
```python
import math

import jax
import jax.numpy as jnp
from jax import lax
from jax.sharding import PartitionSpec as P

C = 512
EMB = 1024
HEADS = 8
HEAD = 64
GROUPS = 32
SIDE = 32
HW = 1024
BLOCKS = 26
VECS = 13
STEP = 2


EPS_NORM = 1e-05
ADAM_EPS = 1e-08
MOMENT_DECAY = 0.5
WEIGHT_DECAY = 0.01
VECTOR_RATE = 0.2
PRECISE = lax.Precision.HIGHEST


def block_spread(block_index):
    return jnp.where(
        block_index < 18,
        (9.0 * C) ** (-0.5),
        jnp.where(
            block_index < 22,
            EMB ** (-0.5),
            jnp.where(
                block_index < 24,
                1.25 * C ** (-0.5),
                jnp.where(
                    block_index < 25,
                    C ** (-0.5),
                    jnp.where(block_index < 26, 0.295 * (HW / C) ** 0.5, C ** (-0.5)),
                ),
            ),
        ),
    )


def norm_forward(values_in):
    row_count = values_in.shape[0]
    grouped = values_in.reshape(row_count, GROUPS, C // GROUPS)
    group_mean = jnp.mean(grouped, axis=(0, 2), keepdims=True)
    centered = grouped - group_mean
    group_var = jnp.mean(centered * centered, axis=(0, 2), keepdims=True)
    inv_std = lax.rsqrt(group_var + EPS_NORM)
    return ((centered * inv_std).reshape(row_count, C), inv_std)


def norm_back(normed, inv_std, grad_in):
    row_count = normed.shape[0]
    normed_groups = normed.reshape(row_count, GROUPS, C // GROUPS)
    grad_groups = grad_in.reshape(row_count, GROUPS, C // GROUPS)
    mean_grad = jnp.mean(grad_groups, axis=(0, 2), keepdims=True)
    mean_cross = jnp.mean(grad_groups * normed_groups, axis=(0, 2), keepdims=True)
    return (inv_std * (grad_groups - mean_grad - normed_groups * mean_cross)).reshape(row_count, C)


def silu_slope(inputs):
    sigma_val = jax.nn.sigmoid(inputs)
    return sigma_val * (1.0 + inputs * (1.0 - sigma_val))


def pad_grid(activation):
    return jnp.pad(activation.reshape(SIDE, SIDE, C), ((1, 1), (1, 1), (0, 0)))


def tap_view(padded, tap_index):
    row_off = tap_index // 3
    col_off = tap_index % 3
    return padded[row_off : row_off + SIDE, col_off : col_off + SIDE].reshape(HW, C)


def conv_apply(padded, taps):
    total = jnp.dot(tap_view(padded, 0), taps[0], preferred_element_type=jnp.float32)
    for tap_index in range(1, 9):
        total = total + jnp.dot(
            tap_view(padded, tap_index), taps[tap_index], preferred_element_type=jnp.float32
        )
    return total


def conv_back_data(padded_grad, taps):
    dims = (((1,), (1,)), ((), ()))
    total = lax.dot_general(
        tap_view(padded_grad, 0), taps[8], dims, preferred_element_type=jnp.float32
    )
    for tap_index in range(1, 9):
        total = total + lax.dot_general(
            tap_view(padded_grad, tap_index),
            taps[8 - tap_index],
            dims,
            preferred_element_type=jnp.float32,
        )
    return total


def conv_back_taps(padded, grad_rows):
    dims = (((0,), (0,)), ((), ()))
    return jnp.stack(
        [
            lax.dot_general(
                tap_view(padded, tap_index), grad_rows, dims, preferred_element_type=jnp.float32
            )
            for tap_index in range(9)
        ]
    )


def attend(queries, keys_in, values):
    row_count = queries.shape[0]
    block_rows = min(512, row_count)
    key_heads = keys_in.reshape(row_count, HEADS, HEAD)
    value_heads = values.reshape(row_count, HEADS, HEAD)
    scale_factor = 1.0 / math.sqrt(HEAD)

    def one_block(row_start):
        query_block = lax.dynamic_slice_in_dim(queries, row_start, block_rows, 0).reshape(
            block_rows, HEADS, HEAD
        )
        scores = (
            jnp.einsum("qhd,khd->hqk", query_block, key_heads, preferred_element_type=jnp.float32)
            * scale_factor
        )
        row_max = jnp.max(scores, axis=-1, keepdims=True)
        exponent = jnp.exp(scores - row_max)
        row_total = jnp.sum(exponent, axis=-1, keepdims=True)
        probabilities = (exponent / row_total).astype(jnp.bfloat16)
        mixed_rows = jnp.einsum(
            "hqk,khd->qhd", probabilities, value_heads, preferred_element_type=jnp.float32
        )
        return (mixed_rows.reshape(block_rows, C), (row_max + jnp.log(row_total))[..., 0])

    starts = jnp.arange(row_count // block_rows, dtype=jnp.int32) * block_rows
    mixed_rows, log_total = lax.map(one_block, starts)
    return (mixed_rows.reshape(row_count, C), log_total)


def attend_back(queries, keys_in, values, log_total, grad_attended):
    row_count = queries.shape[0]
    block_rows = min(512, row_count)
    key_heads = keys_in.reshape(row_count, HEADS, HEAD)
    value_heads = values.reshape(row_count, HEADS, HEAD)
    scale_factor = 1.0 / math.sqrt(HEAD)

    def one_block(loop_state, inputs):
        grad_keys, grad_values = loop_state
        row_start, block_total = inputs
        query_block = lax.dynamic_slice_in_dim(queries, row_start, block_rows, 0).reshape(
            block_rows, HEADS, HEAD
        )
        grad_block = lax.dynamic_slice_in_dim(grad_attended, row_start, block_rows, 0).reshape(
            block_rows, HEADS, HEAD
        )
        scores = (
            jnp.einsum("qhd,khd->hqk", query_block, key_heads, preferred_element_type=jnp.float32)
            * scale_factor
        )
        probabilities = jnp.exp(scores - block_total[..., None])
        grad_probs = jnp.einsum(
            "qhd,khd->hqk", grad_block, value_heads, preferred_element_type=jnp.float32
        )
        row_dot = jnp.sum(probabilities * grad_probs, axis=-1, keepdims=True)
        grad_scores = (probabilities * (grad_probs - row_dot)).astype(jnp.bfloat16)
        grad_query = (
            jnp.einsum("hqk,khd->qhd", grad_scores, key_heads, preferred_element_type=jnp.float32)
            * scale_factor
        )
        grad_keys = (
            grad_keys
            + jnp.einsum(
                "hqk,qhd->khd", grad_scores, query_block, preferred_element_type=jnp.float32
            )
            * scale_factor
        )
        grad_values = grad_values + jnp.einsum(
            "hqk,qhd->khd",
            probabilities.astype(jnp.bfloat16),
            grad_block,
            preferred_element_type=jnp.float32,
        )
        return ((grad_keys, grad_values), grad_query.reshape(block_rows, C))

    starts = jnp.arange(row_count // block_rows, dtype=jnp.int32) * block_rows
    empty_heads = jnp.zeros((row_count, HEADS, HEAD), jnp.float32)
    (grad_keys, grad_values), grad_query = lax.scan(
        one_block, (empty_heads, empty_heads), (starts, log_total)
    )
    return (
        grad_query.reshape(row_count, C),
        grad_keys.reshape(row_count, C),
        grad_values.reshape(row_count, C),
    )


def shards(
    images,
    embeds,
    cotangent,
    counts,
    bucket_weight,
    owner,
    master,
    first_moment,
    second_moment,
    left_basis,
    right_basis,
    vec_master,
    vec_first,
    vec_second,
):
    mat_dev = master.shape[0]
    mats_all = mat_dev * lax.axis_size("shard")
    slot_weights, vec_full = (
        lax.all_gather(master.astype(jnp.bfloat16), "shard", axis=0, tiled=True),
        lax.all_gather(vec_master.astype(jnp.bfloat16), "shard", axis=1, tiled=True),
    )
    blocks = slot_weights[owner[:BLOCKS]]
    vectors = vec_full.astype(jnp.float32)
    conv_one = blocks[0:9]
    conv_two = blocks[9:18]
    embed_maps = blocks[18:22].astype(jnp.float32)
    qkv_map = jnp.concatenate([blocks[22], blocks[23], blocks[24]], axis=1)
    proj_map = blocks[25]
    bucket_zero = counts[0, 0]
    live_count = counts[0, 0] + counts[0, 1]

    def one_image(slot_index, loop_state):
        grad_blocks, grad_vectors, outputs, grad_images, grad_embeds = loop_state
        image_rows = lax.dynamic_index_in_dim(images, slot_index, 0, keepdims=False).astype(
            jnp.float32
        )
        embed_row = lax.dynamic_index_in_dim(embeds, slot_index, 0, keepdims=False).astype(
            jnp.float32
        )
        weight = jnp.where(slot_index < bucket_zero, bucket_weight[0], bucket_weight[1])
        grad_out = (
            lax.dynamic_index_in_dim(cotangent, slot_index, 0, keepdims=False).astype(jnp.float32)
            * weight
        )
        normed_one, inv_one = norm_forward(image_rows)
        pre_one = normed_one * vectors[0] + vectors[1]
        padded_one = pad_grid(jax.nn.silu(pre_one).astype(jnp.bfloat16))
        hidden_one = conv_apply(padded_one, conv_one) + vectors[2]
        emb_act = jax.nn.silu(embed_row).astype(jnp.bfloat16).astype(jnp.float32)
        ada_scale = (
            jnp.dot(emb_act[:C], embed_maps[0], precision=PRECISE)
            + jnp.dot(emb_act[C:], embed_maps[1], precision=PRECISE)
            + vectors[3]
        )
        ada_shift = (
            jnp.dot(emb_act[:C], embed_maps[2], precision=PRECISE)
            + jnp.dot(emb_act[C:], embed_maps[3], precision=PRECISE)
            + vectors[4]
        )
        normed_two, inv_two = norm_forward(hidden_one)
        affine_two = normed_two * vectors[5] + vectors[6]
        pre_two = affine_two * (1.0 + ada_scale) + ada_shift
        padded_two = pad_grid(jax.nn.silu(pre_two).astype(jnp.bfloat16))
        hidden_two = conv_apply(padded_two, conv_two) + vectors[7]
        resid = image_rows + hidden_two
        normed_three, inv_three = norm_forward(resid)
        affine_three = (normed_three * vectors[8] + vectors[9]).astype(jnp.bfloat16)
        projected = jnp.dot(affine_three, qkv_map, preferred_element_type=jnp.float32)
        queries = (projected[:, :C] + vectors[10]).astype(jnp.bfloat16)
        keys_in = projected[:, C : 2 * C].astype(jnp.bfloat16)
        values = (projected[:, 2 * C :] + vectors[11]).astype(jnp.bfloat16)
        attended, log_total = attend(queries, keys_in, values)
        attended = attended.astype(jnp.bfloat16)
        result_rows = (
            resid + jnp.dot(attended, proj_map, preferred_element_type=jnp.float32) + vectors[12]
        )
        grad_low = grad_out.astype(jnp.bfloat16)
        row_dims = (((0,), (0,)), ((), ()))
        grad_proj = lax.dot_general(
            attended, grad_low, row_dims, preferred_element_type=jnp.float32
        )
        grad_attended = lax.dot_general(
            grad_low, proj_map, (((1,), (1,)), ((), ())), preferred_element_type=jnp.float32
        ).astype(jnp.bfloat16)
        grad_query, grad_keys, grad_values = attend_back(
            queries, keys_in, values, log_total, grad_attended
        )
        grad_qkv = jnp.concatenate([grad_query, grad_keys, grad_values], axis=1).astype(
            jnp.bfloat16
        )
        grad_qkv_map = lax.dot_general(
            affine_three, grad_qkv, row_dims, preferred_element_type=jnp.float32
        )
        qkv_sums = jnp.sum(grad_qkv.astype(jnp.float32), axis=0)
        grad_three = lax.dot_general(
            grad_qkv, qkv_map, (((1,), (1,)), ((), ())), preferred_element_type=jnp.float32
        )
        grad_resid = grad_out + norm_back(normed_three, inv_three, grad_three * vectors[8])
        grad_hidden_two = grad_resid.astype(jnp.bfloat16)
        grad_conv_two = conv_back_taps(padded_two, grad_hidden_two)
        grad_act_two = conv_back_data(pad_grid(grad_hidden_two), conv_two)
        grad_pre_two = grad_act_two * silu_slope(pre_two)
        grad_scale = jnp.sum(grad_pre_two * affine_two, axis=0)
        grad_shift = jnp.sum(grad_pre_two, axis=0)
        grad_affine_two = grad_pre_two * (1.0 + ada_scale)
        grad_hidden_one = norm_back(normed_two, inv_two, grad_affine_two * vectors[5]).astype(
            jnp.bfloat16
        )
        grad_conv_one = conv_back_taps(padded_one, grad_hidden_one)
        grad_act_one = conv_back_data(pad_grid(grad_hidden_one), conv_one)
        grad_pre_one = grad_act_one * silu_slope(pre_one)
        grad_image = grad_resid + norm_back(normed_one, inv_one, grad_pre_one * vectors[0])
        grad_emb_act = jnp.concatenate(
            [
                jnp.dot(embed_maps[0], grad_scale, precision=PRECISE)
                + jnp.dot(embed_maps[2], grad_shift, precision=PRECISE),
                jnp.dot(embed_maps[1], grad_scale, precision=PRECISE)
                + jnp.dot(embed_maps[3], grad_shift, precision=PRECISE),
            ]
        )
        grad_embed = grad_emb_act * silu_slope(embed_row)
        emb_lower = emb_act[:C]
        emb_upper = emb_act[C:]
        grad_maps = jnp.stack(
            [
                jnp.outer(emb_lower, grad_scale),
                jnp.outer(emb_upper, grad_scale),
                jnp.outer(emb_lower, grad_shift),
                jnp.outer(emb_upper, grad_shift),
            ]
        )
        block_terms = jnp.concatenate(
            [
                grad_conv_one,
                grad_conv_two,
                grad_maps,
                grad_qkv_map.reshape(C, 3, C).transpose(1, 0, 2),
                grad_proj[None],
            ],
            axis=0,
        )
        vector_terms = jnp.stack(
            [
                jnp.sum(grad_pre_one * normed_one, axis=0),
                jnp.sum(grad_pre_one, axis=0),
                jnp.sum(grad_hidden_one.astype(jnp.float32), axis=0),
                grad_scale,
                grad_shift,
                jnp.sum(grad_affine_two * normed_two, axis=0),
                jnp.sum(grad_affine_two, axis=0),
                jnp.sum(grad_hidden_two.astype(jnp.float32), axis=0),
                jnp.sum(grad_three * normed_three, axis=0),
                jnp.sum(grad_three, axis=0),
                qkv_sums[:C],
                qkv_sums[2 * C :],
                jnp.sum(grad_low.astype(jnp.float32), axis=0),
            ]
        )
        outputs = lax.dynamic_update_index_in_dim(
            outputs, result_rows.astype(jnp.bfloat16), slot_index, 0
        )
        grad_images = lax.dynamic_update_index_in_dim(grad_images, grad_image, slot_index, 0)
        grad_embeds = lax.dynamic_update_index_in_dim(grad_embeds, grad_embed, slot_index, 0)
        return (
            grad_blocks + block_terms,
            grad_vectors + vector_terms,
            outputs,
            grad_images,
            grad_embeds,
        )

    start_state = (
        jnp.zeros((BLOCKS, C, C), jnp.float32),
        jnp.zeros((VECS, C), jnp.float32),
        jnp.zeros(images.shape, jnp.bfloat16),
        jnp.zeros(images.shape, jnp.float32),
        jnp.zeros(embeds.shape, jnp.float32),
    )
    grad_blocks, grad_vectors, outputs, grad_images, grad_embeds = lax.fori_loop(
        0, live_count, one_image, start_state
    )
    block_ids = jnp.arange(mats_all, dtype=jnp.int32)
    all_slots = jnp.sum(
        jnp.where(owner[None, :] == block_ids[:, None], block_ids[None, :], 0), axis=1
    )
    slot_block = lax.dynamic_slice_in_dim(all_slots, lax.axis_index("shard") * mat_dev, mat_dev, 0)
    picked = jnp.take(grad_blocks, jnp.minimum(all_slots, BLOCKS - 1), axis=0)
    grad_slot = jnp.where((all_slots < BLOCKS)[:, None, None], picked, 0.0)
    own_grads, own_vec = (
        lax.psum_scatter(
            grad_slot.astype(jnp.bfloat16), "shard", scatter_dimension=0, tiled=True
        ).astype(jnp.float32),
        lax.psum_scatter(
            grad_vectors.astype(jnp.bfloat16), "shard", scatter_dimension=1, tiled=True
        ).astype(jnp.float32),
    )
    own_grads, own_vec = (
        lax.psum(own_grads.astype(jnp.bfloat16), "rep").astype(jnp.float32),
        lax.psum(own_vec.astype(jnp.bfloat16), "rep").astype(jnp.float32),
    )
    rotated = jnp.matmul(
        jnp.matmul(jnp.swapaxes(left_basis, 1, 2), own_grads, precision=PRECISE),
        right_basis,
        precision=PRECISE,
    )
    new_first = MOMENT_DECAY * first_moment + (1.0 - MOMENT_DECAY) * rotated
    new_second = MOMENT_DECAY * second_moment + (1.0 - MOMENT_DECAY) * rotated * rotated
    correction = 1.0 - MOMENT_DECAY**STEP
    direction = new_first / correction / (jnp.sqrt(new_second / correction) + ADAM_EPS)
    update = jnp.matmul(
        jnp.matmul(left_basis, direction, precision=PRECISE),
        jnp.swapaxes(right_basis, 1, 2),
        precision=PRECISE,
    )
    step_rate = jnp.where(slot_block < BLOCKS, 2.0 * block_spread(slot_block), 0.0)
    new_master = master - step_rate[:, None, None] * (update + WEIGHT_DECAY * master)
    vec_first_new = MOMENT_DECAY * vec_first + (1.0 - MOMENT_DECAY) * own_vec
    vec_second_new = MOMENT_DECAY * vec_second + (1.0 - MOMENT_DECAY) * own_vec * own_vec
    vec_master_new = vec_master - VECTOR_RATE * (vec_first_new / correction) / (
        jnp.sqrt(vec_second_new / correction) + ADAM_EPS
    )
    return (
        outputs,
        grad_images,
        grad_embeds,
        new_first,
        new_second,
        new_master,
        new_master.astype(jnp.bfloat16),
        vec_first_new,
        vec_second_new,
        vec_master_new,
        vec_master_new.astype(jnp.bfloat16),
    )


def solution(mesh):
    return jax.shard_map(
        shards,
        mesh=mesh,
        in_specs=(
            P(("rep", "shard"), None, None),
            P(("rep", "shard"), None),
            P(("rep", "shard"), None, None),
            P(("rep", "shard"), None),
            P(),
            P(),
            P("shard", None, None),
            P("shard", None, None),
            P("shard", None, None),
            P("shard", None, None),
            P("shard", None, None),
            P(None, "shard"),
            P(None, "shard"),
            P(None, "shard"),
        ),
        out_specs=(
            P(("rep", "shard"), None, None),
            P(("rep", "shard"), None, None),
            P(("rep", "shard"), None),
            P("shard", None, None),
            P("shard", None, None),
            P("shard", None, None),
            P("shard", None, None),
            P(None, "shard"),
            P(None, "shard"),
            P(None, "shard"),
            P(None, "shard"),
        ),
        check_vma=False,
    )
```

profile of v0, /device:TPU:0, one launch (start us, length us, event | category | flops | bytes accessed | tf_op | source)
XLA Modules:
  0.0 1324.7 jit_solution(1649938380181234496)
XLA Ops:
  10.2 23.8 %all-gather = bf16[16,32,13]{1,2,0:T(8,128)(2,1)S(1)} all-gather(bf16[1,32,13]{1,2,0:T(8,128)(2,1)S(1)} %convert_bitcast_fusion), channel_id=1, replica_groups=mesh['rep'=2,'shard'=16] {'shard'}, dimensions={0}, use_global_device_ids=true | all-gather | bytes 14144 | tf_op jit(solution)/shard_map/all_gather | solution.py:224
  37.9 102.6 %all-gather.3.cloned.1.call-done = bf16[32,512,512]{2,1,0:T(8,128)(2,1)} async-done(((bf16[2,512,512]{2,1,0:T(8,128)(2,1)}), bf16[32,512,512]{2,1,0:T(8,128)(2,1)}) %all-gather.3.cloned.1.call-update) | async-done | bytes 16777232 | tf_op jit(solution)/shard_map/all_gather | solution.py:223
  140.5 12.3 gather_fusion
  155.2 8.1 fusion.246
  168.8 12.5 broadcast_in_dim.148
  186.5 781.9 %while.76 = (s32[]{:T(128)}, f32[26,512,512]{2,1,0:T(8,128)}, f32[13,512]{1,0:T(8,128)}, bf16[2,1024,512]{2,1,0:T(8,128)(2,1)}, f32[2,1024,512]{2,1,0:T(8,128)},...) while((s32[]{:T(128)}, f32[26,512,512]{2,1,0:T(8,128)}, ...), condition=%wide.region_44.45_spmd, body=%wide.region_0.44_spmd.sunk | while | flops 39459495936 | bytes 1156580864 | solution.py:383
  251.6 38.7 %while.77 = (s32[]{:T(128)}, bf16[2,512,512]{2,1,0:T(8,128)(2,1)}, f32[2,8,512]{2,1,0:T(8,128)}, s32[2]{0:T(128)S(1)}, bf16[1024,512]{0,1:T(8,128)(2,1)}, /*inde...) while((s32[]{:T(128)}, bf16[2,512,512]{2,1,0:T(8,128)(2,1)}, ...), condition=%wide.region_16.16_spmd, body=%wide.region_13.15_spmd.sunk | while | flops 1111486464 | bytes 60949680 | solution.py:143
  281.3 5.0 fusion.779
  296.9 130.3 %while.78 = (s32[]{:T(128)}, f32[1024,8,64]{0,2,1:T(8,128)}, f32[1024,8,64]{0,2,1:T(8,128)}, bf16[2,512,512]{2,1,0:T(8,128)(2,1)}, s32[2]{0:T(128)S(1)}, /*index...) while((s32[]{:T(128)}, f32[1024,8,64]{0,2,1:T(8,128)}, ...), condition=%wide.region_19.19_spmd.clone, body=%wide.region_17.18_spmd.clone.sunk | while | flops 2737827840 | bytes 246137840 | solution.py:194
  300.8 8.2 fusion.790
  309.8 15.0 %multiply_reduce_fusion.24 = (f32[8,512]{1,0:T(8,128)}, f32[8,512,1024]{2,1,0:T(8,128)}) fusion(f32[8,512,1024]{2,1,0:T(8,128)} %fusion.790, f32[8,512]{1,0:T(8,128)S(1)} %dynamic-slice_bitcast_fusion.2, bf16[512,8,64]{0,2,1:T(8,128)(2,1)S(1)} %bitcast.1045, bf16[1024,8,64]{0,2,1:T(8,128)(2,1)} %get-tuple-element.1178), kind=kOutput, calls=%fused_computation.12.clone.1 | convolution fusion | flops 553644032 | bytes 35160064 | tf_op jit(solution)/shard_map/while/body/while/body/eval_jaxpr/qhd,khd->hqk/dot_general | solution.py:168
  326.5 10.5 multiply_convert_fusion.13
  337.0 6.6 bitcast_add_fusion.6
  351.0 10.5 bitcast_add_fusion.7
  365.2 8.2 fusion.790
  374.2 15.0 %multiply_reduce_fusion.24 = (f32[8,512]{1,0:T(8,128)}, f32[8,512,1024]{2,1,0:T(8,128)}) fusion(f32[8,512,1024]{2,1,0:T(8,128)} %fusion.790, f32[8,512]{1,0:T(8,128)S(1)} %dynamic-slice_bitcast_fusion.2, bf16[512,8,64]{0,2,1:T(8,128)(2,1)S(1)} %bitcast.1045, bf16[1024,8,64]{0,2,1:T(8,128)(2,1)} %get-tuple-element.1178), kind=kOutput, calls=%fused_computation.12.clone.1 | convolution fusion | flops 553644032 | bytes 35160064 | tf_op jit(solution)/shard_map/while/body/while/body/eval_jaxpr/qhd,khd->hqk/dot_general | solution.py:168
  390.9 10.5 multiply_convert_fusion.13
  401.4 7.2 bitcast_add_fusion.6
  416.0 11.0 bitcast_add_fusion.7
  437.0 6.1 multiply_reduce_fusion.21
  480.9 6.2 bitcast_dynamic-update-slice_fusion.7
  532.1 6.2 bitcast_dynamic-update-slice_fusion.6
  540.1 27.4 %add.985 = f32[26,512,512]{2,1,0:T(8,128)} add(f32[26,512,512]{2,1,0:T(8,128)} %get-tuple-element.1211, f32[26,512,512]{2,1,0:T(8,128)} %fusion.759) | non-fusion elementwise | flops 6815744 | bytes 81788928 | tf_op jit(solution)/shard_map/while/body/add | solution.py:369
  640.7 38.7 %while.77 = (s32[]{:T(128)}, bf16[2,512,512]{2,1,0:T(8,128)(2,1)}, f32[2,8,512]{2,1,0:T(8,128)}, s32[2]{0:T(128)S(1)}, bf16[1024,512]{0,1:T(8,128)(2,1)}, /*inde...) while((s32[]{:T(128)}, bf16[2,512,512]{2,1,0:T(8,128)(2,1)}, ...), condition=%wide.region_16.16_spmd, body=%wide.region_13.15_spmd.sunk | while | flops 1111486464 | bytes 60949680 | solution.py:143
  670.4 5.0 fusion.779
  686.0 130.5 %while.78 = (s32[]{:T(128)}, f32[1024,8,64]{0,2,1:T(8,128)}, f32[1024,8,64]{0,2,1:T(8,128)}, bf16[2,512,512]{2,1,0:T(8,128)(2,1)}, s32[2]{0:T(128)S(1)}, /*index...) while((s32[]{:T(128)}, f32[1024,8,64]{0,2,1:T(8,128)}, ...), condition=%wide.region_19.19_spmd.clone, body=%wide.region_17.18_spmd.clone.sunk | while | flops 2737827840 | bytes 246137840 | solution.py:194
  690.2 8.2 fusion.790
  699.1 15.0 %multiply_reduce_fusion.24 = (f32[8,512]{1,0:T(8,128)}, f32[8,512,1024]{2,1,0:T(8,128)}) fusion(f32[8,512,1024]{2,1,0:T(8,128)} %fusion.790, f32[8,512]{1,0:T(8,128)S(1)} %dynamic-slice_bitcast_fusion.2, bf16[512,8,64]{0,2,1:T(8,128)(2,1)S(1)} %bitcast.1045, bf16[1024,8,64]{0,2,1:T(8,128)(2,1)} %get-tuple-element.1178), kind=kOutput, calls=%fused_computation.12.clone.1 | convolution fusion | flops 553644032 | bytes 35160064 | tf_op jit(solution)/shard_map/while/body/while/body/eval_jaxpr/qhd,khd->hqk/dot_general | solution.py:168
  715.9 10.5 multiply_convert_fusion.13
  726.4 6.6 bitcast_add_fusion.6
  740.4 10.5 bitcast_add_fusion.7
  754.5 8.2 fusion.790
  763.5 15.0 %multiply_reduce_fusion.24 = (f32[8,512]{1,0:T(8,128)}, f32[8,512,1024]{2,1,0:T(8,128)}) fusion(f32[8,512,1024]{2,1,0:T(8,128)} %fusion.790, f32[8,512]{1,0:T(8,128)S(1)} %dynamic-slice_bitcast_fusion.2, bf16[512,8,64]{0,2,1:T(8,128)(2,1)S(1)} %bitcast.1045, bf16[1024,8,64]{0,2,1:T(8,128)(2,1)} %get-tuple-element.1178), kind=kOutput, calls=%fused_computation.12.clone.1 | convolution fusion | flops 553644032 | bytes 35160064 | tf_op jit(solution)/shard_map/while/body/while/body/eval_jaxpr/qhd,khd->hqk/dot_general | solution.py:168
  780.2 10.5 multiply_convert_fusion.13
  790.7 7.2 bitcast_add_fusion.6
  805.3 11.0 bitcast_add_fusion.7
  826.3 6.1 multiply_reduce_fusion.21
  870.0 6.2 bitcast_dynamic-update-slice_fusion.7
  921.4 6.2 bitcast_dynamic-update-slice_fusion.6
  929.4 27.4 %add.985 = f32[26,512,512]{2,1,0:T(8,128)} add(f32[26,512,512]{2,1,0:T(8,128)} %get-tuple-element.1211, f32[26,512,512]{2,1,0:T(8,128)} %fusion.759) | non-fusion elementwise | flops 6815744 | bytes 81788928 | tf_op jit(solution)/shard_map/while/body/add | solution.py:369
  968.4 17.4 %gather_fusion.1 = bf16[32,512,512]{2,1,0:T(8,128)(2,1)} fusion(f32[26,512,512]{2,1,0:T(8,128)} %get-tuple-element.334, s32[1024]{0:T(1024)} %pad_clamp_fusion), kind=kCustom, calls=%fused_computation.1 | custom fusion | bytes 33554560 | tf_op jit(solution)/shard_map/jit(_take)/gather | solution.py:391
  985.8 22.6 %copy.136 = bf16[32,512,512]{1,2,0:T(8,128)(2,1)} copy(bf16[32,512,512]{2,1,0:T(8,128)(2,1)} %gather_fusion.1) | data formatting | bytes 33554432 | tf_op jit(solution)/shard_map/jit(_take)/gather | solution.py:391
  1008.4 15.2 %select_convert_fusion = bf16[32,512,512]{1,2,0:T(8,128)(2,1)} fusion(bf16[32,512,512]{1,2,0:T(8,128)(2,1)} %copy.136, pred[32]{0:T(512)(128)(4,1)S(1)} %copy-done.110, pred[32]{0:T(512)(128)(4,1)S(1)} %copy-done.109), kind=kLoop, calls=%fused_computation.349 | loop fusion | flops 16777216 | bytes 33554496 | tf_op jit(solution)/shard_map/convert_element_type | solution.py:395
  1025.2 175.2 %reduce-scatter.5.cloned.1.call-done = bf16[2,512,512]{1,2,0:T(8,128)(2,1)} async-done(((bf16[32,512,512]{1,2,0:T(8,128)(2,1)}), bf16[2,512,512]{1,2,0:T(8,128)(2,1)}) %reduce-scatter.5.cloned.1.call-update) | async-done | bytes 1048592 | tf_op jit(solution)/shard_map/reduce_scatter | solution.py:394
  1200.6 58.1 %reduce-scatter.7.cloned.1.call-done = bf16[32,13]{1,0:T(8,128)(2,1)} async-done(((bf16[512,13]{1,0:T(8,128)(2,1)}), bf16[32,13]{1,0:T(8,128)(2,1)}) %reduce-scatter.7.cloned.1.call-update) | async-done | bytes 848
  1259.4 5.2 psum.15
  1265.3 34.6 %all-reduce.6.cloned.1.call-done = bf16[2,512,512]{1,2,0:T(8,128)(2,1)} async-done(((bf16[2,512,512]{1,2,0:T(8,128)(2,1)}), bf16[2,512,512]{1,2,0:T(8,128)(2,1)}) %all-reduce.6.cloned.1.call-update) | async-done | bytes 1048592 | tf_op jit(solution)/shard_map/psum | solution.py:402
  1312.3 5.3 fusion.248
  (978 shorter events, 482.9 us)
Async XLA Ops:
  7.2 1296.6 %copy-start = (f32[2,512,512]{2,1,0:T(8,128)S(1)}, f32[2,512,512]{2,1,0:T(8,128)}, u32[]{:S(2)}) copy-start(f32[2,512,512]{2,1,0:T(8,128)} %param.30) | copy-start | bytes 6291460
  7.2 27.5 %copy-start.108 = (s32[1,2]{1,0:T(1,128)S(1)}, s32[1,2]{1,0:T(1,128)}, u32[]{:S(2)}) copy-start(s32[1,2]{1,0:T(1,128)} %param.23) | copy-start | bytes 28
  7.2 29.4 %copy-start.111 = (s32[32]{0:T(128)S(1)}, s32[32]{0:T(128)}, u32[]{:S(2)}) copy-start(s32[32]{0:T(128)} %param.25) | copy-start | bytes 388
  7.2 133.2 %all-gather.3.cloned.1.call-start = ((), (), s32[]{:S(2)}) async-start(), calls=%async_computation.2 | async-start | bytes 17825792 | tf_op jit(solution)/shard_map/all_gather | solution.py:223
  10.1 1190.3 %reduce-scatter.5.cloned.1.call-start = ((), (), s32[]{:S(2)}) async-start(), calls=%async_computation.3 | async-start | bytes 17825792 | tf_op jit(solution)/shard_map/reduce_scatter | solution.py:394
  36.7 116.0 %copy-start.112 = (s32[32]{0:T(128)}, s32[32]{0:T(128)S(1)}, u32[]{:S(2)}) copy-start(s32[32]{0:T(128)S(1)} %select_reduce_fusion) | copy-start | bytes 388
  188.5 15.0 %copy-start.70 = (f32[512]{0:T(512)}, f32[512]{0:T(512)S(1)}, u32[]{:S(2)}) copy-start(f32[512]{0:T(512)S(1)} %sub.526) | copy-start | bytes 6148 | tf_op jit(solution)/shard_map/while
  193.6 25.0 %copy-start.90 = (f32[1,512]{1,0:T(1,128)}, f32[1,512]{1,0:T(1,128)S(1)}, u32[]{:S(2)}) copy-start(f32[1,512]{1,0:T(1,128)S(1)} %get-tuple-element.1021) | copy-start | bytes 6148 | tf_op jit(solution)/shard_map/while
  193.6 25.0 %copy-start.96 = (f32[1,512]{1,0:T(1,128)}, f32[1,512]{1,0:T(1,128)S(1)}, u32[]{:S(2)}) copy-start(f32[1,512]{1,0:T(1,128)S(1)} %get-tuple-element.1022) | copy-start | bytes 6148 | tf_op jit(solution)/shard_map/while
  193.7 42.2 %copy-start.86 = (f32[1,512]{1,0:T(1,128)}, f32[1,512]{1,0:T(1,128)S(1)}, u32[]{:S(2)}) copy-start(f32[1,512]{1,0:T(1,128)S(1)} %get-tuple-element.1035) | copy-start | bytes 6148 | tf_op jit(solution)/shard_map/while
  193.7 42.2 %copy-start.100 = (f32[1,512]{1,0:T(1,128)}, f32[1,512]{1,0:T(1,128)S(1)}, u32[]{:S(2)}) copy-start(f32[1,512]{1,0:T(1,128)S(1)} %get-tuple-element.1036) | copy-start | bytes 6148 | tf_op jit(solution)/shard_map/while
  251.6 39.3 %copy-start.98 = (f32[2]{0:T(128)S(1)}, f32[2]{0:T(128)}, u32[]{:S(2)}) copy-start(f32[2]{0:T(128)} %get-tuple-element.1250) | copy-start | bytes 28 | tf_op jit(solution)/shard_map/while
  309.4 15.4 %copy-start.5 = (bf16[512,512]{0,1:T(8,128)(2,1)}, bf16[512,512]{0,1:T(8,128)(2,1)S(1)}, u32[]{:S(2)}) copy-start(bf16[512,512]{0,1:T(8,128)(2,1)S(1)} %copy.205) | copy-start | bytes 1572868 | tf_op jit(solution)/shard_map/while/body/while
  309.8 15.0 %slice-start = ((s8[16777216]{0:T(1024)(128)(4,1)}), s8[4194304]{0:T(1024)(128)(4,1)S(1)}, s32[]{:S(2)}) async-start(s8[16777216]{0:T(1024)(128)(4,1)} %bitcast.1040), calls=%async_computation.6 | async-start | bytes 8388608 | tf_op jit(solution)/shard_map/while/body/while
  309.8 15.0 %slice-start.1 = ((s8[16777216]{0:T(1024)(128)(4,1)}), s8[4194304]{0:T(1024)(128)(4,1)S(1)}, s32[]{:S(2)}) async-start(s8[16777216]{0:T(1024)(128)(4,1)} %bitcast.1040), calls=%async_computation.7 | async-start | bytes 8388608 | tf_op jit(solution)/shard_map/while/body/while
  309.8 15.6 %slice-start.2 = ((s8[16777216]{0:T(1024)(128)(4,1)}), s8[4194304]{0:T(1024)(128)(4,1)S(1)}, s32[]{:S(2)}) async-start(s8[16777216]{0:T(1024)(128)(4,1)} %bitcast.1040), calls=%async_computation.8 | async-start | bytes 8388608 | tf_op jit(solution)/shard_map/while/body/while
  309.8 16.7 %slice-start.3 = ((s8[16777216]{0:T(1024)(128)(4,1)}), s8[4194304]{0:T(1024)(128)(4,1)S(1)}, s32[]{:S(2)}) async-start(s8[16777216]{0:T(1024)(128)(4,1)} %bitcast.1040), calls=%async_computation.9 | async-start | bytes 8388608 | tf_op jit(solution)/shard_map/while/body/while
  373.7 15.4 %copy-start.5 = (bf16[512,512]{0,1:T(8,128)(2,1)}, bf16[512,512]{0,1:T(8,128)(2,1)S(1)}, u32[]{:S(2)}) copy-start(bf16[512,512]{0,1:T(8,128)(2,1)S(1)} %copy.205) | copy-start | bytes 1572868 | tf_op jit(solution)/shard_map/while/body/while
  374.1 15.0 %slice-start = ((s8[16777216]{0:T(1024)(128)(4,1)}), s8[4194304]{0:T(1024)(128)(4,1)S(1)}, s32[]{:S(2)}) async-start(s8[16777216]{0:T(1024)(128)(4,1)} %bitcast.1040), calls=%async_computation.6 | async-start | bytes 8388608 | tf_op jit(solution)/shard_map/while/body/while
  374.1 15.0 %slice-start.1 = ((s8[16777216]{0:T(1024)(128)(4,1)}), s8[4194304]{0:T(1024)(128)(4,1)S(1)}, s32[]{:S(2)}) async-start(s8[16777216]{0:T(1024)(128)(4,1)} %bitcast.1040), calls=%async_computation.7 | async-start | bytes 8388608 | tf_op jit(solution)/shard_map/while/body/while
  374.1 15.6 %slice-start.2 = ((s8[16777216]{0:T(1024)(128)(4,1)}), s8[4194304]{0:T(1024)(128)(4,1)S(1)}, s32[]{:S(2)}) async-start(s8[16777216]{0:T(1024)(128)(4,1)} %bitcast.1040), calls=%async_computation.8 | async-start | bytes 8388608 | tf_op jit(solution)/shard_map/while/body/while
  374.1 16.7 %slice-start.3 = ((s8[16777216]{0:T(1024)(128)(4,1)}), s8[4194304]{0:T(1024)(128)(4,1)S(1)}, s32[]{:S(2)}) async-start(s8[16777216]{0:T(1024)(128)(4,1)} %bitcast.1040), calls=%async_computation.9 | async-start | bytes 8388608 | tf_op jit(solution)/shard_map/while/body/while
  540.1 27.4 %copy-start.9 = (f32[4,512,512]{2,1,0:T(8,128)S(1)}, f32[4,512,512]{2,1,0:T(8,128)}, u32[]{:S(2)}) copy-start(f32[4,512,512]{2,1,0:T(8,128)} %get-tuple-element.1252) | copy-start | bytes 12582916 | tf_op jit(solution)/shard_map/while
  577.9 15.0 %copy-start.70 = (f32[512]{0:T(512)}, f32[512]{0:T(512)S(1)}, u32[]{:S(2)}) copy-start(f32[512]{0:T(512)S(1)} %sub.526) | copy-start | bytes 6148 | tf_op jit(solution)/shard_map/while
  583.0 25.0 %copy-start.90 = (f32[1,512]{1,0:T(1,128)}, f32[1,512]{1,0:T(1,128)S(1)}, u32[]{:S(2)}) copy-start(f32[1,512]{1,0:T(1,128)S(1)} %get-tuple-element.1021) | copy-start | bytes 6148 | tf_op jit(solution)/shard_map/while
  583.0 25.0 %copy-start.96 = (f32[1,512]{1,0:T(1,128)}, f32[1,512]{1,0:T(1,128)S(1)}, u32[]{:S(2)}) copy-start(f32[1,512]{1,0:T(1,128)S(1)} %get-tuple-element.1022) | copy-start | bytes 6148 | tf_op jit(solution)/shard_map/while
  583.1 41.9 %copy-start.86 = (f32[1,512]{1,0:T(1,128)}, f32[1,512]{1,0:T(1,128)S(1)}, u32[]{:S(2)}) copy-start(f32[1,512]{1,0:T(1,128)S(1)} %get-tuple-element.1035) | copy-start | bytes 6148 | tf_op jit(solution)/shard_map/while
  583.1 41.9 %copy-start.100 = (f32[1,512]{1,0:T(1,128)}, f32[1,512]{1,0:T(1,128)S(1)}, u32[]{:S(2)}) copy-start(f32[1,512]{1,0:T(1,128)S(1)} %get-tuple-element.1036) | copy-start | bytes 6148 | tf_op jit(solution)/shard_map/while
  640.7 39.3 %copy-start.98 = (f32[2]{0:T(128)S(1)}, f32[2]{0:T(128)}, u32[]{:S(2)}) copy-start(f32[2]{0:T(128)} %get-tuple-element.1250) | copy-start | bytes 28 | tf_op jit(solution)/shard_map/while
  698.7 15.4 %copy-start.5 = (bf16[512,512]{0,1:T(8,128)(2,1)}, bf16[512,512]{0,1:T(8,128)(2,1)S(1)}, u32[]{:S(2)}) copy-start(bf16[512,512]{0,1:T(8,128)(2,1)S(1)} %copy.205) | copy-start | bytes 1572868 | tf_op jit(solution)/shard_map/while/body/while
  699.1 15.0 %slice-start = ((s8[16777216]{0:T(1024)(128)(4,1)}), s8[4194304]{0:T(1024)(128)(4,1)S(1)}, s32[]{:S(2)}) async-start(s8[16777216]{0:T(1024)(128)(4,1)} %bitcast.1040), calls=%async_computation.6 | async-start | bytes 8388608 | tf_op jit(solution)/shard_map/while/body/while
  699.1 15.0 %slice-start.1 = ((s8[16777216]{0:T(1024)(128)(4,1)}), s8[4194304]{0:T(1024)(128)(4,1)S(1)}, s32[]{:S(2)}) async-start(s8[16777216]{0:T(1024)(128)(4,1)} %bitcast.1040), calls=%async_computation.7 | async-start | bytes 8388608 | tf_op jit(solution)/shard_map/while/body/while
  699.1 15.6 %slice-start.2 = ((s8[16777216]{0:T(1024)(128)(4,1)}), s8[4194304]{0:T(1024)(128)(4,1)S(1)}, s32[]{:S(2)}) async-start(s8[16777216]{0:T(1024)(128)(4,1)} %bitcast.1040), calls=%async_computation.8 | async-start | bytes 8388608 | tf_op jit(solution)/shard_map/while/body/while
  699.1 16.7 %slice-start.3 = ((s8[16777216]{0:T(1024)(128)(4,1)}), s8[4194304]{0:T(1024)(128)(4,1)S(1)}, s32[]{:S(2)}) async-start(s8[16777216]{0:T(1024)(128)(4,1)} %bitcast.1040), calls=%async_computation.9 | async-start | bytes 8388608 | tf_op jit(solution)/shard_map/while/body/while
  763.1 15.4 %copy-start.5 = (bf16[512,512]{0,1:T(8,128)(2,1)}, bf16[512,512]{0,1:T(8,128)(2,1)S(1)}, u32[]{:S(2)}) copy-start(bf16[512,512]{0,1:T(8,128)(2,1)S(1)} %copy.205) | copy-start | bytes 1572868 | tf_op jit(solution)/shard_map/while/body/while
  763.5 15.0 %slice-start = ((s8[16777216]{0:T(1024)(128)(4,1)}), s8[4194304]{0:T(1024)(128)(4,1)S(1)}, s32[]{:S(2)}) async-start(s8[16777216]{0:T(1024)(128)(4,1)} %bitcast.1040), calls=%async_computation.6 | async-start | bytes 8388608 | tf_op jit(solution)/shard_map/while/body/while
  763.5 15.0 %slice-start.1 = ((s8[16777216]{0:T(1024)(128)(4,1)}), s8[4194304]{0:T(1024)(128)(4,1)S(1)}, s32[]{:S(2)}) async-start(s8[16777216]{0:T(1024)(128)(4,1)} %bitcast.1040), calls=%async_computation.7 | async-start | bytes 8388608 | tf_op jit(solution)/shard_map/while/body/while
  763.5 15.6 %slice-start.2 = ((s8[16777216]{0:T(1024)(128)(4,1)}), s8[4194304]{0:T(1024)(128)(4,1)S(1)}, s32[]{:S(2)}) async-start(s8[16777216]{0:T(1024)(128)(4,1)} %bitcast.1040), calls=%async_computation.8 | async-start | bytes 8388608 | tf_op jit(solution)/shard_map/while/body/while
  763.5 16.7 %slice-start.3 = ((s8[16777216]{0:T(1024)(128)(4,1)}), s8[4194304]{0:T(1024)(128)(4,1)S(1)}, s32[]{:S(2)}) async-start(s8[16777216]{0:T(1024)(128)(4,1)} %bitcast.1040), calls=%async_computation.9 | async-start | bytes 8388608 | tf_op jit(solution)/shard_map/while/body/while
  929.4 27.4 %copy-start.9 = (f32[4,512,512]{2,1,0:T(8,128)S(1)}, f32[4,512,512]{2,1,0:T(8,128)}, u32[]{:S(2)}) copy-start(f32[4,512,512]{2,1,0:T(8,128)} %get-tuple-element.1252) | copy-start | bytes 12582916 | tf_op jit(solution)/shard_map/while
  985.8 22.6 %copy-start.109 = (pred[32]{0:T(512)(128)(4,1)S(1)}, pred[32]{0:T(512)(128)(4,1)}, u32[]{:S(2)}) copy-start(pred[32]{0:T(512)(128)(4,1)} %get-tuple-element.674) | copy-start | bytes 100
  985.8 22.6 %copy-start.110 = (pred[32]{0:T(512)(128)(4,1)S(1)}, pred[32]{0:T(512)(128)(4,1)}, u32[]{:S(2)}) copy-start(pred[32]{0:T(512)(128)(4,1)} %get-tuple-element.675) | copy-start | bytes 100
  1023.6 176.9 %copy-start.113 = (s32[32]{0:T(128)S(1)}, s32[32]{0:T(128)}, u32[]{:S(2)}) copy-start(s32[32]{0:T(128)} %copy-done.112) | copy-start | bytes 388
  1023.6 241.1 %copy-start.103 = (f32[13,32]{1,0:T(8,128)S(1)}, f32[13,32]{1,0:T(8,128)}, u32[]{:S(2)}) copy-start(f32[13,32]{1,0:T(8,128)} %param.31) | copy-start | bytes 4996
  1023.6 241.1 %copy-start.104 = (f32[13,32]{1,0:T(8,128)S(1)}, f32[13,32]{1,0:T(8,128)}, u32[]{:S(2)}) copy-start(f32[13,32]{1,0:T(8,128)} %param.33) | copy-start | bytes 4996
  1023.6 241.1 %copy-start.105 = (f32[13,32]{1,0:T(8,128)S(1)}, f32[13,32]{1,0:T(8,128)}, u32[]{:S(2)}) copy-start(f32[13,32]{1,0:T(8,128)} %param.32) | copy-start | bytes 4996
  1023.6 235.0 %reduce-scatter.7.cloned.1.call-start = ((), (), s32[]{:S(2)}) async-start(), calls=%async_computation.5 | async-start | bytes 139264
  1025.1 274.7 %all-reduce.6.cloned.1.call-start = ((), (), s32[]{:S(2)}) async-start(), calls=%async_computation.4 | async-start | bytes 2097152 | tf_op jit(solution)/shard_map/psum | solution.py:402
  (214 other events, 876.0 us)
Sparse Core Ops, SparseCore 0:
  10.8 129.6 all-gather.2
  1023.7 176.6 reduce-scatter.4
  1204.5 54.0 reduce-scatter.6
  1260.7 39.0 all-reduce.5
where the time goes:
time: 1330 us; the launch traced here: 1320 us
  matrix products  433 us (33%)
  waiting for transfers between devices  371 us (28%)
  local copies, waits for them, and re-layouts  231 us (17%)
  other arithmetic  220 us (17%)
  blocking collectives  29 us (2%)
  loops' own time  26.1 us (2%)
  between operations  15.9 us (1%)
    reduce_scatter x1, waiting for transfers between devices, shards(): lax.psum_scatter(grad_slot.astype(jnp.bfloat16), 'shard', scatter_dimensi...  175 us
    all_gather x1, waiting for transfers between devices, shards(): lax.all_gather(master.astype(jnp.bfloat16), 'shard', axis=0, tiled=True)  103 us
    dot_general x36, matrix products, conv_back_taps(): lax.dot_general(tap_view(padded, tap_index), grad_rows, dims, preferred_e...  66 us
    dot_general x4, matrix products, one_block(): jnp.einsum('qhd,khd->hqk', grad_block, value_heads, preferred_element_typ...  59.9 us
    unnamed x5, waiting for transfers between devices  58.1 us
    add x2, other arithmetic, one_image(): grad_blocks + block_terms  54.8 us
    dot_general x4, matrix products, one_block(): jnp.einsum('hqk,qhd->khd', probabilities.astype(jnp.bfloat16), grad_block...  43 us
    dot_general x8, matrix products, one_block(): jnp.einsum('qhd,khd->hqk', query_block, key_heads, preferred_element_type...  42.7 us
  transfers between devices with their start and end apart: 4, of which 4 were waited for; matrix products, arithmetic and copies ran while one was open for 0% of the time, Pallas kernels for 0%

commit v1 on v0

v1 whole, which is shorter than its diff:
```python
import functools
import math

import jax
import jax.numpy as jnp
from jax import lax
from jax.experimental import pallas as pl
from jax.experimental.pallas import tpu as pltpu
from jax.sharding import PartitionSpec as P

C = 512
EMB = 1024
HEADS = 8
HEAD = 64
GROUPS = 32
SIDE = 32
HW = 1024
BLOCKS = 26
VECS = 13
STEP = 2
PAD = SIDE
SLAB = HW + 2 * PAD
ROWS = 128
QROWS = 256

EPS_NORM = 1e-05
ADAM_EPS = 1e-08
MOMENT_DECAY = 0.5
WEIGHT_DECAY = 0.01
VECTOR_RATE = 0.2
PRECISE = lax.Precision.HIGHEST
F32 = jnp.float32
BF16 = jnp.bfloat16
ANY = pl.BlockSpec(memory_space=pl.ANY)
SMEM = pl.BlockSpec(memory_space=pltpu.SMEM)
VMEM = pl.BlockSpec(memory_space=pltpu.VMEM)
VMEM_LIMIT = 56 * 2**20


def block_spread(block_index):
    return jnp.where(
        block_index < 18,
        (9.0 * C) ** (-0.5),
        jnp.where(
            block_index < 22,
            EMB ** (-0.5),
            jnp.where(
                block_index < 24,
                1.25 * C ** (-0.5),
                jnp.where(
                    block_index < 25,
                    C ** (-0.5),
                    jnp.where(block_index < 26, 0.295 * (HW / C) ** 0.5, C ** (-0.5)),
                ),
            ),
        ),
    )


def mm(a, b):
    return jnp.dot(a, b, preferred_element_type=F32)


def mm_t(a, b):
    return lax.dot_general(a, b, (((1,), (1,)), ((), ())), preferred_element_type=F32)


def sigmoid(u):
    return 1.0 / (1.0 + jnp.exp(-u))


def silu_slope(u):
    s = sigmoid(u)
    return s * (1.0 + u * (1.0 - s))


def chunks(count, body, init=0):
    return lax.fori_loop(0, count, body, init)


def rows_of(index, size):
    return pl.ds(pl.multiple_of(index * size, size), size)


def group_mean(column_sum):
    total = jnp.broadcast_to(column_sum, (8, C))
    lane = lax.broadcasted_iota(jnp.int32, (8, C), 1)
    for step in (1, 2, 4, 8):
        other = jnp.where(
            (lane & step) != 0, pltpu.roll(total, step, 1), pltpu.roll(total, C - step, 1)
        )
        total = total + other
    return total[0:1] * (1.0 / (HW * (C // GROUPS)))


def norm_stats(read):
    zero = jnp.zeros((1, C), F32)
    total = chunks(
        HW // ROWS,
        lambda c, t: t + jnp.sum(read(rows_of(c, ROWS)), axis=0, keepdims=True),
        zero,
    )
    mean = group_mean(total)

    def squares(c, t):
        centered = read(rows_of(c, ROWS)) - mean
        return t + jnp.sum(centered * centered, axis=0, keepdims=True)

    var = group_mean(chunks(HW // ROWS, squares, zero))
    return mean, lax.rsqrt(var + EPS_NORM)


def clear_pads(slab):
    zeros = jnp.zeros((PAD, C), BF16)
    for lead in slab_leads(slab):
        slab[lead + (pl.ds(0, PAD), slice(None))] = zeros
        slab[lead + (pl.ds(PAD + HW, PAD), slice(None))] = zeros


def slab_leads(slab):
    if len(slab.shape) == 3:
        return [(j,) for j in range(3)]
    return [(i, j) for i in range(slab.shape[0]) for j in range(3)]


def store_slab(slab, lead, c, chunk):
    column = lax.broadcasted_iota(jnp.int32, (ROWS, C), 0) & (SIDE - 1)
    before = jnp.where(column == 0, 0.0, pltpu.roll(chunk, 1, 0))
    after = jnp.where(column == SIDE - 1, 0.0, pltpu.roll(chunk, ROWS - 1, 0))
    rows = pl.ds(pl.multiple_of(c * ROWS + PAD, PAD), ROWS)
    slab[lead + (0, rows, slice(None))] = before.astype(BF16)
    slab[lead + (1, rows, slice(None))] = chunk.astype(BF16)
    slab[lead + (2, rows, slice(None))] = after.astype(BF16)


def conv_rows(slab, lead, weights, base, size, back):
    total = None
    for tap in range(9):
        di, dj = tap // 3, tap % 3
        if back:
            di, dj = 2 - di, 2 - dj
        rows = pl.ds(pl.multiple_of(base + di * SIDE, SIDE), size)
        piece = slab[lead + (dj, rows, slice(None))]
        term = (mm_t if back else mm)(piece, weights[tap])
        total = term if total is None else total + term
    return total


CONV_ROWS = 512


def block_copies(owner, slots, dest, sem, first, count, offset=0):
    return [
        pltpu.make_async_copy(slots.at[owner[first + n]], dest.at[offset + n], sem.at[offset + n])
        for n in range(count)
    ]


def fwd_one(owner, slots, x, vec, h1, a1, weights, slab, sem):
    step = pl.program_id(0)

    @pl.when(step == 0)
    def _():
        for copy in block_copies(owner, slots, weights, sem, 0, 9):
            copy.start()
        clear_pads(slab)

    def read(rows):
        return x[0, rows, :].astype(F32)

    mean, inv = norm_stats(read)
    gain = inv * vec[0:1]
    bias = vec[1:2]

    def activate(c, _):
        rows = rows_of(c, ROWS)
        pre = (read(rows) - mean) * gain + bias
        act = pre * sigmoid(pre)
        a1[0, rows, :] = act.astype(BF16)
        store_slab(slab, (), c, act)
        return 0

    chunks(HW // ROWS, activate)

    @pl.when(step == 0)
    def _():
        for copy in block_copies(owner, slots, weights, sem, 0, 9):
            copy.wait()

    def conv(c, _):
        h1[0, rows_of(c, CONV_ROWS), :] = (
            conv_rows(slab, (), weights, c * CONV_ROWS, CONV_ROWS, False) + vec[2:3]
        )
        return 0

    chunks(HW // CONV_ROWS, conv)


def fwd_two(owner, slots, h1, x, act, vec, a2, r1, nhat, stats, weights, maps, slab, sem):
    step = pl.program_id(0)

    def copies():
        return block_copies(owner, slots, maps, sem, 18, 4) + block_copies_at(
            owner, slots, weights, sem, 9, 9, 4
        )

    @pl.when(step == 0)
    def _():
        for copy in copies():
            copy.start()
        clear_pads(slab)

    mean, inv = norm_stats(lambda rows: h1[0, rows, :])

    @pl.when(step == 0)
    def _():
        for copy in block_copies(owner, slots, maps, sem, 18, 4):
            copy.wait()

    row = act[0]
    scale = (mm(row[:, :C], maps[0]) + mm(row[:, C:], maps[1]))[0:1] + vec[3:4]
    shift = (mm(row[:, :C], maps[2]) + mm(row[:, C:], maps[3]))[0:1] + vec[4:5]
    stats[0] = jnp.concatenate([scale, shift, inv, jnp.zeros((5, C), F32)], axis=0)
    gain = vec[5:6]
    bias = vec[6:7]

    def activate(c, _):
        rows = rows_of(c, ROWS)
        normed = (h1[0, rows, :] - mean) * inv
        nhat[0, rows, :] = normed
        pre = (normed * gain + bias) * (1.0 + scale) + shift
        act_two = pre * sigmoid(pre)
        a2[0, rows, :] = act_two.astype(BF16)
        store_slab(slab, (), c, act_two)
        return 0

    chunks(HW // ROWS, activate)

    @pl.when(step == 0)
    def _():
        for copy in block_copies_at(owner, slots, weights, sem, 9, 9, 4):
            copy.wait()

    def conv(c, _):
        rows = rows_of(c, CONV_ROWS)
        hidden = conv_rows(slab, (), weights, c * CONV_ROWS, CONV_ROWS, False) + vec[7:8]
        r1[0, rows, :] = x[0, rows, :].astype(F32) + hidden
        return 0

    chunks(HW // CONV_ROWS, conv)


def block_copies_at(owner, slots, dest, sem, first, count, sem_from):
    return [
        pltpu.make_async_copy(slots.at[owner[first + n]], dest.at[n], sem.at[sem_from + n])
        for n in range(count)
    ]


MM_ROWS = 512


def attention(
    owner, slots, weight, live, r1, cot, vec, out, dr1, grads, sums,
    weights, nhat, n3, n3t, q, k, v, da, dat, qt, att, dyb, dq, dk, dv, dkt, dvt, dn3, acc, sem,
):
    step = pl.program_id(0)

    @pl.when(step == 0)
    def _():
        for copy in block_copies(owner, slots, weights, sem, 22, 4):
            copy.start()
        sums[...] = jnp.zeros((8, C), F32)

    mean, inv = norm_stats(lambda rows: r1[0, rows, :])
    gain = vec[8:9]
    bias = vec[9:10]
    image_weight = weight[step]

    def normalize(c, total):
        rows = rows_of(c, ROWS)
        normed = (r1[0, rows, :] - mean) * inv
        nhat[rows, :] = normed
        n3[rows, :] = (normed * gain + bias).astype(BF16)
        low = (cot[0, rows, :].astype(F32) * image_weight).astype(BF16)
        dyb[rows, :] = low
        return total + jnp.sum(low.astype(F32), axis=0, keepdims=True)

    zero = jnp.zeros((1, C), F32)
    sum_dy = chunks(HW // ROWS, normalize, zero)

    @pl.when(step == 0)
    def _():
        for copy in block_copies(owner, slots, weights, sem, 22, 4):
            copy.wait()

    def project(c, _):
        rows = rows_of(c, MM_ROWS)
        normed = n3[rows, :]
        q[rows, :] = (mm(normed, weights[0]) + vec[10:11]).astype(BF16) * 0.125
        k[rows, :] = mm(normed, weights[1]).astype(BF16)
        v[rows, :] = (mm(normed, weights[2]) + vec[11:12]).astype(BF16)
        da[rows, :] = mm_t(dyb[rows, :], weights[3]).astype(BF16)
        return 0

    chunks(HW // MM_ROWS, project)
    n3t[...] = n3[...].T
    qt[...] = q[...].T
    dat[...] = da[...].T

    def head_pair(pair, _):
        cols = pl.ds(pl.multiple_of(pair * 128, 128), 128)
        dkt[...] = jnp.zeros((128, HW), F32)
        dvt[...] = jnp.zeros((128, HW), F32)

        def query_rows(c, _):
            rows = rows_of(c, QROWS)
            keys = k[:, cols]
            values = v[:, cols]
            q_pair = q[rows, cols]
            da_pair = da[rows, cols]
            lane = lax.broadcasted_iota(jnp.int32, (QROWS, 128), 1)
            parts = []
            for side in range(2):
                mine = (lane < HEAD) if side == 0 else (lane >= HEAD)
                q_one = jnp.where(mine, q_pair, jnp.zeros_like(q_pair))
                da_one = jnp.where(mine, da_pair, jnp.zeros_like(da_pair))
                head_rows = pl.ds(pl.multiple_of(pair * 128 + side * HEAD, HEAD), HEAD)
                scores = mm_t(q_one, keys)
                top = jnp.max(scores, axis=1, keepdims=True)
                expo = jnp.exp(scores - top)
                probs = expo * (1.0 / jnp.sum(expo, axis=1, keepdims=True))
                low = probs.astype(BF16)
                dprobs = mm_t(da_one, values)
                dot = jnp.sum(probs * dprobs, axis=1, keepdims=True)
                dscores = (probs * (dprobs - dot)).astype(BF16)
                acc_rows = slice(side * HEAD, (side + 1) * HEAD)
                dvt[acc_rows, :] += mm(dat[head_rows, rows], low)
                dkt[acc_rows, :] += mm(qt[head_rows, rows], dscores)
                parts.append((mm(low, values), mm(dscores, keys)))
            first = lane < HEAD
            att[rows, cols] = jnp.where(first, parts[0][0], parts[1][0]).astype(BF16)
            dq[rows, cols] = (jnp.where(first, parts[0][1], parts[1][1]) * 0.125).astype(BF16)
            return 0

        chunks(HW // QROWS, query_rows)
        dk[:, cols] = dkt[...].astype(BF16).T
        dv[:, cols] = dvt[...].astype(BF16).T
        return 0

    chunks(HEADS // 2, head_pair)

    is_live = live[step] > 0

    def result(c, _):
        rows = rows_of(c, MM_ROWS)
        y = r1[0, rows, :] + mm(att[rows, :], weights[3]) + vec[12:13]
        out[0, rows, :] = jnp.where(is_live, y, 0.0).astype(BF16)
        dn3[rows, :] = (
            mm_t(dq[rows, :], weights[0])
            + mm_t(dk[rows, :], weights[1])
            + mm_t(dv[rows, :], weights[2])
        )
        return 0

    chunks(HW // MM_ROWS, result)

    qt[...] = att[...].T
    terms = (
        lambda: mm(n3t[...], dq[...]),
        lambda: mm(n3t[...], dk[...]),
        lambda: mm(n3t[...], dv[...]),
        lambda: mm(qt[...], dyb[...]),
    )
    for n, term in enumerate(terms):
        @pl.when(step == 0)
        def _(n=n, term=term):
            acc[n] = term()

        @pl.when(step != 0)
        def _(n=n, term=term):
            grads[n] = (acc[n] + term()).astype(BF16)

    def column_sums(c, totals):
        rows = rows_of(c, ROWS)
        grad = dn3[rows, :]
        new = (
            grad * nhat[rows, :],
            grad,
            dq[rows, :].astype(F32),
            dv[rows, :].astype(F32),
        )
        return tuple(t + jnp.sum(n, axis=0, keepdims=True) for t, n in zip(totals, new))

    sum_cross, sum_grad, sum_q, sum_v = chunks(HW // ROWS, column_sums, (zero,) * 4)
    sums[...] += jnp.concatenate(
        [sum_cross, sum_grad, sum_q, sum_v, sum_dy, jnp.zeros((3, C), F32)], axis=0
    )
    mean_grad = group_mean(gain * sum_grad)
    mean_cross = group_mean(gain * sum_cross)

    def back(c, _):
        rows = rows_of(c, ROWS)
        inner = gain * dn3[rows, :] - mean_grad - nhat[rows, :] * mean_cross
        dr1[0, rows, :] = cot[0, rows, :].astype(F32) * image_weight + inv * inner
        return 0

    chunks(HW // ROWS, back)


def split_three(value):
    high = value.astype(BF16)
    rest = value - high.astype(F32)
    middle = rest.astype(BF16)
    return high, middle, (rest - middle.astype(F32)).astype(BF16)


def bwd_two(
    owner, slots, dr1, a2, nhat, stats, vec, emb, actt, dh1, grads, map_grads, demb, sums,
    weights, maps, slab, at, dz, keep, sem,
):
    step = pl.program_id(0)
    last = pl.num_programs(0) - 1

    def copies():
        return block_copies(owner, slots, weights, sem, 9, 9) + block_copies_at(
            owner, slots, maps, sem, 18, 4, 9
        )

    @pl.when(step == 0)
    def _():
        for copy in copies():
            copy.start()
        clear_pads(slab)
        sums[...] = jnp.zeros((8, C), F32)

    zero = jnp.zeros((1, C), F32)

    def fill(c, total):
        chunk = dr1[0, rows_of(c, ROWS), :]
        store_slab(slab, (step,), c, chunk)
        return total + jnp.sum(chunk.astype(BF16).astype(F32), axis=0, keepdims=True)

    sum_h2 = chunks(HW // ROWS, fill, zero)
    at[step] = a2[0].T

    @pl.when(step == 0)
    def _():
        for copy in copies():
            copy.wait()

    scale = 1.0 + stats[0, 0:1]
    shift = stats[0, 1:2]
    inv = stats[0, 2:3]
    gain = vec[5:6]
    bias = vec[6:7]

    def conv(c, _):
        dz[rows_of(c, CONV_ROWS), :] = conv_rows(
            slab, (step,), weights, c * CONV_ROWS, CONV_ROWS, True
        )
        return 0

    chunks(HW // CONV_ROWS, conv)

    def slope(c, totals):
        rows = rows_of(c, ROWS)
        normed = nhat[0, rows, :]
        pre = (normed * gain + bias) * scale + shift
        grad = dz[rows, :] * silu_slope(pre)
        dz[rows, :] = grad
        return (
            totals[0] + jnp.sum(grad, axis=0, keepdims=True),
            totals[1] + jnp.sum(grad * normed, axis=0, keepdims=True),
        )

    sum_dz, sum_cross = chunks(HW // ROWS, slope, (zero, zero))
    factor = scale * gain
    mean_grad = group_mean(factor * sum_dz)
    mean_cross = group_mean(factor * sum_cross)

    def back(c, total):
        rows = rows_of(c, ROWS)
        low = (inv * (factor * dz[rows, :] - mean_grad - nhat[0, rows, :] * mean_cross)).astype(BF16)
        dh1[0, rows, :] = low
        return total + jnp.sum(low.astype(F32), axis=0, keepdims=True)

    sum_h1 = chunks(HW // ROWS, back, zero)
    dscale = gain * sum_cross + bias * sum_dz
    sums[...] += jnp.concatenate(
        [sum_h1, dscale, sum_dz, scale * sum_cross, scale * sum_dz, sum_h2, jnp.zeros((2, C), F32)],
        axis=0,
    )
    pieces_scale = split_three(dscale)
    pieces_shift = split_three(sum_dz)
    blank = jnp.zeros((5, C), F32)

    def stack(pieces):
        return jnp.concatenate([p.astype(F32) for p in pieces] + [blank], axis=0).astype(BF16)

    d_scale = stack(pieces_scale)
    d_shift = stack(pieces_shift)

    def reach(upper):
        parts = mm_t(d_scale, maps[upper]) + mm_t(d_shift, maps[2 + upper])
        return jnp.sum(parts, axis=0, keepdims=True)

    row = jnp.concatenate([reach(0), reach(1)], axis=1)
    demb[0] = jnp.broadcast_to(row * silu_slope(emb[0, 0:1].astype(F32)), (8, EMB))
    keep[step, 0] = d_scale
    keep[step, 1] = d_shift

    @pl.when(step == last)
    def _():
        def tap_grad(tap, _):
            di = 2 - tap // 3
            dj = tap // 3 * 3 + 2 - tap
            rows = pl.ds(pl.multiple_of(di * SIDE, SIDE), HW)
            grads[tap] = (mm(at[0], slab[0, dj, rows, :]) + mm(at[1], slab[1, dj, rows, :])).astype(
                BF16
            )
            return 0

        chunks(9, tap_grad)
        for n in range(4):
            half = n % 2
            seg = slice(half * C, (half + 1) * C)
            map_grads[n] = (
                mm(actt[0, seg, :], keep[0, n // 2]) + mm(actt[1, seg, :], keep[1, n // 2])
            ).astype(BF16)


def bwd_one_taps(dh1, a1, grads, slab, at):
    step = pl.program_id(0)

    @pl.when(step == 0)
    def _():
        clear_pads(slab)

    def fill(c, _):
        store_slab(slab, (step,), c, dh1[0, rows_of(c, ROWS), :].astype(F32))
        return 0

    chunks(HW // ROWS, fill)
    at[step] = a1[0].T

    @pl.when(step == pl.num_programs(0) - 1)
    def _():
        def tap_grad(tap, _):
            di = 2 - tap // 3
            dj = tap // 3 * 3 + 2 - tap
            rows = pl.ds(pl.multiple_of(di * SIDE, SIDE), HW)
            grads[tap] = (mm(at[0], slab[0, dj, rows, :]) + mm(at[1], slab[1, dj, rows, :])).astype(
                BF16
            )
            return 0

        chunks(9, tap_grad)


def bwd_one_data(owner, slots, dh1, x, dr1, vec, dx, sums, weights, slab, dp, sem):
    step = pl.program_id(0)

    @pl.when(step == 0)
    def _():
        for copy in block_copies(owner, slots, weights, sem, 0, 9):
            copy.start()
        clear_pads(slab)
        sums[...] = jnp.zeros((8, C), F32)

    def fill(c, _):
        store_slab(slab, (), c, dh1[0, rows_of(c, ROWS), :].astype(F32))
        return 0

    chunks(HW // ROWS, fill)

    def read(rows):
        return x[0, rows, :].astype(F32)

    mean, inv = norm_stats(read)
    gain = vec[0:1]
    bias = vec[1:2]

    @pl.when(step == 0)
    def _():
        for copy in block_copies(owner, slots, weights, sem, 0, 9):
            copy.wait()

    def conv(c, _):
        dp[rows_of(c, CONV_ROWS), :] = conv_rows(
            slab, (), weights, c * CONV_ROWS, CONV_ROWS, True
        )
        return 0

    chunks(HW // CONV_ROWS, conv)
    zero = jnp.zeros((1, C), F32)

    def slope(c, totals):
        rows = rows_of(c, ROWS)
        normed = (read(rows) - mean) * inv
        grad = dp[rows, :] * silu_slope(normed * gain + bias)
        dp[rows, :] = grad
        return (
            totals[0] + jnp.sum(grad * normed, axis=0, keepdims=True),
            totals[1] + jnp.sum(grad, axis=0, keepdims=True),
        )

    sum_cross, sum_grad = chunks(HW // ROWS, slope, (zero, zero))
    sums[...] += jnp.concatenate([sum_cross, sum_grad, jnp.zeros((6, C), F32)], axis=0)
    mean_grad = group_mean(gain * sum_grad)
    mean_cross = group_mean(gain * sum_cross)

    def back(c, _):
        rows = rows_of(c, ROWS)
        normed = (read(rows) - mean) * inv
        dx[0, rows, :] = dr1[0, rows, :] + inv * (
            gain * dp[rows, :] - mean_grad - normed * mean_cross
        )
        return 0

    chunks(HW // ROWS, back)


def per_image(*shape):
    return pl.BlockSpec((1,) + shape, lambda i: (i,) + (0,) * len(shape))


def whole(*shape):
    return pl.BlockSpec(shape, lambda i: (0,) * len(shape))


def struct(shape, kind):
    return jax.ShapeDtypeStruct(shape, kind)


def call(body, images, in_specs, out_specs, out_shape, scratch, args, name):
    return pl.pallas_call(
        body,
        grid=(images,),
        in_specs=in_specs,
        out_specs=out_specs,
        out_shape=out_shape,
        scratch_shapes=scratch,
        name=name,
        compiler_params=pltpu.CompilerParams(
            vmem_limit_bytes=VMEM_LIMIT, dimension_semantics=("arbitrary",)
        ),
    )(*args)


IMAGE = per_image(HW, C)
VEC = whole(VECS, C)
TAPS = whole(9, C, C)


def layer(images, embeds, cotangent, weight, live, owner, slots, vectors):
    count = images.shape[0]
    big = lambda kind: struct((count, HW, C), kind)
    taps = pltpu.VMEM((9, C, C), BF16)
    slab = pltpu.VMEM((3, SLAB, C), BF16)
    slabs = pltpu.VMEM((count, 3, SLAB, C), BF16)
    h1, a1 = call(
        fwd_one, count, [SMEM, ANY, IMAGE, VEC], [IMAGE, IMAGE], [big(F32), big(BF16)],
        [taps, slab, pltpu.SemaphoreType.DMA((9,))],
        (owner, slots, images, vectors), "first_conv",
    )
    emb = embeds.astype(F32)
    act = jax.nn.silu(emb).astype(BF16)
    act_rows = jnp.broadcast_to(act[:, None, :], (count, 16, EMB))
    a2, r1, nhat, stats = call(
        fwd_two, count, [SMEM, ANY, IMAGE, IMAGE, per_image(16, EMB), VEC],
        [IMAGE, IMAGE, IMAGE, per_image(8, C)],
        [big(BF16), big(F32), big(F32), struct((count, 8, C), F32)],
        [taps, pltpu.VMEM((4, C, C), BF16), slab, pltpu.SemaphoreType.DMA((13,))],
        (owner, slots, h1, images, act_rows, vectors), "second_conv",
    )
    low = pltpu.VMEM((HW, C), BF16)
    lowt = pltpu.VMEM((C, HW), BF16)
    full = pltpu.VMEM((HW, C), F32)
    pair = pltpu.VMEM((128, HW), F32)
    out, dr1, grads_attn, sums_attn = call(
        attention, count, [SMEM, ANY, SMEM, SMEM, IMAGE, IMAGE, VEC],
        [IMAGE, IMAGE, whole(4, C, C), whole(8, C)],
        [big(BF16), big(F32), struct((4, C, C), BF16), struct((8, C), F32)],
        [pltpu.VMEM((4, C, C), BF16), full, low, lowt, low, low, low, low, lowt, lowt, low, low,
         low, low, low, pair, pair, full, pltpu.VMEM((4, C, C), F32), pltpu.SemaphoreType.DMA((4,))],
        (owner, slots, weight, live, r1, cotangent, vectors), "attention",
    )
    actt = jnp.pad(jnp.broadcast_to(act[:, :, None], (count, EMB, 3)), ((0, 0), (0, 0), (0, 5)))
    emb_rows = jnp.broadcast_to(emb[:, None, :], (count, 8, EMB))
    dh1, grads_two, grads_maps, demb, sums_two = call(
        bwd_two, count,
        [SMEM, ANY, IMAGE, IMAGE, IMAGE, per_image(8, C), VEC, per_image(8, EMB), whole(count, EMB, 8)],
        [IMAGE, TAPS, whole(4, C, C), per_image(8, EMB), whole(8, C)],
        [big(BF16), struct((9, C, C), BF16), struct((4, C, C), BF16), struct((count, 8, EMB), F32),
         struct((8, C), F32)],
        [taps, pltpu.VMEM((4, C, C), BF16), slabs, pltpu.VMEM((count, C, HW), BF16), full,
         pltpu.VMEM((count, 2, 8, C), BF16), pltpu.SemaphoreType.DMA((13,))],
        (owner, slots, dr1, a2, nhat, stats, vectors, emb_rows, actt), "second_conv_back",
    )
    (grads_one,) = call(
        bwd_one_taps, count, [IMAGE, IMAGE], [TAPS], [struct((9, C, C), BF16)],
        [slabs, pltpu.VMEM((count, C, HW), BF16)], (dh1, a1), "first_conv_taps",
    )
    dx, sums_one = call(
        bwd_one_data, count, [SMEM, ANY, IMAGE, IMAGE, IMAGE, VEC], [IMAGE, whole(8, C)],
        [big(F32), struct((8, C), F32)],
        [taps, slab, full, pltpu.SemaphoreType.DMA((9,))],
        (owner, slots, dh1, images, dr1, vectors), "first_conv_back",
    )
    grads = (grads_one, grads_two, grads_maps, grads_attn)
    grad_vectors = jnp.concatenate([sums_one[:2], sums_two[:6], sums_attn[:5]], axis=0)
    return out, dx, demb[:, 0], grads, grad_vectors


def shards(
    images,
    embeds,
    cotangent,
    counts,
    bucket_weight,
    owner,
    master,
    first_moment,
    second_moment,
    left_basis,
    right_basis,
    vec_master,
    vec_first,
    vec_second,
):
    mat_dev = master.shape[0]
    mats_all = mat_dev * lax.axis_size("shard")
    slot_weights, vec_full = (
        lax.all_gather(master.astype(jnp.bfloat16), "shard", axis=0, tiled=True),
        lax.all_gather(vec_master.astype(jnp.bfloat16), "shard", axis=1, tiled=True),
    )
    vectors = vec_full.astype(jnp.float32)
    slot_ids = jnp.arange(images.shape[0], dtype=jnp.int32)
    live = (slot_ids < counts[0, 0] + counts[0, 1]).astype(jnp.int32)
    weight = jnp.where(slot_ids < counts[0, 0], bucket_weight[0], bucket_weight[1])
    weight = jnp.where(live > 0, weight, 0.0)
    outputs, grad_images, grad_embeds, grads, grad_vectors = layer(
        images, embeds, cotangent, weight, live, owner, slot_weights, vectors
    )
    one, two, maps, attn = grads
    grad_blocks = jnp.concatenate([one, two, maps, attn], axis=0)
    block_ids = jnp.arange(mats_all, dtype=jnp.int32)
    all_slots = jnp.sum(
        jnp.where(owner[None, :] == block_ids[:, None], block_ids[None, :], 0), axis=1
    )
    slot_block = lax.dynamic_slice_in_dim(all_slots, lax.axis_index("shard") * mat_dev, mat_dev, 0)
    picked = jnp.take(grad_blocks, jnp.minimum(all_slots, BLOCKS - 1), axis=0)
    grad_slot = jnp.where((all_slots < BLOCKS)[:, None, None], picked, jnp.zeros((), BF16))
    own_grads, own_vec = (
        lax.psum_scatter(grad_slot, "shard", scatter_dimension=0, tiled=True),
        lax.psum_scatter(
            grad_vectors.astype(jnp.bfloat16), "shard", scatter_dimension=1, tiled=True
        ),
    )
    own_grads, own_vec = (
        lax.psum(own_grads, "rep").astype(jnp.float32),
        lax.psum(own_vec, "rep").astype(jnp.float32),
    )
    rotated = jnp.matmul(
        jnp.matmul(jnp.swapaxes(left_basis, 1, 2), own_grads, precision=PRECISE),
        right_basis,
        precision=PRECISE,
    )
    new_first = MOMENT_DECAY * first_moment + (1.0 - MOMENT_DECAY) * rotated
    new_second = MOMENT_DECAY * second_moment + (1.0 - MOMENT_DECAY) * rotated * rotated
    correction = 1.0 - MOMENT_DECAY**STEP
    direction = new_first / correction / (jnp.sqrt(new_second / correction) + ADAM_EPS)
    update = jnp.matmul(
        jnp.matmul(left_basis, direction, precision=PRECISE),
        jnp.swapaxes(right_basis, 1, 2),
        precision=PRECISE,
    )
    step_rate = jnp.where(slot_block < BLOCKS, 2.0 * block_spread(slot_block), 0.0)
    new_master = master - step_rate[:, None, None] * (update + WEIGHT_DECAY * master)
    vec_first_new = MOMENT_DECAY * vec_first + (1.0 - MOMENT_DECAY) * own_vec
    vec_second_new = MOMENT_DECAY * vec_second + (1.0 - MOMENT_DECAY) * own_vec * own_vec
    vec_master_new = vec_master - VECTOR_RATE * (vec_first_new / correction) / (
        jnp.sqrt(vec_second_new / correction) + ADAM_EPS
    )
    return (
        outputs,
        grad_images,
        grad_embeds,
        new_first,
        new_second,
        new_master,
        new_master.astype(jnp.bfloat16),
        vec_first_new,
        vec_second_new,
        vec_master_new,
        vec_master_new.astype(jnp.bfloat16),
    )


def solution(mesh):
    return jax.shard_map(
        shards,
        mesh=mesh,
        in_specs=(
            P(("rep", "shard"), None, None),
            P(("rep", "shard"), None),
            P(("rep", "shard"), None, None),
            P(("rep", "shard"), None),
            P(),
            P(),
            P("shard", None, None),
            P("shard", None, None),
            P("shard", None, None),
            P("shard", None, None),
            P("shard", None, None),
            P(None, "shard"),
            P(None, "shard"),
            P(None, "shard"),
        ),
        out_specs=(
            P(("rep", "shard"), None, None),
            P(("rep", "shard"), None, None),
            P(("rep", "shard"), None),
            P("shard", None, None),
            P("shard", None, None),
            P("shard", None, None),
            P("shard", None, None),
            P(None, "shard"),
            P(None, "shard"),
            P(None, "shard"),
            P(None, "shard"),
        ),
        check_vma=False,
    )
```

time: 1330 us -> 681 us (0.51)
  matrix products: 433 us -> 17.6 us
  Pallas kernels: 0 us -> 224 us
  local copies, waits for them, and re-layouts: 231 us -> 21 us
  other arithmetic: 220 us -> 31.5 us
  waiting for transfers between devices: 371 us -> 341 us
  loops' own time: 26.1 us -> 0 us
    dot_general x164 -> x0, matrix products: 415 us -> none  [the longest x36 66 us: conv_back_taps(): lax.dot_general(tap_view(padded, tap_index), grad_rows, dims, preferred_e...]
    pallas_call x0 -> x6, Pallas kernels: none -> 224 us  [call(): pl.pallas_call(body, grid=(images,), in_specs=in_specs, out_specs=out_spe...]
    convert_element_type x19 -> x2, other arithmetic: 72.9 us -> 0.53 us  [the longest x1 0.51 us: shards(): live = (slot_ids < counts[0, 0] + counts[0, 1]).astype(jnp.int32)]
    add x10 -> x0, other arithmetic: 54.9 us -> none  [the longest x2 54.8 us: one_image(): grad_blocks + block_terms]
    slice x28 -> x6, local copies, waits for them, and re-layouts: 53 us -> 2.74 us  [the longest x1 0.84 us: layer(): return (out, dx, demb[:, 0], grads, grad_vectors)]
    reduce_sum x42 -> x0, other arithmetic: 45 us -> none  [the longest x4 13.8 us: one_block(): row_total = jnp.sum(exponent, axis=-1, keepdims=True)]
    dynamic_update_slice x18 -> x0, local copies, waits for them, and re-layouts: 31.7 us -> none  [the longest x16 31.6 us: attend(): mixed_rows, log_total = lax.map(one_block, starts)]
    gather x2 -> x1, local copies, waits for them, and re-layouts: 40 us -> 12.2 us  [shards(): picked = jnp.take(grad_blocks, jnp.minimum(all_slots, BLOCKS - 1), axis=0)]
  transfers between devices with their start and end apart: 4 -> 4, of which waited for: 4 -> 4; matrix products, arithmetic and copies ran while one was open for 0% -> 2% of each run, Pallas kernels for 0% -> 4%
where the time goes in v1:
time: 681 us; the launch traced here: 680 us
  waiting for transfers between devices  341 us (50%)
  Pallas kernels  224 us (33%)
  other arithmetic  31.5 us (5%)
  blocking collectives  28.7 us (4%)
  local copies, waits for them, and re-layouts  21 us (3%)
  matrix products  17.6 us (3%)
  between operations  15.4 us (2%)
    pallas_call x6, Pallas kernels, call(): pl.pallas_call(body, grid=(images,), in_specs=in_specs, out_specs=out_spe...  224 us
    reduce_scatter x1, waiting for transfers between devices, shards(): lax.psum_scatter(grad_slot, 'shard', scatter_dimension=0, tiled=True)  150 us
    all_gather x1, waiting for transfers between devices, shards(): lax.all_gather(master.astype(jnp.bfloat16), 'shard', axis=0, tiled=True)  98.9 us
    unnamed x5, waiting for transfers between devices  56.6 us
    psum x1, waiting for transfers between devices, shards(): lax.psum(own_grads, 'rep').astype(jnp.float32)  34.9 us
    all_gather x1, blocking collectives, shards(): lax.all_gather(vec_master.astype(jnp.bfloat16), 'shard', axis=1, tiled=True)  23.8 us
    select_n x1, other arithmetic, shards(): jnp.where((all_slots < BLOCKS)[:, None, None], picked, jnp.zeros((), BF16))  14.3 us
  transfers between devices with their start and end apart: 4, of which 4 were waited for; matrix products, arithmetic and copies ran while one was open for 2% of the time, Pallas kernels for 4%

profile of v1, /device:TPU:0, one launch (start us, length us, event | category | flops | bytes accessed | tf_op | source)
XLA Modules:
  0.0 679.8 jit_solution(15190742407112798941)
XLA Ops:
  7.2 0.0 copy-start
  7.2 0.0 all-gather.3.cloned.1.call-start
  7.3 2.8 convert_element_type.31
  10.1 0.0 all-gather.3.cloned.1.call-update
  10.1 0.0 reduce-scatter.5.cloned.1.call-start
  10.2 23.8 %all-gather = bf16[16,32,13]{1,2,0:T(8,128)(2,1)S(1)} all-gather(bf16[1,32,13]{1,2,0:T(8,128)(2,1)S(1)} %convert_bitcast_fusion), channel_id=1, replica_groups=mesh['rep'=2,'shard'=16] {'shard'}, dimensions={0}, use_global_device_ids=true | all-gather | bytes 14144 | tf_op jit(solution)/shard_map/all_gather | solution.py:736
  34.0 0.7 reshape.63
  34.7 0.6 fusion.17
  36.6 0.3 broadcast_in_dim.95
  37.0 0.9 pad.4.actt
  37.9 0.5 compare_convert_fusion.live
  38.4 0.6 fusion.18
  39.0 2.5 compare_select_fusion.7.weight
  41.4 0.1 select_reduce_fusion
  41.6 98.9 %all-gather.3.cloned.1.call-done.slots = bf16[32,512,512]{2,1,0:T(8,128)(2,1)} async-done(((bf16[2,512,512]{2,1,0:T(8,128)(2,1)}), bf16[32,512,512]{2,1,0:T(8,128)(2,1)}) %all-gather.3.cloned.1.call-update) | async-done | bytes 16777232 | tf_op jit(solution)/shard_map/all_gather | solution.py:735
  140.5 18.2 %first_conv.1 = (f32[2,1024,512]{2,1,0:T(8,128)}, bf16[2,1024,512]{2,1,0:T(8,128)(2,1)}) custom-call(s32[32]{0:T(128)} %owner.9, bf16[32,512,512]{2,1,0:T(8,128)(2,1)} %all-gather.3.cloned.1.call-done.slots, bf16[2,1024,512]{2,1,0:T(8,128)(2,1)} %x.7, f32[13,512]{1,0:T(8,128)} %bitcast.29), custom_call_target="tpu_custom_call" | custom-call | tf_op jit(solution)/shard_map/first_conv/pallas_call | solution.py:637
  158.6 0.6 broadcast_in_dim.93.act
  159.3 21.4 %second_conv.1 = (bf16[2,1024,512]{2,1,0:T(8,128)(2,1)}, f32[2,1024,512]{2,1,0:T(8,128)}, f32[2,1024,512]{2,1,0:T(8,128)}, f32[2,8,512]{2,1,0:T(8,128)}) custom-call(s32[32]{0:T(128)} %owner.9, bf16[32,512,512]{2,1,0:T(8,128)(2,1)} %all-gather.3.cloned.1.call-done.slots, f32[2,1024,512]{2,1,0:T(8,128)} %get-tuple-element.28.h1, bf16[2,1024,512]{2,1,0:T(8,128)(2,1)} %x.7, ...), custom_call_target="tpu_custom_call" | custom-call | tf_op jit(solution)/shard_map/second_conv/pallas_call | solution.py:637
  180.7 103.8 %attention.1 = (bf16[2,1024,512]{2,1,0:T(8,128)(2,1)}, f32[2,1024,512]{2,1,0:T(8,128)}, bf16[4,512,512]{2,1,0:T(8,128)(2,1)}, f32[8,512]{1,0:T(8,128)}) custom-call(s32[32]{0:T(128)} %owner.9, bf16[32,512,512]{2,1,0:T(8,128)(2,1)} %all-gather.3.cloned.1.call-done.slots, f32[2]{0:T(128)} %compare_select_fusion.7.weight, s32[2]{0:T(128)} %compare_convert_fusion.live, ...), custom_call_target="tpu_custom_call" | custom-call | tf_op jit(solution)/shard_map/attention/pallas_call | solution.py:637
  284.4 0.6 broadcast_in_dim.94.emb
  285.1 40.0 %second_conv_back.1 = (bf16[2,1024,512]{2,1,0:T(8,128)(2,1)}, bf16[9,512,512]{2,1,0:T(8,128)(2,1)}, bf16[4,512,512]{2,1,0:T(8,128)(2,1)}, f32[2,8,1024]{2,1,0:T(8,128)}, f32[8,512]{1,0:T(8,128)}) custom-call(s32[32]{0:T(128)} %owner.9, bf16[32,512,512]{2,1,0:T(8,128)(2,1)} %all-gather.3.cloned.1.call-done.slots, f32[2,1024,512]{2,1,0:T(8,128)} %get-tuple-element.31.dr1, ...), custom_call_target="tpu_custom_call" | custom-call | tf_op jit(solution)/shard_map/second_conv_back/pallas_call | solution.py:637
  325.1 17.0 %first_conv_taps.1 = bf16[9,512,512]{2,1,0:T(8,128)(2,1)} custom-call(bf16[2,1024,512]{2,1,0:T(8,128)(2,1)} %get-tuple-element.35.dh1, bf16[2,1024,512]{2,1,0:T(8,128)(2,1)} %get-tuple-element.38.a1), custom_call_target="tpu_custom_call" | custom-call | tf_op jit(solution)/shard_map/first_conv_taps/pallas_call | solution.py:637
  342.1 10.5 %pad_maximum_fusion = bf16[26,512,512]{2,1,0:T(8,128)(2,1)} fusion(bf16[4,512,512]{2,1,0:T(8,128)(2,1)} %get-tuple-element.41, bf16[4,512,512]{2,1,0:T(8,128)(2,1)} %get-tuple-element.40, bf16[9,512,512]{2,1,0:T(8,128)(2,1)S(1)} %bitcast.28, bf16[9,512,512]{2,1,0:T(8,128)(2,1)} %first_conv_taps.1), kind=kLoop, calls=%fused_computation.2 | loop fusion | flops 20447232 | bytes 27262976 | tf_op jit(solution)/shard_map/concatenate | solution.py:747
  352.6 12.2 %gather_fusion = bf16[32,512,512]{2,1,0:T(8,128)(2,1)} fusion(bf16[26,512,512]{2,1,0:T(8,128)(2,1)} %pad_maximum_fusion, s32[1024]{0:T(1024)S(1)} %pad_clamp_fusion), kind=kCustom, calls=%fused_computation | custom fusion | bytes 33554560 | tf_op jit(solution)/shard_map/jit(_take)/gather | solution.py:753
  364.8 14.3 %select_select_fusion = bf16[32,512,512]{2,1,0:T(8,128)(2,1)} fusion(bf16[32,512,512]{2,1,0:T(8,128)(2,1)} %gather_fusion, pred[32]{0:T(512)(128)(4,1)S(1)} %get-tuple-element.52, pred[32]{0:T(512)(128)(4,1)S(1)} %get-tuple-element.51), kind=kLoop, calls=%fused_computation.1 | loop fusion | flops 16777216 | bytes 33554496 | tf_op jit(solution)/shard_map/jit(_where)/select_n | solution.py:754
  379.1 0.0 reduce-scatter.5.cloned.1.call-update
  379.1 0.0 reduce-scatter.7.cloned.1.call-start
  379.2 0.6 copy-done.12
  379.9 24.2 %first_conv_back.1 = (f32[2,1024,512]{2,1,0:T(8,128)}, f32[8,512]{1,0:T(8,128)}) custom-call(s32[32]{0:T(128)} %owner.9, bf16[32,512,512]{2,1,0:T(8,128)(2,1)} %all-gather.3.cloned.1.call-done.slots, bf16[2,1024,512]{2,1,0:T(8,128)(2,1)} %get-tuple-element.35.dh1, bf16[2,1024,512]{2,1,0:T(8,128)(2,1)} %x.7, f32[2,1024,512]{2,1,0:T(8,128)} %get-tuple-element.31.dr1, ...), custom_call_target="tpu_custom_call" | custom-call | tf_op jit(solution)/shard_map/first_conv_back/pallas_call | solution.py:637
  404.0 0.7 slice.46
  404.8 0.8 copy.41
  405.6 0.0 reduce-scatter.7.cloned.1.call-update
  405.6 0.0 all-reduce.3.cloned.1.call-start
  405.6 150.4 %reduce-scatter.5.cloned.1.call-done = bf16[2,512,512]{2,1,0:T(8,128)(2,1)} async-done(((bf16[32,512,512]{2,1,0:T(8,128)(2,1)}), bf16[2,512,512]{2,1,0:T(8,128)(2,1)}) %reduce-scatter.5.cloned.1.call-update) | async-done | bytes 1048592 | tf_op jit(solution)/shard_map/reduce_scatter | solution.py:756
  556.1 0.0 all-reduce.3.cloned.1.call-update
  556.1 0.1 compare_select_fusion.8
  556.2 0.8 slice.32
  557.0 0.6 copy.46
  557.6 56.6 %reduce-scatter.7.cloned.1.call-done = bf16[32,13]{1,0:T(8,128)(2,1)} async-done(((bf16[512,13]{1,0:T(8,128)(2,1)}), bf16[32,13]{1,0:T(8,128)(2,1)}) %reduce-scatter.7.cloned.1.call-update) | async-done | bytes 848
  614.2 0.8 copy.42
  615.0 4.9 psum.15
  619.9 0.6 fusion.15
  620.5 34.9 %all-reduce.3.cloned.1.call-done = bf16[2,512,512]{2,1,0:T(8,128)(2,1)} async-done(((bf16[2,512,512]{2,1,0:T(8,128)(2,1)}), bf16[2,512,512]{2,1,0:T(8,128)(2,1)}) %all-reduce.3.cloned.1.call-update) | async-done | bytes 1048592 | tf_op jit(solution)/shard_map/psum | solution.py:762
  655.5 3.9 fusion.20
  659.4 0.0 copy-start.2
  659.4 3.7 fusion
  663.2 4.7 fusion.1
  668.0 5.3 fusion.19
  (43 shorter events, 0.2 us)
Async XLA Ops:
  7.2 652.2 %copy-start = (f32[2,512,512]{2,1,0:T(8,128)S(1)}, f32[2,512,512]{2,1,0:T(8,128)}, u32[]{:S(2)}) copy-start(f32[2,512,512]{2,1,0:T(8,128)} %param.24) | copy-start | bytes 6291460
  7.2 3.0 copy-start.7
  7.2 27.5 %copy-start.14 = (s32[1,2]{1,0:T(1,128)S(1)}, s32[1,2]{1,0:T(1,128)}, u32[]{:S(2)}) copy-start(s32[1,2]{1,0:T(1,128)} %param.17) | copy-start | bytes 28
  7.2 29.4 %copy-start.8 = (bf16[2,1024]{1,0:T(2,128)(2,1)S(1)}, bf16[2,1024]{1,0:T(2,128)(2,1)}, u32[]{:S(2)}) copy-start(bf16[2,1024]{1,0:T(2,128)(2,1)} %param.15) | copy-start | bytes 12292
  7.2 133.2 %all-gather.3.cloned.1.call-start = ((), (), s32[]{:S(2)}) async-start(), calls=%async_computation.2 | async-start | bytes 17825792 | tf_op jit(solution)/shard_map/all_gather | solution.py:735
  10.1 28.3 %copy-start.15 = (f32[2]{0:T(128)S(1)}, f32[2]{0:T(128)}, u32[]{:S(2)}) copy-start(f32[2]{0:T(128)} %param.18) | copy-start | bytes 28
  10.1 31.3 %copy-start.9 = (s32[32]{0:T(128)S(1)}, s32[32]{0:T(128)}, u32[]{:S(2)}) copy-start(s32[32]{0:T(128)} %owner.9) | copy-start | bytes 388
  10.1 545.9 %reduce-scatter.5.cloned.1.call-start = ((), (), s32[]{:S(2)}) async-start(), calls=%async_computation.3 | async-start | bytes 17825792 | tf_op jit(solution)/shard_map/reduce_scatter | solution.py:756
  325.1 17.1 %slice-start = ((s8[4718592]{0:T(1024)(128)(4,1)}), s8[4194304]{0:T(1024)(128)(4,1)S(1)}, s32[]{:S(2)}) async-start(s8[4718592]{0:T(1024)(128)(4,1)} %bitcast.27), calls=%async_computation.6 | async-start | bytes 8388608
  325.1 17.1 %slice-start.1 = ((s8[4718592]{0:T(1024)(128)(4,1)}), s8[524288]{0:T(1024)(128)(4,1)S(1)}, s32[]{:S(2)}) async-start(s8[4718592]{0:T(1024)(128)(4,1)} %bitcast.27), calls=%async_computation.7 | async-start | bytes 1048576
  379.1 0.7 copy-start.12
  379.1 235.1 %reduce-scatter.7.cloned.1.call-start = ((), (), s32[]{:S(2)}) async-start(), calls=%async_computation.5 | async-start | bytes 139264
  379.8 24.9 %copy-start.13 = (f32[8,512]{1,0:T(8,128)S(1)}, f32[8,512]{1,0:T(8,128)}, u32[]{:S(2)}) copy-start(f32[8,512]{1,0:T(8,128)} %get-tuple-element.43) | copy-start | bytes 49156
  379.8 240.1 %copy-start.10 = (f32[13,32]{1,0:T(8,128)S(1)}, f32[13,32]{1,0:T(8,128)}, u32[]{:S(2)}) copy-start(f32[13,32]{1,0:T(8,128)} %param.27) | copy-start | bytes 4996
  379.8 240.1 %copy-start.11 = (f32[13,32]{1,0:T(8,128)S(1)}, f32[13,32]{1,0:T(8,128)}, u32[]{:S(2)}) copy-start(f32[13,32]{1,0:T(8,128)} %param.26) | copy-start | bytes 4996
  405.6 249.9 %all-reduce.3.cloned.1.call-start = ((), (), s32[]{:S(2)}) async-start(), calls=%async_computation.4 | async-start | bytes 2097152 | tf_op jit(solution)/shard_map/psum | solution.py:762
  655.5 3.9 copy-start.3
  655.5 3.9 copy-start.4
  659.4 3.8 copy-start.2
  663.1 4.8 copy-start.5
  663.2 4.8 copy-start.6
  663.2 4.8 copy-start.1
Sparse Core Ops, SparseCore 0:
  10.8 129.6 all-gather.2
  379.3 176.7 reduce-scatter.4
  560.1 54.0 reduce-scatter.6
  616.4 39.0 all-reduce.2

commit v2 on v1

--- a/solution.py
+++ b/solution.py
@@ -149,20 +149,78 @@
 CONV_ROWS = 512
 
 
-def block_copies(owner, slots, dest, sem, first, count, offset=0):
-    return [
-        pltpu.make_async_copy(slots.at[owner[first + n]], dest.at[offset + n], sem.at[offset + n])
-        for n in range(count)
-    ]
-
-
-def fwd_one(owner, slots, x, vec, h1, a1, weights, slab, sem):
+PIECES = 32
+PIECE = C // PIECES
+
+
+def piece_rows(ids, core, plane, line):
+    index = ((ids[0] ^ core) * 4 + (ids[1] ^ plane)) * 4 + (ids[2] ^ line)
+    return pl.ds(pl.multiple_of(index * PIECE, PIECE), PIECE)
+
+
+def flat_place(n):
+    return (n % 2 * 4 + n // 16 * 2 + n // 2 % 2) * 4 + n // 4 % 4
+
+
+def block_copies(ids, parts, dest, sem, first, count):
+    if len(parts) == 1:
+        return [
+            pltpu.make_async_copy(
+                parts[0].at[n, pl.ds(first, count)],
+                dest.at[:, pl.ds(flat_place(n) * PIECE, PIECE), :],
+                sem.at[n],
+            )
+            for n in range(PIECES)
+        ]
+    copies = []
+    for core in range(2):
+        for plane in range(4):
+            for line in range(4):
+                copies.append(
+                    pltpu.make_async_copy(
+                        parts[core * 4 + plane].at[line, pl.ds(first, count)],
+                        dest.at[:, piece_rows(ids, core, plane, line), :],
+                        sem.at[len(copies)],
+                    )
+                )
+    return copies
+
+
+def start_all(*args):
+    for copy in block_copies(*args):
+        copy.start()
+
+
+def wait_all(*args):
+    for copy in block_copies(*args):
+        copy.wait()
+
+
+def store_flat(out, block, grad):
+    for n in range(PIECES):
+        place = flat_place(n) * PIECE
+        out[n % 16, block, n // 16] = grad[place : place + PIECE]
+
+
+def store_pieces(ids, keep, send, block, grad):
+    half = C // 2
+    mine = ids[0] == 0
+    kept = jnp.where(mine, grad[:half], grad[half:])
+    sent = jnp.where(mine, grad[half:], grad[:half])
+    for plane in range(4):
+        for line in range(4):
+            rows = slice((plane * 4 + line) * PIECE, (plane * 4 + line + 1) * PIECE)
+            keep[plane ^ ids[1], line ^ ids[2], block] = kept[rows]
+            send[plane ^ ids[1], line ^ ids[2], block] = sent[rows]
+
+
+def fwd_one(ids, *refs):
+    parts, (x, vec, h1, a1, weights, slab, sem) = refs[:8], refs[8:]
     step = pl.program_id(0)
 
     @pl.when(step == 0)
     def _():
-        for copy in block_copies(owner, slots, weights, sem, 0, 9):
-            copy.start()
+        start_all(ids, parts, weights, sem, 0, 9)
         clear_pads(slab)
 
     def read(rows):
@@ -184,8 +242,7 @@
 
     @pl.when(step == 0)
     def _():
-        for copy in block_copies(owner, slots, weights, sem, 0, 9):
-            copy.wait()
+        wait_all(ids, parts, weights, sem, 0, 9)
 
     def conv(c, _):
         h1[0, rows_of(c, CONV_ROWS), :] = (
@@ -196,26 +253,22 @@
     chunks(HW // CONV_ROWS, conv)
 
 
-def fwd_two(owner, slots, h1, x, act, vec, a2, r1, nhat, stats, weights, maps, slab, sem):
+def fwd_two(ids, *refs):
+    parts = refs[:8]
+    h1, x, act, vec, a2, r1, nhat, stats, weights, maps, slab, sem, map_sem = refs[8:]
     step = pl.program_id(0)
 
-    def copies():
-        return block_copies(owner, slots, maps, sem, 18, 4) + block_copies_at(
-            owner, slots, weights, sem, 9, 9, 4
-        )
-
-    @pl.when(step == 0)
-    def _():
-        for copy in copies():
-            copy.start()
+    @pl.when(step == 0)
+    def _():
+        start_all(ids, parts, maps, map_sem, 9, 4)
+        start_all(ids, parts, weights, sem, 0, 9)
         clear_pads(slab)
 
     mean, inv = norm_stats(lambda rows: h1[0, rows, :])
 
     @pl.when(step == 0)
     def _():
-        for copy in block_copies(owner, slots, maps, sem, 18, 4):
-            copy.wait()
+        wait_all(ids, parts, maps, map_sem, 9, 4)
 
     row = act[0]
     scale = (mm(row[:, :C], maps[0]) + mm(row[:, C:], maps[1]))[0:1] + vec[3:4]
@@ -238,8 +291,7 @@
 
     @pl.when(step == 0)
     def _():
-        for copy in block_copies_at(owner, slots, weights, sem, 9, 9, 4):
-            copy.wait()
+        wait_all(ids, parts, weights, sem, 0, 9)
 
     def conv(c, _):
         rows = rows_of(c, CONV_ROWS)
@@ -250,26 +302,19 @@
     chunks(HW // CONV_ROWS, conv)
 
 
-def block_copies_at(owner, slots, dest, sem, first, count, sem_from):
-    return [
-        pltpu.make_async_copy(slots.at[owner[first + n]], dest.at[n], sem.at[sem_from + n])
-        for n in range(count)
-    ]
-
-
 MM_ROWS = 512
 
 
-def attention(
-    owner, slots, weight, live, r1, cot, vec, out, dr1, grads, sums,
-    weights, nhat, n3, n3t, q, k, v, da, dat, qt, att, dyb, dq, dk, dv, dkt, dvt, dn3, acc, sem,
-):
+def attention(ids, weight, live, *refs):
+    parts = refs[:1]
+    (
+    r1, cot, vec, out, dr1, grads, sums, weights, nhat, n3, n3t, q, k, v, da, dat, qt, att, dyb, dq, dk, dv, dkt, dvt, dn3, acc, sem,
+    ) = refs[1:]
     step = pl.program_id(0)
 
     @pl.when(step == 0)
     def _():
-        for copy in block_copies(owner, slots, weights, sem, 22, 4):
-            copy.start()
+        start_all(ids, parts, weights, sem, 0, 4)
         sums[...] = jnp.zeros((8, C), F32)
 
     mean, inv = norm_stats(lambda rows: r1[0, rows, :])
@@ -291,8 +336,7 @@
 
     @pl.when(step == 0)
     def _():
-        for copy in block_copies(owner, slots, weights, sem, 22, 4):
-            copy.wait()
+        wait_all(ids, parts, weights, sem, 0, 4)
 
     def project(c, _):
         rows = rows_of(c, MM_ROWS)
@@ -379,7 +423,7 @@
 
         @pl.when(step != 0)
         def _(n=n, term=term):
-            grads[n] = (acc[n] + term()).astype(BF16)
+            store_flat(grads, n, (acc[n] + term()).astype(BF16))
 
     def column_sums(c, totals):
         rows = rows_of(c, ROWS)
@@ -415,22 +459,16 @@
     return high, middle, (rest - middle.astype(F32)).astype(BF16)
 
 
-def bwd_two(
-    owner, slots, dr1, a2, nhat, stats, vec, emb, actt, dh1, grads, map_grads, demb, sums,
-    weights, maps, slab, at, dz, keep, sem,
-):
+def bwd_two_data(ids, *refs):
+    parts = refs[:8]
+    dr1, nhat, stats, vec, emb, dh1, dvec, demb, sums = refs[8:17]
+    weights, maps, slab, dz, sem, map_sem = refs[17:]
     step = pl.program_id(0)
-    last = pl.num_programs(0) - 1
-
-    def copies():
-        return block_copies(owner, slots, weights, sem, 9, 9) + block_copies_at(
-            owner, slots, maps, sem, 18, 4, 9
-        )
-
-    @pl.when(step == 0)
-    def _():
-        for copy in copies():
-            copy.start()
+
+    @pl.when(step == 0)
+    def _():
+        start_all(ids, parts, weights, sem, 0, 9)
+        start_all(ids, parts, maps, map_sem, 9, 4)
         clear_pads(slab)
         sums[...] = jnp.zeros((8, C), F32)
 
@@ -438,16 +476,15 @@
 
     def fill(c, total):
         chunk = dr1[0, rows_of(c, ROWS), :]
-        store_slab(slab, (step,), c, chunk)
+        store_slab(slab, (), c, chunk)
         return total + jnp.sum(chunk.astype(BF16).astype(F32), axis=0, keepdims=True)
 
     sum_h2 = chunks(HW // ROWS, fill, zero)
-    at[step] = a2[0].T
-
-    @pl.when(step == 0)
-    def _():
-        for copy in copies():
-            copy.wait()
+
+    @pl.when(step == 0)
+    def _():
+        wait_all(ids, parts, weights, sem, 0, 9)
+        wait_all(ids, parts, maps, map_sem, 9, 4)
 
     scale = 1.0 + stats[0, 0:1]
     shift = stats[0, 1:2]
@@ -457,7 +494,7 @@
 
     def conv(c, _):
         dz[rows_of(c, CONV_ROWS), :] = conv_rows(
-            slab, (step,), weights, c * CONV_ROWS, CONV_ROWS, True
+            slab, (), weights, c * CONV_ROWS, CONV_ROWS, True
         )
         return 0
 
@@ -507,64 +544,67 @@
 
     row = jnp.concatenate([reach(0), reach(1)], axis=1)
     demb[0] = jnp.broadcast_to(row * silu_slope(emb[0, 0:1].astype(F32)), (8, EMB))
-    keep[step, 0] = d_scale
-    keep[step, 1] = d_shift
-
-    @pl.when(step == last)
-    def _():
-        def tap_grad(tap, _):
-            di = 2 - tap // 3
-            dj = tap // 3 * 3 + 2 - tap
-            rows = pl.ds(pl.multiple_of(di * SIDE, SIDE), HW)
-            grads[tap] = (mm(at[0], slab[0, dj, rows, :]) + mm(at[1], slab[1, dj, rows, :])).astype(
-                BF16
-            )
+    dvec[0] = jnp.concatenate([dscale, sum_dz, jnp.zeros((6, C), F32)], axis=0)
+
+
+def fill_taps(grad, act, slab, at):
+    step = pl.program_id(0)
+
+    @pl.when(step == 0)
+    def _():
+        clear_pads(slab)
+
+    def fill(c, _):
+        store_slab(slab, (step,), c, grad[0, rows_of(c, ROWS), :].astype(F32))
+        return 0
+
+    chunks(HW // ROWS, fill)
+    at[step] = act[0].T
+
+
+def tap_grad(slab, at, tap):
+    di = 2 - tap // 3
+    dj = tap // 3 * 3 + 2 - tap
+    rows = pl.ds(pl.multiple_of(di * SIDE, SIDE), HW)
+    total = mm(at[0], slab[0, dj, rows, :])
+    for image in range(1, slab.shape[0]):
+        total = total + mm(at[image], slab[image, dj, rows, :])
+    return total.astype(BF16)
+
+
+def one_taps(ids, grad, act, keep, send, slab, at):
+    fill_taps(grad, act, slab, at)
+
+    @pl.when(pl.program_id(0) == pl.num_programs(0) - 1)
+    def _():
+        def one(tap, _):
+            store_pieces(ids, keep, send, tap, tap_grad(slab, at, tap))
             return 0
 
-        chunks(9, tap_grad)
-        for n in range(4):
-            half = n % 2
-            seg = slice(half * C, (half + 1) * C)
-            map_grads[n] = (
-                mm(actt[0, seg, :], keep[0, n // 2]) + mm(actt[1, seg, :], keep[1, n // 2])
-            ).astype(BF16)
-
-
-def bwd_one_taps(dh1, a1, grads, slab, at):
+        chunks(9, one)
+
+
+def two_taps(grad, act, others, out, slab, at):
+    fill_taps(grad, act, slab, at)
+
+    @pl.when(pl.program_id(0) == pl.num_programs(0) - 1)
+    def _():
+        out[:, pl.ds(9, 4)] = others[...]
+
+        def one(tap, _):
+            store_flat(out, tap, tap_grad(slab, at, tap))
+            return 0
+
+        chunks(9, one)
+
+
+def bwd_one_data(ids, *refs):
+    parts, (dh1, x, dr1, vec, dx, sums, weights, slab, dp, sem) = refs[:8], refs[8:]
     step = pl.program_id(0)
 
     @pl.when(step == 0)
     def _():
-        clear_pads(slab)
-
-    def fill(c, _):
-        store_slab(slab, (step,), c, dh1[0, rows_of(c, ROWS), :].astype(F32))
-        return 0
-
-    chunks(HW // ROWS, fill)
-    at[step] = a1[0].T
-
-    @pl.when(step == pl.num_programs(0) - 1)
-    def _():
-        def tap_grad(tap, _):
-            di = 2 - tap // 3
-            dj = tap // 3 * 3 + 2 - tap
-            rows = pl.ds(pl.multiple_of(di * SIDE, SIDE), HW)
-            grads[tap] = (mm(at[0], slab[0, dj, rows, :]) + mm(at[1], slab[1, dj, rows, :])).astype(
-                BF16
-            )
-            return 0
-
-        chunks(9, tap_grad)
-
-
-def bwd_one_data(owner, slots, dh1, x, dr1, vec, dx, sums, weights, slab, dp, sem):
-    step = pl.program_id(0)
-
-    @pl.when(step == 0)
-    def _():
-        for copy in block_copies(owner, slots, weights, sem, 0, 9):
-            copy.start()
+        start_all(ids, parts, weights, sem, 0, 9)
         clear_pads(slab)
         sums[...] = jnp.zeros((8, C), F32)
 
@@ -583,8 +623,7 @@
 
     @pl.when(step == 0)
     def _():
-        for copy in block_copies(owner, slots, weights, sem, 0, 9):
-            copy.wait()
+        wait_all(ids, parts, weights, sem, 0, 9)
 
     def conv(c, _):
         dp[rows_of(c, CONV_ROWS), :] = conv_rows(
@@ -633,7 +672,7 @@
     return jax.ShapeDtypeStruct(shape, kind)
 
 
-def call(body, images, in_specs, out_specs, out_shape, scratch, args, name):
+def call(body, images, in_specs, out_specs, out_shape, scratch, args, name, flops=20 * 10**9):
     return pl.pallas_call(
         body,
         grid=(images,),
@@ -645,72 +684,245 @@
         compiler_params=pltpu.CompilerParams(
             vmem_limit_bytes=VMEM_LIMIT, dimension_semantics=("arbitrary",)
         ),
+        cost_estimate=pl.CostEstimate(flops=flops, bytes_accessed=30 * 2**20, transcendentals=0),
     )(*args)
 
 
 IMAGE = per_image(HW, C)
-VEC = whole(VECS, C)
-TAPS = whole(9, C, C)
-
-
-def layer(images, embeds, cotangent, weight, live, owner, slots, vectors):
+VEC = whole(16, C)
+PARTS = [ANY] * 8
+SEMS = pltpu.SemaphoreType.DMA((PIECES,))
+
+
+def layer(images, embeds, cotangent, weight, live, plan, gathered):
+    chunk_one, vectors, planes_two, chunk_attn = gathered
+    ids = plan.ids
     count = images.shape[0]
     big = lambda kind: struct((count, HW, C), kind)
     taps = pltpu.VMEM((9, C, C), BF16)
+    maps = pltpu.VMEM((4, C, C), BF16)
     slab = pltpu.VMEM((3, SLAB, C), BF16)
     slabs = pltpu.VMEM((count, 3, SLAB, C), BF16)
+    turned = pltpu.VMEM((count, C, HW), BF16)
+    low = pltpu.VMEM((HW, C), BF16)
+    lowt = pltpu.VMEM((C, HW), BF16)
+    full = pltpu.VMEM((HW, C), F32)
+    pair = pltpu.VMEM((128, HW), F32)
     h1, a1 = call(
-        fwd_one, count, [SMEM, ANY, IMAGE, VEC], [IMAGE, IMAGE], [big(F32), big(BF16)],
-        [taps, slab, pltpu.SemaphoreType.DMA((9,))],
-        (owner, slots, images, vectors), "first_conv",
-    )
+        fwd_one, count, [SMEM] + PARTS + [IMAGE, VEC], [IMAGE, IMAGE], [big(F32), big(BF16)],
+        [taps, slab, SEMS], (ids, *chunk_one, images, vectors), "first_conv",
+    )
+    planes_two, h1 = lax.optimization_barrier((planes_two, h1))
+    chunk_two = plan.gather_core(planes_two)
     emb = embeds.astype(F32)
     act = jax.nn.silu(emb).astype(BF16)
     act_rows = jnp.broadcast_to(act[:, None, :], (count, 16, EMB))
     a2, r1, nhat, stats = call(
-        fwd_two, count, [SMEM, ANY, IMAGE, IMAGE, per_image(16, EMB), VEC],
+        fwd_two, count, [SMEM] + PARTS + [IMAGE, IMAGE, per_image(16, EMB), VEC],
         [IMAGE, IMAGE, IMAGE, per_image(8, C)],
         [big(BF16), big(F32), big(F32), struct((count, 8, C), F32)],
-        [taps, pltpu.VMEM((4, C, C), BF16), slab, pltpu.SemaphoreType.DMA((13,))],
-        (owner, slots, h1, images, act_rows, vectors), "second_conv",
-    )
-    low = pltpu.VMEM((HW, C), BF16)
-    lowt = pltpu.VMEM((C, HW), BF16)
-    full = pltpu.VMEM((HW, C), F32)
-    pair = pltpu.VMEM((128, HW), F32)
+        [taps, maps, slab, SEMS, SEMS],
+        (ids, *chunk_two, h1, images, act_rows, vectors), "second_conv",
+    )
     out, dr1, grads_attn, sums_attn = call(
-        attention, count, [SMEM, ANY, SMEM, SMEM, IMAGE, IMAGE, VEC],
-        [IMAGE, IMAGE, whole(4, C, C), whole(8, C)],
-        [big(BF16), big(F32), struct((4, C, C), BF16), struct((8, C), F32)],
-        [pltpu.VMEM((4, C, C), BF16), full, low, lowt, low, low, low, low, lowt, lowt, low, low,
-         low, low, low, pair, pair, full, pltpu.VMEM((4, C, C), F32), pltpu.SemaphoreType.DMA((4,))],
-        (owner, slots, weight, live, r1, cotangent, vectors), "attention",
-    )
-    actt = jnp.pad(jnp.broadcast_to(act[:, :, None], (count, EMB, 3)), ((0, 0), (0, 0), (0, 5)))
+        attention, count, [SMEM, SMEM, SMEM, ANY] + [IMAGE, IMAGE, VEC],
+        [IMAGE, IMAGE, whole(16, 4, 2, PIECE, C), whole(8, C)],
+        [big(BF16), big(F32), struct((16, 4, 2, PIECE, C), BF16), struct((8, C), F32)],
+        [maps, full, low, lowt, low, low, low, low, lowt, lowt, low, low,
+         low, low, low, pair, pair, full, pltpu.VMEM((4, C, C), F32), SEMS],
+        (ids, weight, live, chunk_attn, r1, cotangent, vectors), "attention", 80 * 10**9,
+    )
+    (early,) = call(
+        two_taps, count, [IMAGE, IMAGE, whole(16, 4, 2, PIECE, C)],
+        [whole(16, 13, 2, PIECE, C)], [struct((16, 13, 2, PIECE, C), BF16)],
+        [slabs, turned], (dr1, a2, grads_attn), "second_conv_taps",
+    )
+    grads_early = plan.reduce_early(early)
+    dr1, _ = lax.optimization_barrier((dr1, early))
     emb_rows = jnp.broadcast_to(emb[:, None, :], (count, 8, EMB))
-    dh1, grads_two, grads_maps, demb, sums_two = call(
-        bwd_two, count,
-        [SMEM, ANY, IMAGE, IMAGE, IMAGE, per_image(8, C), VEC, per_image(8, EMB), whole(count, EMB, 8)],
-        [IMAGE, TAPS, whole(4, C, C), per_image(8, EMB), whole(8, C)],
-        [big(BF16), struct((9, C, C), BF16), struct((4, C, C), BF16), struct((count, 8, EMB), F32),
-         struct((8, C), F32)],
-        [taps, pltpu.VMEM((4, C, C), BF16), slabs, pltpu.VMEM((count, C, HW), BF16), full,
-         pltpu.VMEM((count, 2, 8, C), BF16), pltpu.SemaphoreType.DMA((13,))],
-        (owner, slots, dr1, a2, nhat, stats, vectors, emb_rows, actt), "second_conv_back",
-    )
-    (grads_one,) = call(
-        bwd_one_taps, count, [IMAGE, IMAGE], [TAPS], [struct((9, C, C), BF16)],
-        [slabs, pltpu.VMEM((count, C, HW), BF16)], (dh1, a1), "first_conv_taps",
-    )
+    dh1, dvec, demb, sums_two = call(
+        bwd_two_data, count,
+        [SMEM] + PARTS + [IMAGE, IMAGE, per_image(8, C), VEC, per_image(8, EMB)],
+        [IMAGE, per_image(8, C), per_image(8, EMB), whole(8, C)],
+        [big(BF16), struct((count, 8, C), F32), struct((count, 8, EMB), F32), struct((8, C), F32)],
+        [taps, maps, slab, full, SEMS, SEMS],
+        (ids, *chunk_two, dr1, nhat, stats, vectors, emb_rows), "second_conv_back",
+    )
+    late = call(
+        one_taps, count, [SMEM, IMAGE, IMAGE], [whole(4, 4, 9, PIECE, C)] * 2,
+        [struct((4, 4, 9, PIECE, C), BF16)] * 2,
+        [slabs, turned], (ids, dh1, a1), "first_conv_taps",
+    )
+    planes = plan.reduce_core(*late)
+    dh1, _ = lax.optimization_barrier((dh1, planes))
     dx, sums_one = call(
-        bwd_one_data, count, [SMEM, ANY, IMAGE, IMAGE, IMAGE, VEC], [IMAGE, whole(8, C)],
+        bwd_one_data, count, [SMEM] + PARTS + [IMAGE, IMAGE, IMAGE, VEC], [IMAGE, whole(8, C)],
         [big(F32), struct((8, C), F32)],
-        [taps, slab, full, pltpu.SemaphoreType.DMA((9,))],
-        (owner, slots, dh1, images, dr1, vectors), "first_conv_back",
-    )
-    grads = (grads_one, grads_two, grads_maps, grads_attn)
+        [taps, slab, full, SEMS],
+        (ids, *chunk_one, dh1, images, dr1, vectors), "first_conv_back",
+    )
+    grads_late = plan.reduce_late(planes, dx)
+    grads = plan.finish_early(grads_late, grads_early)
+    map_terms = jnp.concatenate([act.astype(F32), dvec[:, 0], dvec[:, 1]], axis=1).astype(BF16)
     grad_vectors = jnp.concatenate([sums_one[:2], sums_two[:6], sums_attn[:5]], axis=0)
-    return out, dx, demb[:, 0], grads, grad_vectors
+    return out, dx, demb[:, 0], grads, map_terms, grad_vectors
+
+
+AXES = ("rep", "shard")
+
+
+def swap(value, mask):
+    return lax.ppermute(value, AXES, [(i, i ^ mask) for i in range(PIECES)])
+
+
+def plane_mask(step):
+    return (step // 2) * 16 + (step % 2) * 2
+
+
+def gather_line(piece):
+    return jnp.stack([piece] + [swap(piece, 4 * k) for k in (1, 2, 3)])
+
+
+def gather_plane(line):
+    return [line] + [swap(line, plane_mask(k)) for k in (1, 2, 3)]
+
+
+def gather_core(plane):
+    return plane + [swap(part, 1) for part in plane]
+
+
+def add_up(*terms):
+    total = terms[0].astype(F32)
+    for term in terms[1:]:
+        total = total + term.astype(F32)
+    return total.astype(BF16)
+
+
+def block_slots(owner, mats_all):
+    block_ids = jnp.arange(mats_all, dtype=jnp.int32)
+    return jnp.sum(
+        jnp.where(owner[None, :] == block_ids[:, None], block_ids[None, :], 0), axis=1
+    )
+
+
+def pick_slots(grads, slots):
+    index = jnp.where(slots < 18, slots, jnp.clip(slots - 4, 0, 21))
+    held = (slots < 18) | ((slots >= 22) & (slots < BLOCKS))
+    picked = jnp.take(grads, index, axis=0)
+    return jnp.where(held.reshape((-1,) + (1,) * (grads.ndim - 1)), picked, jnp.zeros((), BF16))
+
+
+class Split:
+    def __init__(self):
+        self.rep = lax.axis_index("rep")
+        shard = lax.axis_index("shard")
+        self.ids = jnp.stack([shard % 2, self.rep * 2 + shard // 2 % 2, shard // 4])
+
+    def gather(self, master, vec_master, owner):
+        mat_dev = master.shape[0]
+        rows = master.astype(BF16).reshape(mat_dev, 2, 2, 2, 4, PIECE, C)
+        rows = lax.dynamic_index_in_dim(rows, self.rep, 2, keepdims=False)
+        rows = rows.transpose(3, 2, 1, 0, 4, 5).reshape(16, mat_dev, PIECE, C)
+        slots = lax.all_to_all(rows, "shard", 0, 0).reshape(16 * mat_dev, PIECE, C)
+        blocks = jnp.take(slots, owner[:BLOCKS], axis=0)
+        width = vec_master.shape[1]
+        vec = jnp.pad(vec_master.astype(BF16), ((0, 16 - VECS), (0, C - width)))
+        place = lax.axis_index("shard") * width
+        vec = jnp.where(self.rep == 0, jnp.roll(vec, place, axis=1), jnp.zeros((), BF16))
+        attn = lax.all_gather(blocks[22:26], AXES)
+        line_one = gather_line(jnp.concatenate([blocks[:9], vec[None]], axis=0))
+        second, line_one = lax.optimization_barrier((blocks[9:22], line_one))
+        plane_one = gather_plane(line_one)
+        line_two = gather_line(second)
+        line_two, plane_one = lax.optimization_barrier((line_two, plane_one))
+        one = gather_core(plane_one)
+        two = gather_plane(line_two)
+        vectors = sum(jnp.sum(part[:, 9].astype(F32), axis=0) for part in one)
+        return one, vectors, two, attn
+
+    def gather_core(self, planes):
+        return gather_core(planes)
+
+    def reduce_early(self, grads):
+        return lax.psum_scatter(grads, "shard", scatter_dimension=0, tiled=True)[0]
+
+    def finish_early(self, late, *early):
+        own = jnp.concatenate(early, axis=0)
+        mine = lax.dynamic_index_in_dim(own, self.rep, 1, keepdims=False)
+        other = lax.dynamic_index_in_dim(own, 1 - self.rep, 1, keepdims=False)
+        return jnp.concatenate([late, add_up(mine, swap(other, 16))], axis=0)
+
+    def reduce_core(self, keep, send):
+        other = swap(send, 1)
+        return [add_up(keep[k], other[k]) for k in range(4)]
+
+    def reduce_late(self, planes, after):
+        line = [swap(planes[k], plane_mask(k)) for k in (1, 2, 3)]
+        lines = [add_up(planes[0][j], *[part[j] for part in line]) for j in range(4)]
+        lines, _ = lax.optimization_barrier((lines, after))
+        return add_up(lines[0], *[swap(lines[k], 4 * k) for k in (1, 2, 3)])
+
+    def own(self, grads, slots, mat_dev, map_terms, grad_vectors):
+        picked = pick_slots(grads, slots).reshape(16, mat_dev * PIECE, C)
+        terms = jnp.broadcast_to(map_terms.reshape(1, -1, C), (16, map_terms.size // C, C))
+        width = C // 16
+        vec = grad_vectors.astype(BF16).reshape(VECS, 16, width).transpose(1, 0, 2)
+        vec = jnp.pad(vec.reshape(16, 1, VECS * width), ((0, 0), (0, 0), (0, C - VECS * width)))
+        sent = jnp.concatenate([picked, terms, vec], axis=1)
+        mine = lax.all_to_all(sent, "shard", 0, 0)
+        other = swap(mine, 16)
+        first = jnp.where(self.rep == 0, mine, other)
+        second = jnp.where(self.rep == 0, other, mine)
+        both = jnp.stack([first, second])
+        split = mat_dev * PIECE
+        rows = both[:, :, :split].reshape(2, 4, 2, 2, mat_dev, PIECE, C)
+        rows = rows.transpose(4, 3, 0, 2, 1, 5, 6).reshape(mat_dev, C, C)
+        terms = both[:, :, split:-1].reshape(-1, map_terms.shape[1])
+        vec = jnp.sum(both[:, :, -1, : VECS * width].astype(F32), axis=(0, 1))
+        return rows.astype(F32), terms, vec.reshape(VECS, width)
+
+
+class Plain:
+    def __init__(self):
+        self.ids = jnp.zeros((3,), jnp.int32)
+
+    def gather(self, master, vec_master, owner):
+        slots = lax.all_gather(master.astype(BF16), "shard", axis=0, tiled=True)
+        vec = lax.all_gather(vec_master.astype(BF16), "shard", axis=1, tiled=True)
+        blocks = jnp.take(slots, owner[:BLOCKS], axis=0)
+
+        def parts(some):
+            split = some.reshape(-1, 2, 4, 4, PIECE, C).transpose(1, 2, 3, 0, 4, 5)
+            return [split[core, plane] for core in range(2) for plane in range(4)]
+
+        vectors = jnp.pad(vec.astype(F32), ((0, 16 - VECS), (0, 0)))
+        flat = blocks[22:26].reshape(4, 2, 2, 2, 4, PIECE, C).transpose(2, 4, 3, 1, 0, 5, 6)
+        attn = flat.reshape(PIECES, 4, PIECE, C)
+        return parts(blocks[:9]), vectors, parts(blocks[9:22]), attn
+
+    def gather_core(self, planes):
+        return planes
+
+    def reduce_early(self, grads):
+        split = grads.reshape(4, 2, 2, -1, 2, PIECE, C).transpose(3, 2, 4, 1, 0, 5, 6)
+        return split.reshape(-1, C, C)
+
+    def finish_early(self, late, *early):
+        return jnp.concatenate([late, *early], axis=0)
+
+    def reduce_core(self, keep, send):
+        return [jnp.stack([keep, send]).transpose(3, 0, 1, 2, 4, 5).reshape(-1, C, C)]
+
+    def reduce_late(self, planes, after):
+        return planes[0]
+
+    def own(self, grads, slots, mat_dev, map_terms, grad_vectors):
+        picked = pick_slots(grads, slots)
+        mine = lax.psum_scatter(picked, "shard", scatter_dimension=0, tiled=True)
+        rows = lax.psum(mine, "rep").astype(F32)
+        terms = lax.all_gather(map_terms, AXES, axis=0, tiled=True)
+        vec = lax.psum_scatter(grad_vectors, "shard", scatter_dimension=1, tiled=True)
+        return rows, terms, lax.psum(vec, "rep")
 
 
 def shards(
@@ -731,37 +943,30 @@
 ):
     mat_dev = master.shape[0]
     mats_all = mat_dev * lax.axis_size("shard")
-    slot_weights, vec_full = (
-        lax.all_gather(master.astype(jnp.bfloat16), "shard", axis=0, tiled=True),
-        lax.all_gather(vec_master.astype(jnp.bfloat16), "shard", axis=1, tiled=True),
-    )
-    vectors = vec_full.astype(jnp.float32)
+    sizes = (lax.axis_size("rep"), lax.axis_size("shard"))
+    plan = Split() if sizes == (2, 16) else Plain()
+    gathered = plan.gather(master, vec_master, owner)
     slot_ids = jnp.arange(images.shape[0], dtype=jnp.int32)
     live = (slot_ids < counts[0, 0] + counts[0, 1]).astype(jnp.int32)
     weight = jnp.where(slot_ids < counts[0, 0], bucket_weight[0], bucket_weight[1])
     weight = jnp.where(live > 0, weight, 0.0)
-    outputs, grad_images, grad_embeds, grads, grad_vectors = layer(
-        images, embeds, cotangent, weight, live, owner, slot_weights, vectors
-    )
-    one, two, maps, attn = grads
-    grad_blocks = jnp.concatenate([one, two, maps, attn], axis=0)
-    block_ids = jnp.arange(mats_all, dtype=jnp.int32)
-    all_slots = jnp.sum(
-        jnp.where(owner[None, :] == block_ids[:, None], block_ids[None, :], 0), axis=1
-    )
-    slot_block = lax.dynamic_slice_in_dim(all_slots, lax.axis_index("shard") * mat_dev, mat_dev, 0)
-    picked = jnp.take(grad_blocks, jnp.minimum(all_slots, BLOCKS - 1), axis=0)
-    grad_slot = jnp.where((all_slots < BLOCKS)[:, None, None], picked, jnp.zeros((), BF16))
-    own_grads, own_vec = (
-        lax.psum_scatter(grad_slot, "shard", scatter_dimension=0, tiled=True),
-        lax.psum_scatter(
-            grad_vectors.astype(jnp.bfloat16), "shard", scatter_dimension=1, tiled=True
-        ),
-    )
-    own_grads, own_vec = (
-        lax.psum(own_grads, "rep").astype(jnp.float32),
-        lax.psum(own_vec, "rep").astype(jnp.float32),
-    )
+    outputs, grad_images, grad_embeds, grads, map_terms, grad_vectors = layer(
+        images, embeds, cotangent, weight, live, plan, gathered
+    )
+    all_slots = block_slots(owner, mats_all)
+    shard = lax.axis_index("shard")
+    slot_block = lax.dynamic_slice_in_dim(all_slots, shard * mat_dev, mat_dev, 0)
+    own_grads, all_terms, own_vec = plan.own(
+        grads, all_slots, mat_dev, map_terms, grad_vectors
+    )
+    maps = slot_block - 18
+    lower = (maps % 2 == 0)[:, None, None]
+    acts = jnp.where(lower, all_terms[None, :, :C], all_terms[None, :, C:EMB])
+    is_scale = (maps < 2)[:, None, None]
+    sides = jnp.where(is_scale, all_terms[None, :, EMB : EMB + C], all_terms[None, :, EMB + C :])
+    map_grads = jnp.einsum("sic,sio->sco", acts, sides, preferred_element_type=F32)
+    is_map = ((maps >= 0) & (maps < 4))[:, None, None]
+    own_grads = jnp.where(is_map, map_grads, own_grads)
     rotated = jnp.matmul(
         jnp.matmul(jnp.swapaxes(left_basis, 1, 2), own_grads, precision=PRECISE),
         right_basis,

time: 681 us -> 480 us (0.70)
  waiting for transfers between devices: 341 us -> 105 us
  starting transfers between devices: 0.16 us -> 40.2 us
  other arithmetic: 31.5 us -> 23.1 us
  Pallas kernels: 224 us -> 231 us
    reduce_scatter x1, waiting for transfers between devices: 150 us -> 16.8 us  [reduce_early(): return lax.psum_scatter(grads, 'shard', scatter_dimension=0, tiled=True)[0]]
    all_gather x1, waiting for transfers between devices: 98.9 us -> 0.02 us  [gather(): attn = lax.all_gather(blocks[22:26], AXES)]
    ppermute x0 -> x29, waiting for transfers between devices: none -> 74.4 us  [swap(): return lax.ppermute(value, AXES, [(i, i ^ mask) for i in range(PIECES)])]
    unnamed x5 -> x2, waiting for transfers between devices: 56.6 us -> 0.03 us
    psum x1 -> x0, waiting for transfers between devices: 34.9 us -> none  [shards(): lax.psum(own_grads, 'rep').astype(jnp.float32)]
    ppermute x0 -> x29, starting transfers between devices: none -> 32.7 us  [swap(): return lax.ppermute(value, AXES, [(i, i ^ mask) for i in range(PIECES)])]
    all_to_all x0 -> x1, blocking collectives: none -> 24.5 us  [own(): mine = lax.all_to_all(sent, 'shard', 0, 0)]
    all_gather x1 -> x0, blocking collectives: 23.8 us -> none  [shards(): lax.all_gather(vec_master.astype(jnp.bfloat16), 'shard', axis=1, tiled=True)]
  transfers between devices with their start and end apart: 4 -> 32, of which waited for: 4 -> 13; matrix products, arithmetic and copies ran while one was open for 2% -> 5% of each run, Pallas kernels for 4% -> 23%
where the time goes in v2:
time: 480 us; the launch traced here: 474 us
  Pallas kernels  231 us (48%)
  waiting for transfers between devices  105 us (22%)
  starting transfers between devices  40.2 us (8%)
  blocking collectives  24.5 us (5%)
  other arithmetic  23.1 us (5%)
  matrix products  18.2 us (4%)
  between operations  16.4 us (3%)
  local copies, waits for them, and re-layouts  14.6 us (3%)
    pallas_call x7, Pallas kernels, call(): pl.pallas_call(body, grid=(images,), in_specs=in_specs, out_specs=out_spe...  231 us
    ppermute x29, waiting for transfers between devices, swap(): return lax.ppermute(value, AXES, [(i, i ^ mask) for i in range(PIECES)])  74.4 us
    ppermute x29, starting transfers between devices, swap(): return lax.ppermute(value, AXES, [(i, i ^ mask) for i in range(PIECES)])  32.7 us
    all_to_all x1, blocking collectives, own(): mine = lax.all_to_all(sent, 'shard', 0, 0)  24.5 us
    reduce_scatter x1, waiting for transfers between devices, reduce_early(): return lax.psum_scatter(grads, 'shard', scatter_dimension=0, tiled=True)[0]  16.8 us
    all_to_all x1, waiting for transfers between devices, gather(): slots = lax.all_to_all(rows, 'shard', 0, 0).reshape(16 * mat_dev, PIECE, C)  14.2 us
  transfers between devices with their start and end apart: 32, of which 13 were waited for; matrix products, arithmetic and copies ran while one was open for 5% of the time, Pallas kernels for 23%

profile of v2, /device:TPU:0, one launch (start us, length us, event | category | flops | bytes accessed | tf_op | source)
XLA Modules:
  0.0 473.6 jit_solution(6235796518215520142)
XLA Ops:
  7.2 1.9 convert_element_type.246
  10.0 7.4 %all-to-all-start = ((bf16[16,2,16,512]{3,2,1,0:T(8,128)(2,1)}), bf16[16,2,16,512]{3,2,1,0:T(8,128)(2,1)S(1)}, u32[]{:S(2)}, u32[]{:S(2)}) async-start(bf16[16,2,16,512]{3,2,1,0:T(8,128)(2,1)} %bitcast.10), calls=%async_computation | async-start | bytes 1048576 | tf_op jit(solution)/shard_map/all_to_all | solution.py:826
  17.6 14.2 %all-to-all-done = bf16[16,2,16,512]{3,2,1,0:T(8,128)(2,1)S(1)} async-done(((bf16[16,2,16,512]{3,2,1,0:T(8,128)(2,1)}), bf16[16,2,16,512]{3,2,1,0:T(8,128)(2,1)S(1)}, u32[]{:S(2)}, u32[]{:S(2)}) %all-to-all-start) | async-done | bytes 524320 | tf_op jit(solution)/shard_map/all_to_all | solution.py:826
  32.6 1.2 collective-permute-start
  33.8 1.2 collective-permute-start.1
  35.0 2.1 collective-permute-start.2
  37.1 3.5 collective-permute-done
  40.6 8.1 %collective-permute-done.1 = bf16[10,16,512]{2,1,0:T(8,128)(2,1)S(1)} collective-permute-done((bf16[10,16,512]{2,1,0:T(8,128)(2,1)S(1)}, bf16[10,16,512]{2,1,0:T(8,128)(2,1)S(1)}, u32[]{:S(2)}, u32[]{:S(2)}) %collective-permute-start.1) | collective-permute-done | bytes 163872 | tf_op jit(solution)/shard_map/ppermute | solution.py:775
  48.8 1.4 collective-permute-start.6
  50.2 1.5 collective-permute-start.7
  52.4 3.5 collective-permute-start.3
  55.9 5.7 %collective-permute-done.3 = bf16[13,16,512]{2,1,0:T(8,128)(2,1)S(1)} collective-permute-done((bf16[13,16,512]{2,1,0:T(8,128)(2,1)S(1)}, bf16[13,16,512]{2,1,0:T(8,128)(2,1)S(1)}, u32[]{:S(2)}, u32[]{:S(2)}) %collective-permute-start.3) | collective-permute-done | bytes 213024 | tf_op jit(solution)/shard_map/ppermute | solution.py:775
  61.6 2.0 collective-permute-start.5
  63.6 8.8 %collective-permute-done.4 = bf16[13,16,512]{2,1,0:T(8,128)(2,1)S(1)} collective-permute-done((bf16[13,16,512]{2,1,0:T(8,128)(2,1)S(1)}, bf16[13,16,512]{2,1,0:T(8,128)(2,1)S(1)}, u32[]{:S(2)}, u32[]{:S(2)}) %collective-permute-start.4) | collective-permute-done | bytes 213024 | tf_op jit(solution)/shard_map/ppermute | solution.py:775
  72.5 7.3 %collective-permute-done.8.refs_3_ = bf16[4,10,16,512]{3,2,1,0:T(8,128)(2,1)} collective-permute-done((bf16[4,10,16,512]{3,2,1,0:T(8,128)(2,1)S(1)}, bf16[4,10,16,512]{3,2,1,0:T(8,128)(2,1)}, u32[]{:S(2)}, u32[]{:S(2)}) %collective-permute-start.8) | collective-permute-done | bytes 655392 | tf_op jit(solution)/shard_map/ppermute | solution.py:775
  82.2 1.6 collective-permute-start.10
  87.0 1.5 collective-permute-start.9
  91.8 18.6 %first_conv.1 = (f32[2,1024,512]{2,1,0:T(8,128)}, bf16[2,1024,512]{2,1,0:T(8,128)(2,1)}) custom-call(s32[3]{0:T(128)} %pad_add_fusion.ids, bf16[4,10,16,512]{3,2,1,0:T(8,128)(2,1)} %copy-done.8, bf16[4,10,16,512]{3,2,1,0:T(8,128)(2,1)} %collective-permute-done.6.refs_1_, bf16[4,10,16,512]{3,2,1,0:T(8,128)(2,1)} %collective-permute-done.7.refs_2_, ...), custom_call_target="tpu_custom_call" | custom-call | flops 20000000000 | bytes 31457280 | tf_op jit(solution)/shard_map/first_conv/pallas_call | solution.py:676
  110.4 13.5 %collective-permute-done.11.refs_3_ = bf16[4,13,16,512]{3,2,1,0:T(8,128)(2,1)} collective-permute-done((bf16[4,13,16,512]{3,2,1,0:T(8,128)(2,1)S(1)}, bf16[4,13,16,512]{3,2,1,0:T(8,128)(2,1)}, u32[]{:S(2)}, u32[]{:S(2)}) %collective-permute-start.11) | collective-permute-done | bytes 852000 | tf_op jit(solution)/shard_map/ppermute | solution.py:775
  123.9 3.3 collective-permute-done.9.refs_1_
  131.2 2.5 compare_select_fusion.12.weight
  134.9 23.4 %second_conv.1 = (bf16[2,1024,512]{2,1,0:T(8,128)(2,1)}, f32[2,1024,512]{2,1,0:T(8,128)}, f32[2,1024,512]{2,1,0:T(8,128)}, f32[2,8,512]{2,1,0:T(8,128)}) custom-call(s32[3]{0:T(128)} %pad_add_fusion.ids, bf16[4,13,16,512]{3,2,1,0:T(8,128)(2,1)} %copy-done.7, bf16[4,13,16,512]{3,2,1,0:T(8,128)(2,1)} %collective-permute-done.9.refs_1_, ...), custom_call_target="tpu_custom_call" | custom-call | flops 20000000000 | bytes 31457280 | tf_op jit(solution)/shard_map/second_conv/pallas_call | solution.py:676
  158.3 104.4 %attention.1 = (bf16[2,1024,512]{2,1,0:T(8,128)(2,1)}, f32[2,1024,512]{2,1,0:T(8,128)}, bf16[16,4,2,16,512]{4,3,2,1,0:T(8,128)(2,1)}, f32[8,512]{1,0:T(8,128)}) custom-call(s32[3]{0:T(128)} %pad_add_fusion.ids, f32[2]{0:T(128)} %compare_select_fusion.12.weight, s32[2]{0:T(128)} %compare_convert_fusion.live, bf16[32,4,16,512]{3,2,1,0:T(8,128)(2,1)} %bitcast.129, ...), custom_call_target="tpu_custom_call" | custom-call | flops 80000000000 | bytes 31457280 | tf_op jit(solution)/shard_map/attention/pallas_call | solution.py:676
  262.7 18.5 %second_conv_taps.1 = bf16[16,13,2,16,512]{4,3,2,1,0:T(8,128)(2,1)} custom-call(f32[2,1024,512]{2,1,0:T(8,128)} %get-tuple-element.65.grad.refs_8_.refs_10_, bf16[2,1024,512]{2,1,0:T(8,128)(2,1)} %get-tuple-element.63.act, bf16[16,4,2,16,512]{4,3,2,1,0:T(8,128)(2,1)} %get-tuple-element.64.others), custom_call_target="tpu_custom_call" | custom-call | flops 20000000000 | bytes 31457280 | tf_op jit(solution)/shard_map/second_conv_taps/pallas_call | solution.py:676
  281.9 25.2 %second_conv_back.1 = (bf16[2,1024,512]{2,1,0:T(8,128)(2,1)}, f32[2,8,512]{2,1,0:T(8,128)}, f32[2,8,1024]{2,1,0:T(8,128)}, f32[8,512]{1,0:T(8,128)}) custom-call(s32[3]{0:T(128)} %pad_add_fusion.ids, bf16[4,13,16,512]{3,2,1,0:T(8,128)(2,1)} %copy-done.7, bf16[4,13,16,512]{3,2,1,0:T(8,128)(2,1)} %collective-permute-done.9.refs_1_, ...), custom_call_target="tpu_custom_call" | custom-call | flops 20000000000 | bytes 31457280 | tf_op jit(solution)/shard_map/second_conv_back/pallas_call | solution.py:676
  307.2 17.1 %first_conv_taps.1 = (bf16[4,4,9,16,512]{4,3,2,1,0:T(8,128)(2,1)}, bf16[4,4,9,16,512]{4,3,2,1,0:T(8,128)(2,1)}) custom-call(s32[3]{0:T(128)} %pad_add_fusion.ids, bf16[2,1024,512]{2,1,0:T(8,128)(2,1)} %get-tuple-element.72.grad.refs_8_, bf16[2,1024,512]{2,1,0:T(8,128)(2,1)} %get-tuple-element.69.act), custom_call_target="tpu_custom_call" | custom-call | flops 20000000000 | bytes 31457280 | tf_op jit(solution)/shard_map/first_conv_taps/pallas_call | solution.py:676
  325.3 3.9 collective-permute-done.20
  329.1 4.5 add_convert_fusion
  333.6 1.5 collective-permute-start.21
  335.1 1.5 collective-permute-start.22
  337.1 23.9 %first_conv_back.1 = (f32[2,1024,512]{2,1,0:T(8,128)}, f32[8,512]{1,0:T(8,128)}) custom-call(s32[3]{0:T(128)} %pad_add_fusion.ids, bf16[4,10,16,512]{3,2,1,0:T(8,128)(2,1)} %copy-done.8, bf16[4,10,16,512]{3,2,1,0:T(8,128)(2,1)} %collective-permute-done.6.refs_1_, bf16[4,10,16,512]{3,2,1,0:T(8,128)(2,1)} %collective-permute-done.7.refs_2_, ...), custom_call_target="tpu_custom_call" | custom-call | flops 20000000000 | bytes 31457280 | tf_op jit(solution)/shard_map/first_conv_back/pallas_call | solution.py:676
  361.9 1.4 collective-permute-done.23
  363.3 1.9 fusion.32
  365.2 4.6 collective-permute-start.24
  369.8 2.4 collective-permute-start.26
  372.4 16.8 %reduce-scatter.2.cloned.1.call-done = bf16[1,13,2,16,512]{4,3,2,1,0:T(8,128)(2,1)} async-done(((bf16[16,13,2,16,512]{4,3,2,1,0:T(8,128)(2,1)}), bf16[1,13,2,16,512]{4,3,2,1,0:T(8,128)(2,1)}) %reduce-scatter.2.cloned.1.call-update) | async-done | bytes 426000 | tf_op jit(solution)/shard_map/reduce_scatter | solution.py:847
  390.2 1.5 collective-permute-start.27
  391.8 5.6 %collective-permute-done.27 = bf16[13,16,512]{2,1,0:T(8,128)(2,1)S(1)} collective-permute-done((bf16[13,16,512]{2,1,0:T(8,128)(2,1)S(1)}, bf16[13,16,512]{2,1,0:T(8,128)(2,1)S(1)}, u32[]{:S(2)}, u32[]{:S(2)}) %collective-permute-start.27) | collective-permute-done | bytes 213024 | tf_op jit(solution)/shard_map/ppermute | solution.py:775
  397.4 1.0 fusion.16
  399.3 24.5 %all_to_all.10 = bf16[16,41,512]{2,1,0:T(8,128)(2,1)S(1)} all-to-all(bf16[16,41,512]{2,1,0:T(8,128)(2,1)S(1)} %fusion.11), channel_id=1, replica_groups=mesh['rep'=2,'shard'=16] {'shard'}, dimensions={0} | all-to-all | bytes 1343488 | tf_op jit(solution)/shard_map/all_to_all | solution.py:872
  423.9 1.2 copy.74
  425.1 1.5 collective-permute-start.28
  426.5 1.2 compare_select_fusion.13
  429.8 13.3 %collective-permute-done.28 = bf16[16,41,512]{2,0,1:T(8,128)(2,1)S(1)} collective-permute-done((bf16[16,41,512]{2,0,1:T(8,128)(2,1)}, bf16[16,41,512]{2,0,1:T(8,128)(2,1)S(1)}, u32[]{:S(2)}, u32[]{:S(2)}) %collective-permute-start.28) | collective-permute-done | bytes 671776 | tf_op jit(solution)/shard_map/ppermute | solution.py:775
  448.1 3.6 fusion.63
  451.7 3.7 fusion
  455.5 5.0 %fusion.1 = f32[2,512,512]{1,2,0:T(8,128)S(1)} fusion(f32[2,512,512]{2,1,0:T(8,128)S(1)} %copy-done.2, f32[2,512,512]{2,1,0:T(8,128)S(1)} %get-tuple-element.99, f32[2,512,512]{2,1,0:T(8,128)S(1)} %get-tuple-element.100), kind=kOutput, calls=%fused_computation.8 | convolution fusion | flops 3223322624 | bytes 8388608 | tf_op jit(solution)/shard_map/dot_general | solution.py:980
  460.6 5.3 %fusion.62 = (bf16[2,512,512]{2,1,0:T(8,128)(2,1)}, f32[2,512,512]{2,1,0:T(8,128)}) fusion(f32[2,512,512]{2,1,0:T(8,128)S(1)} %copy-done.1, f32[2,512,512]{1,2,0:T(8,128)S(1)} %fusion.1, f32[2,512,512]{2,1,0:T(8,128)S(1)} %copy-done, f32[2]{0:T(128)S(1)} %copy-done.19), kind=kOutput, calls=%fused_computation.149 | convolution fusion | flops 3223846912 | bytes 9437192 | tf_op jit(solution)/shard_map/dot_general | solution.py:979
  (171 shorter events, 28.1 us)
Async XLA Ops:
  7.2 444.5 %copy-start = (f32[2,512,512]{2,1,0:T(8,128)S(1)}, f32[2,512,512]{2,1,0:T(8,128)}, u32[]{:S(2)}) copy-start(f32[2,512,512]{2,1,0:T(8,128)} %param.24) | copy-start | bytes 6291460
  9.1 8.4 %copy-start.11 = (f32[13,32]{1,0:T(8,128)S(1)}, f32[13,32]{1,0:T(8,128)}, u32[]{:S(2)}) copy-start(f32[13,32]{1,0:T(8,128)} %param.25) | copy-start | bytes 4996
  9.1 8.4 %copy-start.26 = (s32[32]{0:T(128)S(1)}, s32[32]{0:T(128)}, u32[]{:S(2)}) copy-start(s32[32]{0:T(128)} %param.19) | copy-start | bytes 388
  10.0 21.9 %all-to-all-start = ((bf16[16,2,16,512]{3,2,1,0:T(8,128)(2,1)}), bf16[16,2,16,512]{3,2,1,0:T(8,128)(2,1)S(1)}, u32[]{:S(2)}, u32[]{:S(2)}) async-start(bf16[16,2,16,512]{3,2,1,0:T(8,128)(2,1)} %bitcast.10), calls=%async_computation | async-start | bytes 1048576 | tf_op jit(solution)/shard_map/all_to_all | solution.py:826
  17.4 140.9 %all-gather.3.cloned.1.call-start = ((), (), s32[]{:S(2)}) async-start(), calls=%async_computation.4 | async-start | bytes 2162688 | tf_op jit(solution)/shard_map/all_gather | solution.py:832
  32.6 8.0 %collective-permute-start = (bf16[10,16,512]{2,1,0:T(8,128)(2,1)S(1)}, bf16[10,16,512]{2,1,0:T(8,128)(2,1)S(1)}, u32[]{:S(2)}, u32[]{:S(2)}) collective-permute-start(bf16[10,16,512]{2,1,0:T(8,128)(2,1)S(1)} %get-tuple-element.108), channel_id=1, source_target_pairs={{0,4},{1,5},{2,6},{3,7},{4,0},{5,1},{6,2},{7,3},{8,12},{9,13},{10,... | collective-permute-start | bytes 491528 | tf_op jit(solution)/shard_map/ppermute | solution.py:775
  33.8 15.0 %collective-permute-start.1 = (bf16[10,16,512]{2,1,0:T(8,128)(2,1)S(1)}, bf16[10,16,512]{2,1,0:T(8,128)(2,1)S(1)}, u32[]{:S(2)}, u32[]{:S(2)}) collective-permute-start(bf16[10,16,512]{2,1,0:T(8,128)(2,1)S(1)} %get-tuple-element.108), channel_id=1, source_target_pairs={{0,8},{1,9},{2,10},{3,11},{4,12},{5,13},{6,14},{7,15},{8,0},{9,1},... | collective-permute-start | bytes 491528 | tf_op jit(solution)/shard_map/ppermute | solution.py:775
  35.0 13.7 %collective-permute-start.2 = (bf16[10,16,512]{2,1,0:T(8,128)(2,1)S(1)}, bf16[10,16,512]{2,1,0:T(8,128)(2,1)S(1)}, u32[]{:S(2)}, u32[]{:S(2)}) collective-permute-start(bf16[10,16,512]{2,1,0:T(8,128)(2,1)S(1)} %get-tuple-element.108), channel_id=1, source_target_pairs={{0,12},{1,13},{2,14},{3,15},{4,8},{5,9},{6,10},{7,11},{8,4},{9,5},... | collective-permute-start | bytes 491528 | tf_op jit(solution)/shard_map/ppermute | solution.py:775
  48.8 23.7 %copy-start.8 = (bf16[4,10,16,512]{3,2,1,0:T(8,128)(2,1)}, bf16[4,10,16,512]{3,2,1,0:T(8,128)(2,1)S(1)}, u32[]{:S(2)}) copy-start(bf16[4,10,16,512]{3,2,1,0:T(8,128)(2,1)S(1)} %pad_maximum_fusion.1.refs_0_) | copy-start | bytes 1966084
  48.8 23.7 %collective-permute-start.6 = (bf16[4,10,16,512]{3,2,1,0:T(8,128)(2,1)S(1)}, bf16[4,10,16,512]{3,2,1,0:T(8,128)(2,1)}, u32[]{:S(2)}, u32[]{:S(2)}) collective-permute-start(bf16[4,10,16,512]{3,2,1,0:T(8,128)(2,1)S(1)} %pad_maximum_fusion.1.refs_0_), channel_id=1, source_target_pairs={{0,2},{1,3},{2,0},{3,1},{4,6},{5,7},{6,4},{7,5},{8,10},{9,11},{10,... | collective-permute-start | bytes 1966088 | tf_op jit(solution)/shard_map/ppermute | solution.py:775
  50.2 22.3 %collective-permute-start.7 = (bf16[4,10,16,512]{3,2,1,0:T(8,128)(2,1)S(1)}, bf16[4,10,16,512]{3,2,1,0:T(8,128)(2,1)}, u32[]{:S(2)}, u32[]{:S(2)}) collective-permute-start(bf16[4,10,16,512]{3,2,1,0:T(8,128)(2,1)S(1)} %pad_maximum_fusion.1.refs_0_), channel_id=1, source_target_pairs={{0,16},{1,17},{2,18},{3,19},{4,20},{5,21},{6,22},{7,23},{8,24},{9,... | collective-permute-start | bytes 1966088 | tf_op jit(solution)/shard_map/ppermute | solution.py:775
  51.7 28.1 %collective-permute-start.8 = (bf16[4,10,16,512]{3,2,1,0:T(8,128)(2,1)S(1)}, bf16[4,10,16,512]{3,2,1,0:T(8,128)(2,1)}, u32[]{:S(2)}, u32[]{:S(2)}) collective-permute-start(bf16[4,10,16,512]{3,2,1,0:T(8,128)(2,1)S(1)} %pad_maximum_fusion.1.refs_0_), channel_id=1, source_target_pairs={{0,18},{1,19},{2,16},{3,17},{4,22},{5,23},{6,20},{7,21},{8,26},{9,... | collective-permute-start | bytes 1966088 | tf_op jit(solution)/shard_map/ppermute | solution.py:775
  52.4 9.2 %collective-permute-start.3 = (bf16[13,16,512]{2,1,0:T(8,128)(2,1)S(1)}, bf16[13,16,512]{2,1,0:T(8,128)(2,1)S(1)}, u32[]{:S(2)}, u32[]{:S(2)}) collective-permute-start(bf16[13,16,512]{2,1,0:T(8,128)(2,1)S(1)} %slice.227), channel_id=1, source_target_pairs={{0,4},{1,5},{2,6},{3,7},{4,0},{5,1},{6,2},{7,3},{8,12},{9,13},{10,... | collective-permute-start | bytes 638984 | tf_op jit(solution)/shard_map/ppermute | solution.py:775
  55.9 16.5 %collective-permute-start.4 = (bf16[13,16,512]{2,1,0:T(8,128)(2,1)S(1)}, bf16[13,16,512]{2,1,0:T(8,128)(2,1)S(1)}, u32[]{:S(2)}, u32[]{:S(2)}) collective-permute-start(bf16[13,16,512]{2,1,0:T(8,128)(2,1)S(1)} %slice.227), channel_id=1, source_target_pairs={{0,8},{1,9},{2,10},{3,11},{4,12},{5,13},{6,14},{7,15},{8,0},{9,1},... | collective-permute-start | bytes 638984 | tf_op jit(solution)/shard_map/ppermute | solution.py:775
  61.6 10.8 %collective-permute-start.5 = (bf16[13,16,512]{2,1,0:T(8,128)(2,1)S(1)}, bf16[13,16,512]{2,1,0:T(8,128)(2,1)S(1)}, u32[]{:S(2)}, u32[]{:S(2)}) collective-permute-start(bf16[13,16,512]{2,1,0:T(8,128)(2,1)S(1)} %slice.227), channel_id=1, source_target_pairs={{0,12},{1,13},{2,14},{3,15},{4,8},{5,9},{6,10},{7,11},{8,4},{9,5},... | collective-permute-start | bytes 638984 | tf_op jit(solution)/shard_map/ppermute | solution.py:775
  72.5 54.7 %copy-start.7 = (bf16[4,13,16,512]{3,2,1,0:T(8,128)(2,1)}, bf16[4,13,16,512]{3,2,1,0:T(8,128)(2,1)S(1)}, u32[]{:S(2)}) copy-start(bf16[4,13,16,512]{3,2,1,0:T(8,128)(2,1)S(1)} %pad_maximum_fusion.refs_0_) | copy-start | bytes 2555908
  79.8 5.7 %collective-permute-start.15 = (bf16[4,10,16,512]{3,2,1,0:T(8,128)(2,1)}, bf16[4,10,16,512]{3,2,1,0:T(8,128)(2,1)}, u32[]{:S(2)}, u32[]{:S(2)}) collective-permute-start(bf16[4,10,16,512]{3,2,1,0:T(8,128)(2,1)} %collective-permute-done.8.refs_3_), channel_id=1, source_target_pairs={{0,1},{1,0},{2,3},{3,2},{4,5},{5,4},{6,7},{7,6},{8,9},{9,8},{10,11... | collective-permute-start | bytes 1966088 | tf_op jit(solution)/shard_map/ppermute | solution.py:775
  79.8 7.2 %collective-permute-start.14 = (bf16[4,10,16,512]{3,2,1,0:T(8,128)(2,1)}, bf16[4,10,16,512]{3,2,1,0:T(8,128)(2,1)}, u32[]{:S(2)}, u32[]{:S(2)}) collective-permute-start(bf16[4,10,16,512]{3,2,1,0:T(8,128)(2,1)} %collective-permute-done.7.refs_2_), channel_id=1, source_target_pairs={{0,1},{1,0},{2,3},{3,2},{4,5},{5,4},{6,7},{7,6},{8,9},{9,8},{10,11... | collective-permute-start | bytes 1966088 | tf_op jit(solution)/shard_map/ppermute | solution.py:775
  80.3 9.0 %collective-permute-start.13 = (bf16[4,10,16,512]{3,2,1,0:T(8,128)(2,1)}, bf16[4,10,16,512]{3,2,1,0:T(8,128)(2,1)}, u32[]{:S(2)}, u32[]{:S(2)}) collective-permute-start(bf16[4,10,16,512]{3,2,1,0:T(8,128)(2,1)} %collective-permute-done.6.refs_1_), channel_id=1, source_target_pairs={{0,1},{1,0},{2,3},{3,2},{4,5},{5,4},{6,7},{7,6},{8,9},{9,8},{10,11... | collective-permute-start | bytes 1966088 | tf_op jit(solution)/shard_map/ppermute | solution.py:775
  80.4 9.9 %collective-permute-start.12 = (bf16[4,10,16,512]{3,2,1,0:T(8,128)(2,1)}, bf16[4,10,16,512]{3,2,1,0:T(8,128)(2,1)}, u32[]{:S(2)}, u32[]{:S(2)}) collective-permute-start(bf16[4,10,16,512]{3,2,1,0:T(8,128)(2,1)} %copy-done.8), channel_id=1, source_target_pairs={{0,1},{1,0},{2,3},{3,2},{4,5},{5,4},{6,7},{7,6},{8,9},{9,8},{10,11... | collective-permute-start | bytes 1966088 | tf_op jit(solution)/shard_map/ppermute | solution.py:775
  82.1 307.1 %reduce-scatter.2.cloned.1.call-start = ((), (), s32[]{:S(2)}) async-start(), calls=%async_computation.3 | async-start | bytes 7241728 | tf_op jit(solution)/shard_map/reduce_scatter | solution.py:847
  82.2 28.2 %collective-permute-start.10 = (bf16[4,13,16,512]{3,2,1,0:T(8,128)(2,1)S(1)}, bf16[4,13,16,512]{3,2,1,0:T(8,128)(2,1)}, u32[]{:S(2)}, u32[]{:S(2)}) collective-permute-start(bf16[4,13,16,512]{3,2,1,0:T(8,128)(2,1)S(1)} %pad_maximum_fusion.refs_0_), channel_id=1, source_target_pairs={{0,16},{1,17},{2,18},{3,19},{4,20},{5,21},{6,22},{7,23},{8,24},{9,... | collective-permute-start | bytes 2555912 | tf_op jit(solution)/shard_map/ppermute | solution.py:775
  85.5 38.4 %collective-permute-start.11 = (bf16[4,13,16,512]{3,2,1,0:T(8,128)(2,1)S(1)}, bf16[4,13,16,512]{3,2,1,0:T(8,128)(2,1)}, u32[]{:S(2)}, u32[]{:S(2)}) collective-permute-start(bf16[4,13,16,512]{3,2,1,0:T(8,128)(2,1)S(1)} %pad_maximum_fusion.refs_0_), channel_id=1, source_target_pairs={{0,18},{1,19},{2,16},{3,17},{4,22},{5,23},{6,20},{7,21},{8,26},{9,... | collective-permute-start | bytes 2555912 | tf_op jit(solution)/shard_map/ppermute | solution.py:775
  87.0 40.1 %collective-permute-start.9 = (bf16[4,13,16,512]{3,2,1,0:T(8,128)(2,1)S(1)}, bf16[4,13,16,512]{3,2,1,0:T(8,128)(2,1)}, u32[]{:S(2)}, u32[]{:S(2)}) collective-permute-start(bf16[4,13,16,512]{3,2,1,0:T(8,128)(2,1)S(1)} %pad_maximum_fusion.refs_0_), channel_id=1, source_target_pairs={{0,2},{1,3},{2,0},{3,1},{4,6},{5,7},{6,4},{7,5},{8,10},{9,11},{10,... | collective-permute-start | bytes 2555912 | tf_op jit(solution)/shard_map/ppermute | solution.py:775
  91.8 36.4 %copy-start.20 = (s32[1,2]{1,0:T(1,128)S(1)}, s32[1,2]{1,0:T(1,128)}, u32[]{:S(2)}) copy-start(s32[1,2]{1,0:T(1,128)} %param.17) | copy-start | bytes 28
  91.8 38.9 %copy-start.21 = (f32[2]{0:T(128)S(1)}, f32[2]{0:T(128)}, u32[]{:S(2)}) copy-start(f32[2]{0:T(128)} %param.18) | copy-start | bytes 28
  91.8 41.9 %copy-start.14 = (bf16[2,1024]{1,0:T(2,128)(2,1)S(1)}, bf16[2,1024]{1,0:T(2,128)(2,1)}, u32[]{:S(2)}) copy-start(bf16[2,1024]{1,0:T(2,128)(2,1)} %param.15) | copy-start | bytes 12292
  127.2 6.5 %collective-permute-start.16 = (bf16[4,13,16,512]{3,2,1,0:T(8,128)(2,1)S(1)}, bf16[4,13,16,512]{3,2,1,0:T(8,128)(2,1)}, u32[]{:S(2)}, u32[]{:S(2)}) collective-permute-start(bf16[4,13,16,512]{3,2,1,0:T(8,128)(2,1)S(1)} %pad_maximum_fusion.refs_0_), channel_id=1, source_target_pairs={{0,1},{1,0},{2,3},{3,2},{4,5},{5,4},{6,7},{7,6},{8,9},{9,8},{10,11... | collective-permute-start | bytes 2555912 | tf_op jit(solution)/shard_map/ppermute | solution.py:775
  127.2 6.5 %collective-permute-start.17 = (bf16[4,13,16,512]{3,2,1,0:T(8,128)(2,1)}, bf16[4,13,16,512]{3,2,1,0:T(8,128)(2,1)}, u32[]{:S(2)}, u32[]{:S(2)}) collective-permute-start(bf16[4,13,16,512]{3,2,1,0:T(8,128)(2,1)} %collective-permute-done.9.refs_1_), channel_id=1, source_target_pairs={{0,1},{1,0},{2,3},{3,2},{4,5},{5,4},{6,7},{7,6},{8,9},{9,8},{10,11... | collective-permute-start | bytes 2555912 | tf_op jit(solution)/shard_map/ppermute | solution.py:775
  127.7 6.0 %collective-permute-start.18 = (bf16[4,13,16,512]{3,2,1,0:T(8,128)(2,1)}, bf16[4,13,16,512]{3,2,1,0:T(8,128)(2,1)}, u32[]{:S(2)}, u32[]{:S(2)}) collective-permute-start(bf16[4,13,16,512]{3,2,1,0:T(8,128)(2,1)} %collective-permute-done.10.refs_2_), channel_id=1, source_target_pairs={{0,1},{1,0},{2,3},{3,2},{4,5},{5,4},{6,7},{7,6},{8,9},{9,8},{10,11... | collective-permute-start | bytes 2555912 | tf_op jit(solution)/shard_map/ppermute | solution.py:775
  127.7 6.0 %collective-permute-start.19 = (bf16[4,13,16,512]{3,2,1,0:T(8,128)(2,1)}, bf16[4,13,16,512]{3,2,1,0:T(8,128)(2,1)}, u32[]{:S(2)}, u32[]{:S(2)}) collective-permute-start(bf16[4,13,16,512]{3,2,1,0:T(8,128)(2,1)} %collective-permute-done.11.refs_3_), channel_id=1, source_target_pairs={{0,1},{1,0},{2,3},{3,2},{4,5},{5,4},{6,7},{7,6},{8,9},{9,8},{10,11... | collective-permute-start | bytes 2555912 | tf_op jit(solution)/shard_map/ppermute | solution.py:775
  307.1 17.1 %copy-start.27 = (s32[32]{0:T(128)S(1)}, s32[32]{0:T(128)}, u32[]{:S(2)}) copy-start(s32[32]{0:T(128)} %param.19) | copy-start | bytes 388
  307.1 17.7 %copy-start.13 = (f32[2,8,512]{2,1,0:T(8,128)S(1)}, f32[2,8,512]{2,1,0:T(8,128)}, u32[]{:S(2)}) copy-start(f32[2,8,512]{2,1,0:T(8,128)} %get-tuple-element.79) | copy-start | bytes 98308
  307.2 17.8 %copy-start.10 = (bf16[2,1024]{1,0:T(2,128)(2,1)S(1)}, bf16[2,1024]{1,0:T(2,128)(2,1)}, u32[]{:S(2)}) copy-start(bf16[2,1024]{1,0:T(2,128)(2,1)} %copy-done.9) | copy-start | bytes 12292
  307.2 17.8 %copy-start.18 = (f32[8,512]{1,0:T(8,128)S(1)}, f32[8,512]{1,0:T(8,128)}, u32[]{:S(2)}) copy-start(f32[8,512]{1,0:T(8,128)} %get-tuple-element.81) | copy-start | bytes 49156
  307.2 18.0 %copy-start.17 = (f32[8,512]{1,0:T(8,128)S(1)}, f32[8,512]{1,0:T(8,128)}, u32[]{:S(2)}) copy-start(f32[8,512]{1,0:T(8,128)} %get-tuple-element.82) | copy-start | bytes 49156
  324.2 4.9 %collective-permute-start.20 = (bf16[4,4,9,16,512]{4,3,2,1,0:T(8,128)(2,1)}, bf16[4,4,9,16,512]{4,3,2,1,0:T(8,128)(2,1)}, u32[]{:S(2)}, u32[]{:S(2)}) collective-permute-start(bf16[4,4,9,16,512]{4,3,2,1,0:T(8,128)(2,1)} %get-tuple-element.71), channel_id=1, source_target_pairs={{0,1},{1,0},{2,3},{3,2},{4,5},{5,4},{6,7},{7,6},{8,9},{9,8},{10,11... | collective-permute-start | bytes 7077896 | tf_op jit(solution)/shard_map/ppermute | solution.py:775
  333.6 28.2 %collective-permute-start.21 = (bf16[4,9,16,512]{3,2,1,0:T(8,128)(2,1)}, bf16[4,9,16,512]{3,2,1,0:T(8,128)(2,1)}, u32[]{:S(2)}, u32[]{:S(2)}) collective-permute-start(bf16[4,9,16,512]{3,2,1,0:T(8,128)(2,1)} %get-tuple-element.94), channel_id=1, source_target_pairs={{0,2},{1,3},{2,0},{3,1},{4,6},{5,7},{6,4},{7,5},{8,10},{9,11},{10,... | collective-permute-start | bytes 1769480 | tf_op jit(solution)/shard_map/ppermute | solution.py:775
  335.1 26.8 %collective-permute-start.22 = (bf16[4,9,16,512]{3,2,1,0:T(8,128)(2,1)}, bf16[4,9,16,512]{3,2,1,0:T(8,128)(2,1)}, u32[]{:S(2)}, u32[]{:S(2)}) collective-permute-start(bf16[4,9,16,512]{3,2,1,0:T(8,128)(2,1)} %get-tuple-element.93), channel_id=1, source_target_pairs={{0,16},{1,17},{2,18},{3,19},{4,20},{5,21},{6,22},{7,23},{8,24},{9,... | collective-permute-start | bytes 1769480 | tf_op jit(solution)/shard_map/ppermute | solution.py:775
  336.6 26.7 %collective-permute-start.23 = (bf16[4,9,16,512]{3,2,1,0:T(8,128)(2,1)S(1)}, bf16[4,9,16,512]{3,2,1,0:T(8,128)(2,1)}, u32[]{:S(2)}, u32[]{:S(2)}) collective-permute-start(bf16[4,9,16,512]{3,2,1,0:T(8,128)(2,1)S(1)} %get-tuple-element.92), channel_id=1, source_target_pairs={{0,18},{1,19},{2,16},{3,17},{4,22},{5,23},{6,20},{7,21},{8,26},{9,... | collective-permute-start | bytes 1769480 | tf_op jit(solution)/shard_map/ppermute | solution.py:775
  365.2 26.5 %collective-permute-start.24 = (bf16[9,16,512]{2,1,0:T(8,128)(2,1)S(1)}, bf16[9,16,512]{2,1,0:T(8,128)(2,1)S(1)}, u32[]{:S(2)}, u32[]{:S(2)}) collective-permute-start(bf16[9,16,512]{2,1,0:T(8,128)(2,1)S(1)} %get-tuple-element.76), channel_id=1, source_target_pairs={{0,4},{1,5},{2,6},{3,7},{4,0},{5,1},{6,2},{7,3},{8,12},{9,13},{10,... | collective-permute-start | bytes 442376 | tf_op jit(solution)/shard_map/ppermute | solution.py:775
  369.8 21.9 %collective-permute-start.25 = (bf16[9,16,512]{2,1,0:T(8,128)(2,1)S(1)}, bf16[9,16,512]{2,1,0:T(8,128)(2,1)S(1)}, u32[]{:S(2)}, u32[]{:S(2)}) collective-permute-start(bf16[9,16,512]{2,1,0:T(8,128)(2,1)S(1)} %get-tuple-element.77), channel_id=1, source_target_pairs={{0,8},{1,9},{2,10},{3,11},{4,12},{5,13},{6,14},{7,15},{8,0},{9,1},... | collective-permute-start | bytes 442376 | tf_op jit(solution)/shard_map/ppermute | solution.py:775
  369.8 21.9 %collective-permute-start.26 = (bf16[9,16,512]{2,1,0:T(8,128)(2,1)S(1)}, bf16[9,16,512]{2,1,0:T(8,128)(2,1)S(1)}, u32[]{:S(2)}, u32[]{:S(2)}) collective-permute-start(bf16[9,16,512]{2,1,0:T(8,128)(2,1)S(1)} %get-tuple-element.78), channel_id=1, source_target_pairs={{0,12},{1,13},{2,14},{3,15},{4,8},{5,9},{6,10},{7,11},{8,4},{9,5},... | collective-permute-start | bytes 442376 | tf_op jit(solution)/shard_map/ppermute | solution.py:775
  390.2 7.2 %collective-permute-start.27 = (bf16[13,16,512]{2,1,0:T(8,128)(2,1)S(1)}, bf16[13,16,512]{2,1,0:T(8,128)(2,1)S(1)}, u32[]{:S(2)}, u32[]{:S(2)}) collective-permute-start(bf16[13,16,512]{2,1,0:T(8,128)(2,1)S(1)} %dynamic-slice_bitcast_fusion), channel_id=1, source_target_pairs={{0,16},{1,17},{2,18},{3,19},{4,20},{5,21},{6,22},{7,23},{8,24},{9,... | collective-permute-start | bytes 638984 | tf_op jit(solution)/shard_map/ppermute | solution.py:775
  425.1 18.0 %collective-permute-start.28 = (bf16[16,41,512]{2,0,1:T(8,128)(2,1)}, bf16[16,41,512]{2,0,1:T(8,128)(2,1)S(1)}, u32[]{:S(2)}, u32[]{:S(2)}) collective-permute-start(bf16[16,41,512]{2,0,1:T(8,128)(2,1)} %copy.74), channel_id=1, source_target_pairs={{0,16},{1,17},{2,18},{3,19},{4,20},{5,21},{6,22},{7,23},{8,24},{9,... | collective-permute-start | bytes 2015240 | tf_op jit(solution)/shard_map/ppermute | solution.py:775
  460.5 5.3 %copy-start.12 = (f32[13,32]{1,0:T(8,128)S(1)}, f32[13,32]{1,0:T(8,128)}, u32[]{:S(2)}) copy-start(f32[13,32]{1,0:T(8,128)} %param.25) | copy-start | bytes 4996
  460.5 5.3 %copy-start.15 = (f32[13,32]{1,0:T(8,128)S(1)}, f32[13,32]{1,0:T(8,128)}, u32[]{:S(2)}) copy-start(f32[13,32]{1,0:T(8,128)} %param.27) | copy-start | bytes 4996
  460.6 5.3 %copy-start.16 = (f32[13,32]{1,0:T(8,128)S(1)}, f32[13,32]{1,0:T(8,128)}, u32[]{:S(2)}) copy-start(f32[13,32]{1,0:T(8,128)} %param.26) | copy-start | bytes 4996
  (12 other events, 32.2 us)
Sparse Core Ops, SparseCore 0:
  82.2 71.1 all-gather.2
  281.4 107.7 reduce-scatter.1

commit v3 on v2

--- a/solution.py
+++ b/solution.py
@@ -146,7 +146,7 @@
     return total
 
 
-CONV_ROWS = 512
+CONV_ROWS = 1024
 
 
 PIECES = 32
@@ -156,6 +156,11 @@
 def piece_rows(ids, core, plane, line):
     index = ((ids[0] ^ core) * 4 + (ids[1] ^ plane)) * 4 + (ids[2] ^ line)
     return pl.ds(pl.multiple_of(index * PIECE, PIECE), PIECE)
+
+
+DIRECT = (((0,), 0), ((1,), 0), ((2,), 0), ((3,), 0))
+HALVED = (((0, 2), 0), ((1, 3), 0), ((0, 1), 1), ((2, 3), 1))
+COPIES = 64
 
 
 def flat_place(n):
@@ -173,13 +178,20 @@
             for n in range(PIECES)
         ]
     copies = []
-    for core in range(2):
-        for plane in range(4):
+    layout = HALVED if parts[0].shape[0] == 2 else DIRECT
+    for n, part in enumerate(parts):
+        planes, half = layout[n % 4]
+        start = half * parts[0].shape[2]
+        low, high = max(first, start), min(first + count, start + part.shape[2])
+        if low >= high:
+            continue
+        for side, plane in enumerate(planes):
             for line in range(4):
+                rows = piece_rows(ids, n // 4, plane, line)
                 copies.append(
                     pltpu.make_async_copy(
-                        parts[core * 4 + plane].at[line, pl.ds(first, count)],
-                        dest.at[:, piece_rows(ids, core, plane, line), :],
+                        part.at[side, line, pl.ds(low - start, high - low)],
+                        dest.at[pl.ds(low - first, high - low), rows, :],
                         sem.at[len(copies)],
                     )
                 )
@@ -215,11 +227,20 @@
 
 
 def fwd_one(ids, *refs):
-    parts, (x, vec, h1, a1, weights, slab, sem) = refs[:8], refs[8:]
+    parts, (x, h1, a1, vec, weights, slab, held, sem, vec_sem) = refs[:8], refs[8:]
     step = pl.program_id(0)
 
-    @pl.when(step == 0)
-    def _():
+    def vec_copies():
+        last = [part for n, part in enumerate(parts) if n % 4 > 1]
+        return [
+            pltpu.make_async_copy(part.at[:, :, part.shape[2] - 1], held.at[n], vec_sem.at[n])
+            for n, part in enumerate(last)
+        ]
+
+    @pl.when(step == 0)
+    def _():
+        for copy in vec_copies():
+            copy.start()
         start_all(ids, parts, weights, sem, 0, 9)
         clear_pads(slab)
 
@@ -227,6 +248,16 @@
         return x[0, rows, :].astype(F32)
 
     mean, inv = norm_stats(read)
+
+    @pl.when(step == 0)
+    def _():
+        for copy in vec_copies():
+            copy.wait()
+        total = jnp.zeros((16, C), F32)
+        for n in range(PIECES):
+            total = total + held[n // 8, n // 4 % 2, n % 4].astype(F32)
+        vec[...] = total
+
     gain = inv * vec[0:1]
     bias = vec[1:2]
 
@@ -308,7 +339,8 @@
 def attention(ids, weight, live, *refs):
     parts = refs[:1]
     (
-    r1, cot, vec, out, dr1, grads, sums, weights, nhat, n3, n3t, q, k, v, da, dat, qt, att, dyb, dq, dk, dv, dkt, dvt, dn3, acc, sem,
+    r1, cot, vec, out, dr1, grads, sums, weights,
+    nhat, n3, n3t, q, k, v, da, dat, qt, kt, vt, att, dyb, dq, dk, dv, dn3, acc, sem,
     ) = refs[1:]
     step = pl.program_id(0)
 
@@ -350,55 +382,53 @@
     chunks(HW // MM_ROWS, project)
     n3t[...] = n3[...].T
     qt[...] = q[...].T
+    kt[...] = k[...].T
+    vt[...] = v[...].T
     dat[...] = da[...].T
 
     def head_pair(pair, _):
         cols = pl.ds(pl.multiple_of(pair * 128, 128), 128)
-        dkt[...] = jnp.zeros((128, HW), F32)
-        dvt[...] = jnp.zeros((128, HW), F32)
-
-        def query_rows(c, _):
-            rows = rows_of(c, QROWS)
-            keys = k[:, cols]
-            values = v[:, cols]
-            q_pair = q[rows, cols]
-            da_pair = da[rows, cols]
-            lane = lax.broadcasted_iota(jnp.int32, (QROWS, 128), 1)
-            parts = []
-            for side in range(2):
-                mine = (lane < HEAD) if side == 0 else (lane >= HEAD)
-                q_one = jnp.where(mine, q_pair, jnp.zeros_like(q_pair))
-                da_one = jnp.where(mine, da_pair, jnp.zeros_like(da_pair))
-                head_rows = pl.ds(pl.multiple_of(pair * 128 + side * HEAD, HEAD), HEAD)
-                scores = mm_t(q_one, keys)
-                top = jnp.max(scores, axis=1, keepdims=True)
-                expo = jnp.exp(scores - top)
-                probs = expo * (1.0 / jnp.sum(expo, axis=1, keepdims=True))
-                low = probs.astype(BF16)
-                dprobs = mm_t(da_one, values)
-                dot = jnp.sum(probs * dprobs, axis=1, keepdims=True)
-                dscores = (probs * (dprobs - dot)).astype(BF16)
-                acc_rows = slice(side * HEAD, (side + 1) * HEAD)
-                dvt[acc_rows, :] += mm(dat[head_rows, rows], low)
-                dkt[acc_rows, :] += mm(qt[head_rows, rows], dscores)
-                parts.append((mm(low, values), mm(dscores, keys)))
-            first = lane < HEAD
-            att[rows, cols] = jnp.where(first, parts[0][0], parts[1][0]).astype(BF16)
-            dq[rows, cols] = (jnp.where(first, parts[0][1], parts[1][1]) * 0.125).astype(BF16)
-            return 0
-
-        chunks(HW // QROWS, query_rows)
-        dk[:, cols] = dkt[...].astype(BF16).T
-        dv[:, cols] = dvt[...].astype(BF16).T
+        first = lax.broadcasted_iota(jnp.int32, (HW, 128), 1) < HEAD
+
+        def one_head(value, side):
+            blank = jnp.zeros_like(value)
+            return jnp.where(first, value, blank) if side == 0 else jnp.where(first, blank, value)
+
+        keys, values = k[:, cols], v[:, cols]
+        expos, scaled, dots = [], [], []
+        for side in range(2):
+            head_rows = pl.ds(pl.multiple_of(pair * 128 + side * HEAD, HEAD), HEAD)
+            scores = mm(one_head(keys, side), qt[cols, :])
+            expo = jnp.exp(scores - jnp.max(scores, axis=0, keepdims=True))
+            inverse = 1.0 / jnp.sum(expo, axis=0, keepdims=True)
+            expos.append(expo.astype(BF16))
+            attended = mm(vt[head_rows, :], expos[side]) * inverse
+            att[head_rows, :] = attended.astype(BF16)
+            scaled.append((dat[head_rows, :].astype(F32) * inverse).astype(BF16))
+            dots.append(jnp.sum(attended * scaled[side].astype(F32), axis=0, keepdims=True))
+        both = jnp.concatenate(scaled, axis=0)
+        turned = both.T
+        dks, dvs = [], []
+        for side in range(2):
+            head_rows = pl.ds(pl.multiple_of(pair * 128 + side * HEAD, HEAD), HEAD)
+            dprobs = mm(one_head(values, side), both)
+            dscores = (expos[side].astype(F32) * (dprobs - dots[side])).astype(BF16)
+            dvs.append(mm(expos[side], turned))
+            dks.append(mm(dscores, q[:, cols]))
+            dat[head_rows, :] = (mm(kt[head_rows, :], dscores) * 0.125).astype(BF16)
+        dk[:, cols] = jnp.where(first, dks[0], dks[1]).astype(BF16)
+        dv[:, cols] = jnp.where(first, dvs[0], dvs[1]).astype(BF16)
         return 0
 
     chunks(HEADS // 2, head_pair)
+    dq[...] = dat[...].T
+    q[...] = att[...].T
 
     is_live = live[step] > 0
 
     def result(c, _):
         rows = rows_of(c, MM_ROWS)
-        y = r1[0, rows, :] + mm(att[rows, :], weights[3]) + vec[12:13]
+        y = r1[0, rows, :] + mm(q[rows, :], weights[3]) + vec[12:13]
         out[0, rows, :] = jnp.where(is_live, y, 0.0).astype(BF16)
         dn3[rows, :] = (
             mm_t(dq[rows, :], weights[0])
@@ -409,12 +439,11 @@
 
     chunks(HW // MM_ROWS, result)
 
-    qt[...] = att[...].T
     terms = (
         lambda: mm(n3t[...], dq[...]),
         lambda: mm(n3t[...], dk[...]),
         lambda: mm(n3t[...], dv[...]),
-        lambda: mm(qt[...], dyb[...]),
+        lambda: mm(att[...], dyb[...]),
     )
     for n, term in enumerate(terms):
         @pl.when(step == 0)
@@ -581,7 +610,8 @@
             store_pieces(ids, keep, send, tap, tap_grad(slab, at, tap))
             return 0
 
-        chunks(9, one)
+        for tap in range(9):
+            one(tap, 0)
 
 
 def two_taps(grad, act, others, out, slab, at):
@@ -595,7 +625,8 @@
             store_flat(out, tap, tap_grad(slab, at, tap))
             return 0
 
-        chunks(9, one)
+        for tap in range(9):
+            one(tap, 0)
 
 
 def bwd_one_data(ids, *refs):
@@ -691,11 +722,11 @@
 IMAGE = per_image(HW, C)
 VEC = whole(16, C)
 PARTS = [ANY] * 8
-SEMS = pltpu.SemaphoreType.DMA((PIECES,))
+SEMS = pltpu.SemaphoreType.DMA((COPIES,))
 
 
 def layer(images, embeds, cotangent, weight, live, plan, gathered):
-    chunk_one, vectors, planes_two, chunk_attn = gathered
+    chunk_one, planes_two, chunk_attn = gathered
     ids = plan.ids
     count = images.shape[0]
     big = lambda kind: struct((count, HW, C), kind)
@@ -707,10 +738,11 @@
     low = pltpu.VMEM((HW, C), BF16)
     lowt = pltpu.VMEM((C, HW), BF16)
     full = pltpu.VMEM((HW, C), F32)
-    pair = pltpu.VMEM((128, HW), F32)
-    h1, a1 = call(
-        fwd_one, count, [SMEM] + PARTS + [IMAGE, VEC], [IMAGE, IMAGE], [big(F32), big(BF16)],
-        [taps, slab, SEMS], (ids, *chunk_one, images, vectors), "first_conv",
+    h1, a1, vectors = call(
+        fwd_one, count, [SMEM] + PARTS + [IMAGE], [IMAGE, IMAGE, VEC],
+        [big(F32), big(BF16), struct((16, C), F32)],
+        [taps, slab, pltpu.VMEM((4, 2, 4, PIECE, C), BF16), SEMS, pltpu.SemaphoreType.DMA((4,))],
+        (ids, *chunk_one, images), "first_conv",
     )
     planes_two, h1 = lax.optimization_barrier((planes_two, h1))
     chunk_two = plan.gather_core(planes_two)
@@ -728,8 +760,8 @@
         attention, count, [SMEM, SMEM, SMEM, ANY] + [IMAGE, IMAGE, VEC],
         [IMAGE, IMAGE, whole(16, 4, 2, PIECE, C), whole(8, C)],
         [big(BF16), big(F32), struct((16, 4, 2, PIECE, C), BF16), struct((8, C), F32)],
-        [maps, full, low, lowt, low, low, low, low, lowt, lowt, low, low,
-         low, low, low, pair, pair, full, pltpu.VMEM((4, C, C), F32), SEMS],
+        [maps, full, low, lowt, low, low, low, low, lowt, lowt, lowt, lowt, lowt,
+         low, low, low, low, full, pltpu.VMEM((4, C, C), F32), SEMS],
         (ids, weight, live, chunk_attn, r1, cotangent, vectors), "attention", 80 * 10**9,
     )
     (early,) = call(
@@ -768,6 +800,60 @@
     return out, dx, demb[:, 0], grads, map_terms, grad_vectors
 
 
+def split_two(value):
+    high = value.astype(BF16)
+    return high, (value - high.astype(F32)).astype(BF16)
+
+
+def mm_two(dot, a, b):
+    return dot(a[0], b[0]) + (dot(a[0], b[1]) + dot(a[1], b[0]))
+
+
+def rotated_adam(block, rate, got, terms, left, right, first, second, master, *refs):
+    new_first, new_second, new_master, low, grad = refs
+    slot = pl.program_id(0)
+    held = block[slot]
+    for n in range(PIECES):
+        place = flat_place(n) * PIECE
+        grad[place : place + PIECE] = got[n, rows_of(slot, PIECE), :]
+
+    @pl.when((held >= 18) & (held < 22))
+    def _():
+        acts = terms[(held - 18) % 2]
+        sides = terms[2 + (held - 18) // 2]
+        grad[...] = mm(acts.astype(F32).T.astype(BF16), sides).astype(BF16)
+
+    lefts = split_two(left[0])
+    rights = split_two(right[0])
+    g = grad[...]
+    turned = split_two(mm(g, rights[0]) + mm(g, rights[1]))
+    rotated = mm_two(mm, (lefts[0].T, lefts[1].T), turned)
+    moment = MOMENT_DECAY * first[0] + (1.0 - MOMENT_DECAY) * rotated
+    square = MOMENT_DECAY * second[0] + (1.0 - MOMENT_DECAY) * rotated * rotated
+    new_first[0] = moment
+    new_second[0] = square
+    correction = 1.0 - MOMENT_DECAY**STEP
+    direction = split_two(
+        moment * (1.0 / correction) / (jnp.sqrt(square * (1.0 / correction)) + ADAM_EPS)
+    )
+    update = mm_two(mm, lefts, split_two(mm_two(mm_t, direction, rights)))
+    fresh = master[0] - rate[slot] * (update + WEIGHT_DECAY * master[0])
+    new_master[0] = fresh
+    low[0] = fresh.astype(BF16)
+
+
+def optimize(slot_block, rate, got, terms, state):
+    count = state[0].shape[0]
+    matrix = per_image(C, C)
+    full = struct((count, C, C), F32)
+    return call(
+        rotated_adam, count,
+        [SMEM, SMEM, whole(*got.shape), whole(*terms.shape)] + [matrix] * 5,
+        [matrix] * 4, [full, full, full, struct((count, C, C), BF16)],
+        [pltpu.VMEM((C, C), BF16)], (slot_block, rate, got, terms, *state), "rotated_adam",
+    )
+
+
 AXES = ("rep", "shard")
 
 
@@ -783,8 +869,20 @@
     return jnp.stack([piece] + [swap(piece, 4 * k) for k in (1, 2, 3)])
 
 
+def gather_first(line):
+    split = (line.shape[1] + 1) // 2
+    halves = line[:, :split], line[:, split:]
+    return [jnp.stack([half, swap(half, mask)]) for half, mask in zip(halves, (16, 2))]
+
+
+def gather_second(firsts):
+    seconds = [swap(first, mask) for first, mask in zip(firsts, (2, 16))]
+    return [firsts[0], seconds[0], firsts[1], seconds[1]]
+
+
 def gather_plane(line):
-    return [line] + [swap(line, plane_mask(k)) for k in (1, 2, 3)]
+    line = line[None]
+    return [line] + [swap(line, mask) for mask in (2, 16, 18)]
 
 
 def gather_core(plane):
@@ -829,16 +927,14 @@
         vec = jnp.pad(vec_master.astype(BF16), ((0, 16 - VECS), (0, C - width)))
         place = lax.axis_index("shard") * width
         vec = jnp.where(self.rep == 0, jnp.roll(vec, place, axis=1), jnp.zeros((), BF16))
-        attn = lax.all_gather(blocks[22:26], AXES)
         line_one = gather_line(jnp.concatenate([blocks[:9], vec[None]], axis=0))
         second, line_one = lax.optimization_barrier((blocks[9:22], line_one))
-        plane_one = gather_plane(line_one)
+        first_one = gather_first(line_one)
         line_two = gather_line(second)
-        line_two, plane_one = lax.optimization_barrier((line_two, plane_one))
-        one = gather_core(plane_one)
-        two = gather_plane(line_two)
-        vectors = sum(jnp.sum(part[:, 9].astype(F32), axis=0) for part in one)
-        return one, vectors, two, attn
+        planes_one = gather_second(first_one)
+        line_two, attn, planes_one = lax.optimization_barrier((line_two, blocks[22:26], planes_one))
+        one = gather_core(planes_one)
+        return one, gather_plane(line_two), lax.all_gather(attn, AXES)
 
     def gather_core(self, planes):
         return gather_core(planes)
@@ -869,17 +965,11 @@
         vec = grad_vectors.astype(BF16).reshape(VECS, 16, width).transpose(1, 0, 2)
         vec = jnp.pad(vec.reshape(16, 1, VECS * width), ((0, 0), (0, 0), (0, C - VECS * width)))
         sent = jnp.concatenate([picked, terms, vec], axis=1)
-        mine = lax.all_to_all(sent, "shard", 0, 0)
-        other = swap(mine, 16)
-        first = jnp.where(self.rep == 0, mine, other)
-        second = jnp.where(self.rep == 0, other, mine)
-        both = jnp.stack([first, second])
+        got = lax.all_to_all(jnp.concatenate([sent, sent]), AXES, 0, 0)
         split = mat_dev * PIECE
-        rows = both[:, :, :split].reshape(2, 4, 2, 2, mat_dev, PIECE, C)
-        rows = rows.transpose(4, 3, 0, 2, 1, 5, 6).reshape(mat_dev, C, C)
-        terms = both[:, :, split:-1].reshape(-1, map_terms.shape[1])
-        vec = jnp.sum(both[:, :, -1, : VECS * width].astype(F32), axis=(0, 1))
-        return rows.astype(F32), terms, vec.reshape(VECS, width)
+        terms = got[:, split:-1].reshape(-1, 4, C).transpose(1, 0, 2)
+        vec = jnp.sum(got[:, -1, : VECS * width].astype(F32), axis=0)
+        return got, terms, vec.reshape(VECS, width)
 
 
 class Plain:
@@ -892,13 +982,19 @@
         blocks = jnp.take(slots, owner[:BLOCKS], axis=0)
 
         def parts(some):
-            split = some.reshape(-1, 2, 4, 4, PIECE, C).transpose(1, 2, 3, 0, 4, 5)
-            return [split[core, plane] for core in range(2) for plane in range(4)]
-
-        vectors = jnp.pad(vec.astype(F32), ((0, 16 - VECS), (0, 0)))
+            split = (some.shape[0] + 1) // 2
+            pieces = some.reshape(-1, 2, 4, 4, PIECE, C).transpose(1, 2, 3, 0, 4, 5)
+            halves = (slice(0, split), slice(split, None))
+            return [
+                jnp.stack([pieces[core, plane][:, halves[n // 2]] for plane in planes])
+                for core in range(2)
+                for n, (planes, _) in enumerate(HALVED)
+            ]
+
+        rows = jnp.zeros((C, C), BF16).at[:VECS].set(vec)
+        one = parts(jnp.concatenate([blocks[:9], rows[None]], axis=0))
         flat = blocks[22:26].reshape(4, 2, 2, 2, 4, PIECE, C).transpose(2, 4, 3, 1, 0, 5, 6)
-        attn = flat.reshape(PIECES, 4, PIECE, C)
-        return parts(blocks[:9]), vectors, parts(blocks[9:22]), attn
+        return one, parts(blocks[9:22]), flat.reshape(PIECES, 4, PIECE, C)
 
     def gather_core(self, planes):
         return planes
@@ -919,10 +1015,12 @@
     def own(self, grads, slots, mat_dev, map_terms, grad_vectors):
         picked = pick_slots(grads, slots)
         mine = lax.psum_scatter(picked, "shard", scatter_dimension=0, tiled=True)
-        rows = lax.psum(mine, "rep").astype(F32)
+        rows = lax.psum(mine, "rep").reshape(mat_dev, 2, 2, 2, 4, PIECE, C)
+        got = rows.transpose(2, 4, 3, 1, 0, 5, 6).reshape(PIECES, mat_dev * PIECE, C)
         terms = lax.all_gather(map_terms, AXES, axis=0, tiled=True)
+        terms = terms.reshape(-1, 4, C).transpose(1, 0, 2)
         vec = lax.psum_scatter(grad_vectors, "shard", scatter_dimension=1, tiled=True)
-        return rows, terms, lax.psum(vec, "rep")
+        return got, terms, lax.psum(vec, "rep")
 
 
 def shards(
@@ -956,33 +1054,16 @@
     all_slots = block_slots(owner, mats_all)
     shard = lax.axis_index("shard")
     slot_block = lax.dynamic_slice_in_dim(all_slots, shard * mat_dev, mat_dev, 0)
-    own_grads, all_terms, own_vec = plan.own(
-        grads, all_slots, mat_dev, map_terms, grad_vectors
-    )
-    maps = slot_block - 18
-    lower = (maps % 2 == 0)[:, None, None]
-    acts = jnp.where(lower, all_terms[None, :, :C], all_terms[None, :, C:EMB])
-    is_scale = (maps < 2)[:, None, None]
-    sides = jnp.where(is_scale, all_terms[None, :, EMB : EMB + C], all_terms[None, :, EMB + C :])
-    map_grads = jnp.einsum("sic,sio->sco", acts, sides, preferred_element_type=F32)
-    is_map = ((maps >= 0) & (maps < 4))[:, None, None]
-    own_grads = jnp.where(is_map, map_grads, own_grads)
-    rotated = jnp.matmul(
-        jnp.matmul(jnp.swapaxes(left_basis, 1, 2), own_grads, precision=PRECISE),
-        right_basis,
-        precision=PRECISE,
-    )
-    new_first = MOMENT_DECAY * first_moment + (1.0 - MOMENT_DECAY) * rotated
-    new_second = MOMENT_DECAY * second_moment + (1.0 - MOMENT_DECAY) * rotated * rotated
+    got, terms, own_vec = plan.own(grads, all_slots, mat_dev, map_terms, grad_vectors)
+    step_rate = jnp.where(slot_block < BLOCKS, 2.0 * block_spread(slot_block), 0.0)
+    new_first, new_second, new_master, master_low = optimize(
+        slot_block,
+        step_rate,
+        got,
+        terms,
+        (left_basis, right_basis, first_moment, second_moment, master),
+    )
     correction = 1.0 - MOMENT_DECAY**STEP
-    direction = new_first / correction / (jnp.sqrt(new_second / correction) + ADAM_EPS)
-    update = jnp.matmul(
-        jnp.matmul(left_basis, direction, precision=PRECISE),
-        jnp.swapaxes(right_basis, 1, 2),
-        precision=PRECISE,
-    )
-    step_rate = jnp.where(slot_block < BLOCKS, 2.0 * block_spread(slot_block), 0.0)
-    new_master = master - step_rate[:, None, None] * (update + WEIGHT_DECAY * master)
     vec_first_new = MOMENT_DECAY * vec_first + (1.0 - MOMENT_DECAY) * own_vec
     vec_second_new = MOMENT_DECAY * vec_second + (1.0 - MOMENT_DECAY) * own_vec * own_vec
     vec_master_new = vec_master - VECTOR_RATE * (vec_first_new / correction) / (
@@ -995,7 +1076,7 @@
         new_first,
         new_second,
         new_master,
-        new_master.astype(jnp.bfloat16),
+        master_low,
         vec_first_new,
         vec_second_new,
         vec_master_new,

time: 480 us -> 452 us (0.942)
  blocking collectives: 24.5 us -> 0 us
  waiting for transfers between devices: 105 us -> 129 us
  matrix products: 18.2 us -> 0 us
  other arithmetic: 23.1 us -> 15.7 us
    all_to_all x0 -> x1, waiting for transfers between devices: none -> 36.5 us  [own(): got = lax.all_to_all(jnp.concatenate([sent, sent]), AXES, 0, 0)]
    all_to_all x1 -> x0, blocking collectives: 24.5 us -> none  [own(): mine = lax.all_to_all(sent, 'shard', 0, 0)]
    dot_general x5 -> x0, matrix products: 18.2 us -> none  [the longest x1 5.3 us: shards(): jnp.matmul(jnp.matmul(left_basis, direction, precision=PRECISE), jnp.swap...]
    ppermute x29, waiting for transfers between devices: 74.4 us -> 61.3 us  [swap(): return lax.ppermute(value, AXES, [(i, i ^ mask) for i in range(PIECES)])]
    reduce_sum x7 -> x1, other arithmetic: 5.33 us -> 0.08 us  [own(): vec = jnp.sum(got[:, -1, :VECS * width].astype(F32), axis=0)]
    pallas_call x7 -> x8, Pallas kernels: 231 us -> 228 us  [call(): pl.pallas_call(body, grid=(images,), in_specs=in_specs, out_specs=out_spe...]
  transfers between devices with their start and end apart: 32 -> 33, of which waited for: 13 -> 14; matrix products, arithmetic and copies ran while one was open for 5% -> 4% of each run, Pallas kernels for 23% -> 24%
where the time goes in v3:
time: 452 us; the launch traced here: 444 us
  Pallas kernels  228 us (50%)
  waiting for transfers between devices  129 us (29%)
  starting transfers between devices  43.1 us (10%)
  between operations  16.4 us (4%)
  other arithmetic  15.7 us (3%)
  local copies, waits for them, and re-layouts  12 us (3%)
    pallas_call x8, Pallas kernels, call(): pl.pallas_call(body, grid=(images,), in_specs=in_specs, out_specs=out_spe...  228 us
    ppermute x29, waiting for transfers between devices, swap(): return lax.ppermute(value, AXES, [(i, i ^ mask) for i in range(PIECES)])  61.3 us
    all_to_all x1, waiting for transfers between devices, own(): got = lax.all_to_all(jnp.concatenate([sent, sent]), AXES, 0, 0)  36.5 us
    ppermute x29, starting transfers between devices, swap(): return lax.ppermute(value, AXES, [(i, i ^ mask) for i in range(PIECES)])  31.7 us
    reduce_scatter x1, waiting for transfers between devices, reduce_early(): return lax.psum_scatter(grads, 'shard', scatter_dimension=0, tiled=True)[0]  17.3 us
    all_to_all x1, waiting for transfers between devices, gather(): slots = lax.all_to_all(rows, 'shard', 0, 0).reshape(16 * mat_dev, PIECE, C)  14.2 us
  transfers between devices with their start and end apart: 33, of which 14 were waited for; matrix products, arithmetic and copies ran while one was open for 4% of the time, Pallas kernels for 24%

profile of v3, /device:TPU:0, one launch (start us, length us, event | category | flops | bytes accessed | tf_op | source)
XLA Modules:
  0.0 444.1 jit_solution(14109615011177113110)
XLA Ops:
  7.2 1.7 convert_element_type.199
  9.0 0.8 copy.61
  9.8 7.4 %all-to-all-start = ((bf16[16,2,16,512]{3,2,1,0:T(8,128)(2,1)}), bf16[16,2,16,512]{3,2,1,0:T(8,128)(2,1)S(1)}, u32[]{:S(2)}, u32[]{:S(2)}) async-start(bf16[16,2,16,512]{3,2,1,0:T(8,128)(2,1)} %bitcast.10), calls=%async_computation | async-start | bytes 1048576 | tf_op jit(solution)/shard_map/all_to_all | solution.py:924
  17.5 14.2 %all-to-all-done = bf16[16,2,16,512]{3,2,1,0:T(8,128)(2,1)S(1)} async-done(((bf16[16,2,16,512]{3,2,1,0:T(8,128)(2,1)}), bf16[16,2,16,512]{3,2,1,0:T(8,128)(2,1)S(1)}, u32[]{:S(2)}, u32[]{:S(2)}) %all-to-all-start) | async-done | bytes 524320 | tf_op jit(solution)/shard_map/all_to_all | solution.py:924
  32.4 1.2 collective-permute-start
  33.6 1.2 collective-permute-start.1
  34.8 2.1 collective-permute-start.2
  36.9 3.5 collective-permute-done
  40.4 8.1 %collective-permute-done.1 = bf16[10,16,512]{2,1,0:T(8,128)(2,1)S(1)} collective-permute-done((bf16[10,16,512]{2,1,0:T(8,128)(2,1)S(1)}, bf16[10,16,512]{2,1,0:T(8,128)(2,1)S(1)}, u32[]{:S(2)}, u32[]{:S(2)}) %collective-permute-start.1) | collective-permute-done | bytes 163872 | tf_op jit(solution)/shard_map/ppermute | solution.py:861
  48.8 1.4 collective-permute-start.8
  50.2 1.5 collective-permute-start.6
  51.7 5.8 %collective-permute-done.8 = bf16[4,5,16,512]{3,2,1,0:T(8,128)(2,1)S(1)} collective-permute-done((bf16[4,5,16,512]{3,2,1,0:T(8,128)(2,1)S(1)}, bf16[4,5,16,512]{3,2,1,0:T(8,128)(2,1)S(1)}, u32[]{:S(2)}, u32[]{:S(2)}) %collective-permute-start.8) | collective-permute-done | bytes 327712 | tf_op jit(solution)/shard_map/ppermute | solution.py:861
  57.5 1.6 collective-permute-start.9
  59.2 1.2 collective-permute-start.7
  60.4 3.5 collective-permute-start.3
  64.0 2.3 collective-permute-start.5
  66.9 3.0 collective-permute-done.3
  69.9 10.8 %collective-permute-done.4 = bf16[13,16,512]{2,1,0:T(8,128)(2,1)S(1)} collective-permute-done((bf16[13,16,512]{2,1,0:T(8,128)(2,1)S(1)}, bf16[13,16,512]{2,1,0:T(8,128)(2,1)S(1)}, u32[]{:S(2)}, u32[]{:S(2)}) %collective-permute-start.4) | collective-permute-done | bytes 213024 | tf_op jit(solution)/shard_map/ppermute | solution.py:861
  83.3 0.8 collective-permute-start.11
  84.1 1.0 collective-permute-done.14.refs_5_
  85.1 1.1 collective-permute-start.12
  86.2 19.6 %first_conv.1 = (f32[2,1024,512]{2,1,0:T(8,128)}, bf16[2,1024,512]{2,1,0:T(8,128)(2,1)}, f32[16,512]{1,0:T(8,128)}) custom-call(s32[3]{0:T(128)} %pad_add_fusion.ids, bf16[2,4,5,16,512]{4,3,2,1,0:T(8,128)(2,1)} %copy-done.3, bf16[2,4,5,16,512]{4,3,2,1,0:T(8,128)(2,1)} %collective-permute-done.7.refs_1_, bf16[2,4,5,16,512]{4,3,2,1,0:T(8,128)(2,1)} %copy-done.2, ...), custom_call_target="tpu_custom_call" | custom-call | flops 20000000000 | bytes 31457280 | tf_op jit(solution)/shard_map/first_conv/pallas_call | solution.py:707
  105.8 19.7 %collective-permute-done.12.refs_3_ = bf16[1,4,13,16,512]{4,3,2,1,0:T(8,128)(2,1)} collective-permute-done((bf16[1,4,13,16,512]{4,3,2,1,0:T(8,128)(2,1)S(1)}, bf16[1,4,13,16,512]{4,3,2,1,0:T(8,128)(2,1)}, u32[]{:S(2)}, u32[]{:S(2)}) %collective-permute-start.12) | collective-permute-done | bytes 852000 | tf_op jit(solution)/shard_map/ppermute | solution.py:861
  129.6 2.5 compare_select_fusion.10.weight
  133.3 23.0 %second_conv.1 = (bf16[2,1024,512]{2,1,0:T(8,128)(2,1)}, f32[2,1024,512]{2,1,0:T(8,128)}, f32[2,1024,512]{2,1,0:T(8,128)}, f32[2,8,512]{2,1,0:T(8,128)}) custom-call(s32[3]{0:T(128)} %pad_add_fusion.ids, bf16[1,4,13,16,512]{4,3,2,1,0:T(8,128)(2,1)} %bitcast.109, bf16[1,4,13,16,512]{4,3,2,1,0:T(8,128)(2,1)} %copy-done.18, ...), custom_call_target="tpu_custom_call" | custom-call | flops 20000000000 | bytes 31457280 | tf_op jit(solution)/shard_map/second_conv/pallas_call | solution.py:707
  156.3 90.0 %attention.1 = (bf16[2,1024,512]{2,1,0:T(8,128)(2,1)}, f32[2,1024,512]{2,1,0:T(8,128)}, bf16[16,4,2,16,512]{4,3,2,1,0:T(8,128)(2,1)}, f32[8,512]{1,0:T(8,128)}) custom-call(s32[3]{0:T(128)} %pad_add_fusion.ids, f32[2]{0:T(128)} %compare_select_fusion.10.weight, s32[2]{0:T(128)} %compare_convert_fusion.live, bf16[32,4,16,512]{3,2,1,0:T(8,128)(2,1)} %bitcast.124, ...), custom_call_target="tpu_custom_call" | custom-call | flops 80000000000 | bytes 31457280 | tf_op jit(solution)/shard_map/attention/pallas_call | solution.py:707
  246.4 17.0 %second_conv_taps.1 = bf16[16,13,2,16,512]{4,3,2,1,0:T(8,128)(2,1)} custom-call(f32[2,1024,512]{2,1,0:T(8,128)} %get-tuple-element.73.grad.refs_8_.refs_10_, bf16[2,1024,512]{2,1,0:T(8,128)(2,1)} %get-tuple-element.71.act, bf16[16,4,2,16,512]{4,3,2,1,0:T(8,128)(2,1)} %get-tuple-element.72.others), custom_call_target="tpu_custom_call" | custom-call | flops 20000000000 | bytes 31457280 | tf_op jit(solution)/shard_map/second_conv_taps/pallas_call | solution.py:707
  264.1 25.2 %second_conv_back.1 = (bf16[2,1024,512]{2,1,0:T(8,128)(2,1)}, f32[2,8,512]{2,1,0:T(8,128)}, f32[2,8,1024]{2,1,0:T(8,128)}, f32[8,512]{1,0:T(8,128)}) custom-call(s32[3]{0:T(128)} %pad_add_fusion.ids, bf16[1,4,13,16,512]{4,3,2,1,0:T(8,128)(2,1)} %bitcast.110, bf16[1,4,13,16,512]{4,3,2,1,0:T(8,128)(2,1)} %copy-done.18, ...), custom_call_target="tpu_custom_call" | custom-call | flops 20000000000 | bytes 31457280 | tf_op jit(solution)/shard_map/second_conv_back/pallas_call | solution.py:707
  289.3 15.8 %first_conv_taps.1 = (bf16[4,4,9,16,512]{4,3,2,1,0:T(8,128)(2,1)}, bf16[4,4,9,16,512]{4,3,2,1,0:T(8,128)(2,1)}) custom-call(s32[3]{0:T(128)} %pad_add_fusion.ids, bf16[2,1024,512]{2,1,0:T(8,128)(2,1)} %get-tuple-element.80.grad.refs_8_, bf16[2,1024,512]{2,1,0:T(8,128)(2,1)} %get-tuple-element.77.act), custom_call_target="tpu_custom_call" | custom-call | flops 20000000000 | bytes 31457280 | tf_op jit(solution)/shard_map/first_conv_taps/pallas_call | solution.py:707
  308.0 1.9 collective-permute-done.21
  309.8 3.7 add_convert_fusion
  313.5 0.8 collective-permute-start.22
  315.0 2.0 collective-permute-start.24
  317.0 24.0 %first_conv_back.1 = (f32[2,1024,512]{2,1,0:T(8,128)}, f32[8,512]{1,0:T(8,128)}) custom-call(s32[3]{0:T(128)} %pad_add_fusion.ids, bf16[2,4,5,16,512]{4,3,2,1,0:T(8,128)(2,1)} %copy-done.3, bf16[2,4,5,16,512]{4,3,2,1,0:T(8,128)(2,1)} %collective-permute-done.7.refs_1_, bf16[2,4,5,16,512]{4,3,2,1,0:T(8,128)(2,1)} %copy-done.2, ...), custom_call_target="tpu_custom_call" | custom-call | flops 20000000000 | bytes 31457280 | tf_op jit(solution)/shard_map/first_conv_back/pallas_call | solution.py:707
  341.9 1.1 collective-permute-done.24
  343.5 4.3 collective-permute-start.25
  347.8 2.4 collective-permute-start.27
  350.2 0.8 maximum_bitcast_fusion
  351.2 17.3 %reduce-scatter.2.cloned.1.call-done = bf16[1,13,2,16,512]{4,3,2,1,0:T(8,128)(2,1)} async-done(((bf16[16,13,2,16,512]{4,3,2,1,0:T(8,128)(2,1)}), bf16[1,13,2,16,512]{4,3,2,1,0:T(8,128)(2,1)}) %reduce-scatter.2.cloned.1.call-update) | async-done | bytes 426000 | tf_op jit(solution)/shard_map/reduce_scatter | solution.py:943
  368.5 0.9 dynamic-slice_bitcast_fusion
  370.2 6.0 %collective-permute-done.28 = bf16[13,16,512]{2,1,0:T(8,128)(2,1)S(1)} collective-permute-done((bf16[13,16,512]{2,1,0:T(8,128)(2,1)S(1)}, bf16[13,16,512]{2,1,0:T(8,128)(2,1)S(1)}, u32[]{:S(2)}, u32[]{:S(2)}) %collective-permute-start.28) | collective-permute-done | bytes 213024 | tf_op jit(solution)/shard_map/ppermute | solution.py:861
  376.2 1.0 fusion.4
  378.2 1.3 maximum_maximum_fusion
  379.5 3.9 all-to-all-start.1
  384.1 0.8 slice.152
  385.6 36.5 %all-to-all-done.1.got = bf16[32,41,512]{2,1,0:T(8,128)(2,1)S(1)} async-done(((bf16[32,41,512]{2,1,0:T(8,128)(2,1)}), bf16[32,41,512]{2,1,0:T(8,128)(2,1)S(1)}, u32[]{:S(2)}, u32[]{:S(2)}) %all-to-all-start.1) | async-done | bytes 1343520 | tf_op jit(solution)/shard_map/all_to_all | solution.py:968
  422.2 0.9 copy.66
  423.9 12.9 %rotated_adam.1 = (f32[2,512,512]{2,1,0:T(8,128)}, f32[2,512,512]{2,1,0:T(8,128)}, f32[2,512,512]{2,1,0:T(8,128)}, bf16[2,512,512]{2,1,0:T(8,128)(2,1)}) custom-call(s32[2]{0:T(128)} %get-tuple-element.100.block, f32[2]{0:T(128)} %get-tuple-element.99.rate, bf16[32,41,512]{2,1,0:T(8,128)(2,1)} %copy-done, bf16[4,64,512]{2,1,0:T(8,128)(2,1)} %bitcast.114, ...), custom_call_target="tpu_custom_call" | custom-call | flops 20000000000 | bytes 31457280 | tf_op jit(solution)/shard_map/rotated_adam/pallas_call | solution.py:707
  (146 shorter events, 18.0 us)
Async XLA Ops:
  9.8 21.9 %all-to-all-start = ((bf16[16,2,16,512]{3,2,1,0:T(8,128)(2,1)}), bf16[16,2,16,512]{3,2,1,0:T(8,128)(2,1)S(1)}, u32[]{:S(2)}, u32[]{:S(2)}) async-start(bf16[16,2,16,512]{3,2,1,0:T(8,128)(2,1)} %bitcast.10), calls=%async_computation | async-start | bytes 1048576 | tf_op jit(solution)/shard_map/all_to_all | solution.py:924
  17.2 139.1 %all-gather.3.cloned.1.call-start = ((), (), s32[]{:S(2)}) async-start(), calls=%async_computation.4 | async-start | bytes 2162688 | tf_op jit(solution)/shard_map/all_gather | solution.py:937
  32.4 8.0 %collective-permute-start = (bf16[10,16,512]{2,1,0:T(8,128)(2,1)S(1)}, bf16[10,16,512]{2,1,0:T(8,128)(2,1)S(1)}, u32[]{:S(2)}, u32[]{:S(2)}) collective-permute-start(bf16[10,16,512]{2,1,0:T(8,128)(2,1)S(1)} %get-tuple-element.116), channel_id=1, source_target_pairs={{0,4},{1,5},{2,6},{3,7},{4,0},{5,1},{6,2},{7,3},{8,12},{9,13},{10,... | collective-permute-start | bytes 491528 | tf_op jit(solution)/shard_map/ppermute | solution.py:861
  33.6 15.0 %collective-permute-start.1 = (bf16[10,16,512]{2,1,0:T(8,128)(2,1)S(1)}, bf16[10,16,512]{2,1,0:T(8,128)(2,1)S(1)}, u32[]{:S(2)}, u32[]{:S(2)}) collective-permute-start(bf16[10,16,512]{2,1,0:T(8,128)(2,1)S(1)} %get-tuple-element.116), channel_id=1, source_target_pairs={{0,8},{1,9},{2,10},{3,11},{4,12},{5,13},{6,14},{7,15},{8,0},{9,1},... | collective-permute-start | bytes 491528 | tf_op jit(solution)/shard_map/ppermute | solution.py:861
  34.8 13.7 %collective-permute-start.2 = (bf16[10,16,512]{2,1,0:T(8,128)(2,1)S(1)}, bf16[10,16,512]{2,1,0:T(8,128)(2,1)S(1)}, u32[]{:S(2)}, u32[]{:S(2)}) collective-permute-start(bf16[10,16,512]{2,1,0:T(8,128)(2,1)S(1)} %get-tuple-element.116), channel_id=1, source_target_pairs={{0,12},{1,13},{2,14},{3,15},{4,8},{5,9},{6,10},{7,11},{8,4},{9,5},... | collective-permute-start | bytes 491528 | tf_op jit(solution)/shard_map/ppermute | solution.py:861
  48.8 8.7 %collective-permute-start.8 = (bf16[4,5,16,512]{3,2,1,0:T(8,128)(2,1)S(1)}, bf16[4,5,16,512]{3,2,1,0:T(8,128)(2,1)S(1)}, u32[]{:S(2)}, u32[]{:S(2)}) collective-permute-start(bf16[4,5,16,512]{3,2,1,0:T(8,128)(2,1)S(1)} %get-tuple-element.113), channel_id=1, source_target_pairs={{0,2},{1,3},{2,0},{3,1},{4,6},{5,7},{6,4},{7,5},{8,10},{9,11},{10,... | collective-permute-start | bytes 983048 | tf_op jit(solution)/shard_map/ppermute | solution.py:861
  50.2 8.9 %collective-permute-start.6 = (bf16[4,5,16,512]{3,2,1,0:T(8,128)(2,1)S(1)}, bf16[4,5,16,512]{3,2,1,0:T(8,128)(2,1)S(1)}, u32[]{:S(2)}, u32[]{:S(2)}) collective-permute-start(bf16[4,5,16,512]{3,2,1,0:T(8,128)(2,1)S(1)} %get-tuple-element.114), channel_id=1, source_target_pairs={{0,16},{1,17},{2,18},{3,19},{4,20},{5,21},{6,22},{7,23},{8,24},{9,... | collective-permute-start | bytes 983048 | tf_op jit(solution)/shard_map/ppermute | solution.py:861
  57.5 28.7 %copy-start.2 = (bf16[2,4,5,16,512]{4,3,2,1,0:T(8,128)(2,1)}, bf16[2,4,5,16,512]{4,3,2,1,0:T(8,128)(2,1)S(1)}, u32[]{:S(2)}) copy-start(bf16[2,4,5,16,512]{4,3,2,1,0:T(8,128)(2,1)S(1)} %pad_maximum_fusion.3.refs_2_) | copy-start | bytes 1966084
  57.5 23.3 %collective-permute-start.9 = (bf16[2,4,5,16,512]{4,3,2,1,0:T(8,128)(2,1)S(1)}, bf16[2,4,5,16,512]{4,3,2,1,0:T(8,128)(2,1)}, u32[]{:S(2)}, u32[]{:S(2)}) collective-permute-start(bf16[2,4,5,16,512]{4,3,2,1,0:T(8,128)(2,1)S(1)} %pad_maximum_fusion.3.refs_2_), channel_id=1, source_target_pairs={{0,16},{1,17},{2,18},{3,19},{4,20},{5,21},{6,22},{7,23},{8,24},{9,... | collective-permute-start | bytes 1966088 | tf_op jit(solution)/shard_map/ppermute | solution.py:861
  59.2 27.0 %copy-start.3 = (bf16[2,4,5,16,512]{4,3,2,1,0:T(8,128)(2,1)}, bf16[2,4,5,16,512]{4,3,2,1,0:T(8,128)(2,1)S(1)}, u32[]{:S(2)}) copy-start(bf16[2,4,5,16,512]{4,3,2,1,0:T(8,128)(2,1)S(1)} %pad_maximum_fusion.2.refs_0_) | copy-start | bytes 1966084
  59.2 21.6 %collective-permute-start.7 = (bf16[2,4,5,16,512]{4,3,2,1,0:T(8,128)(2,1)S(1)}, bf16[2,4,5,16,512]{4,3,2,1,0:T(8,128)(2,1)}, u32[]{:S(2)}, u32[]{:S(2)}) collective-permute-start(bf16[2,4,5,16,512]{4,3,2,1,0:T(8,128)(2,1)S(1)} %pad_maximum_fusion.2.refs_0_), channel_id=1, source_target_pairs={{0,2},{1,3},{2,0},{3,1},{4,6},{5,7},{6,4},{7,5},{8,10},{9,11},{10,... | collective-permute-start | bytes 1966088 | tf_op jit(solution)/shard_map/ppermute | solution.py:861
  60.4 9.5 %collective-permute-start.3 = (bf16[13,16,512]{2,1,0:T(8,128)(2,1)S(1)}, bf16[13,16,512]{2,1,0:T(8,128)(2,1)S(1)}, u32[]{:S(2)}, u32[]{:S(2)}) collective-permute-start(bf16[13,16,512]{2,1,0:T(8,128)(2,1)S(1)} %slice.182), channel_id=1, source_target_pairs={{0,4},{1,5},{2,6},{3,7},{4,0},{5,1},{6,2},{7,3},{8,12},{9,13},{10,... | collective-permute-start | bytes 638984 | tf_op jit(solution)/shard_map/ppermute | solution.py:861
  63.9 16.8 %collective-permute-start.4 = (bf16[13,16,512]{2,1,0:T(8,128)(2,1)S(1)}, bf16[13,16,512]{2,1,0:T(8,128)(2,1)S(1)}, u32[]{:S(2)}, u32[]{:S(2)}) collective-permute-start(bf16[13,16,512]{2,1,0:T(8,128)(2,1)S(1)} %slice.182), channel_id=1, source_target_pairs={{0,8},{1,9},{2,10},{3,11},{4,12},{5,13},{6,14},{7,15},{8,0},{9,1},... | collective-permute-start | bytes 638984 | tf_op jit(solution)/shard_map/ppermute | solution.py:861
  64.0 16.7 %collective-permute-start.5 = (bf16[13,16,512]{2,1,0:T(8,128)(2,1)S(1)}, bf16[13,16,512]{2,1,0:T(8,128)(2,1)S(1)}, u32[]{:S(2)}, u32[]{:S(2)}) collective-permute-start(bf16[13,16,512]{2,1,0:T(8,128)(2,1)S(1)} %slice.182), channel_id=1, source_target_pairs={{0,12},{1,13},{2,14},{3,15},{4,8},{5,9},{6,10},{7,11},{8,4},{9,5},... | collective-permute-start | bytes 638984 | tf_op jit(solution)/shard_map/ppermute | solution.py:861
  80.8 44.7 %copy-start.1 = (bf16[4,13,16,512]{3,2,1,0:T(8,128)(2,1)}, bf16[4,13,16,512]{3,2,1,0:T(8,128)(2,1)S(1)}, u32[]{:S(2)}) copy-start(bf16[4,13,16,512]{3,2,1,0:T(8,128)(2,1)S(1)} %pad_maximum_fusion) | copy-start | bytes 2555908
  80.8 2.4 collective-permute-start.13
  80.9 4.2 collective-permute-start.14
  81.4 4.8 %collective-permute-start.15 = (bf16[2,4,5,16,512]{4,3,2,1,0:T(8,128)(2,1)S(1)}, bf16[2,4,5,16,512]{4,3,2,1,0:T(8,128)(2,1)}, u32[]{:S(2)}, u32[]{:S(2)}) collective-permute-start(bf16[2,4,5,16,512]{4,3,2,1,0:T(8,128)(2,1)S(1)} %pad_maximum_fusion.3.refs_2_), channel_id=1, source_target_pairs={{0,1},{1,0},{2,3},{3,2},{4,5},{5,4},{6,7},{7,6},{8,9},{9,8},{10,11... | collective-permute-start | bytes 1966088 | tf_op jit(solution)/shard_map/ppermute | solution.py:861
  81.5 4.7 %collective-permute-start.16 = (bf16[2,4,5,16,512]{4,3,2,1,0:T(8,128)(2,1)}, bf16[2,4,5,16,512]{4,3,2,1,0:T(8,128)(2,1)}, u32[]{:S(2)}, u32[]{:S(2)}) collective-permute-start(bf16[2,4,5,16,512]{4,3,2,1,0:T(8,128)(2,1)} %collective-permute-done.9.refs_3_), channel_id=1, source_target_pairs={{0,1},{1,0},{2,3},{3,2},{4,5},{5,4},{6,7},{7,6},{8,9},{9,8},{10,11... | collective-permute-start | bytes 1966088 | tf_op jit(solution)/shard_map/ppermute | solution.py:861
  82.5 23.3 %collective-permute-start.10 = (bf16[1,4,13,16,512]{4,3,2,1,0:T(8,128)(2,1)S(1)}, bf16[1,4,13,16,512]{4,3,2,1,0:T(8,128)(2,1)S(1)}, u32[]{:S(2)}, u32[]{:S(2)}) collective-permute-start(bf16[1,4,13,16,512]{4,3,2,1,0:T(8,128)(2,1)S(1)} %bitcast.105), channel_id=1, source_target_pairs={{0,2},{1,3},{2,0},{3,1},{4,6},{5,7},{6,4},{7,5},{8,10},{9,11},{10,... | collective-permute-start | bytes 2555912 | tf_op jit(solution)/shard_map/ppermute | solution.py:861
  83.2 43.4 %copy-start.14 = (s32[1,2]{1,0:T(1,128)S(1)}, s32[1,2]{1,0:T(1,128)}, u32[]{:S(2)}) copy-start(s32[1,2]{1,0:T(1,128)} %param.17) | copy-start | bytes 28
  83.2 45.8 %copy-start.15 = (f32[2]{0:T(128)S(1)}, f32[2]{0:T(128)}, u32[]{:S(2)}) copy-start(f32[2]{0:T(128)} %param.18) | copy-start | bytes 28
  83.2 48.8 %copy-start.9 = (bf16[2,1024]{1,0:T(2,128)(2,1)S(1)}, bf16[2,1024]{1,0:T(2,128)(2,1)}, u32[]{:S(2)}) copy-start(bf16[2,1024]{1,0:T(2,128)(2,1)} %param.15) | copy-start | bytes 12292
  83.2 285.3 %reduce-scatter.2.cloned.1.call-start = ((), (), s32[]{:S(2)}) async-start(), calls=%async_computation.3 | async-start | bytes 7241728 | tf_op jit(solution)/shard_map/reduce_scatter | solution.py:943
  83.3 22.6 %collective-permute-start.11 = (bf16[1,4,13,16,512]{4,3,2,1,0:T(8,128)(2,1)S(1)}, bf16[1,4,13,16,512]{4,3,2,1,0:T(8,128)(2,1)}, u32[]{:S(2)}, u32[]{:S(2)}) collective-permute-start(bf16[1,4,13,16,512]{4,3,2,1,0:T(8,128)(2,1)S(1)} %bitcast.106), channel_id=1, source_target_pairs={{0,16},{1,17},{2,18},{3,19},{4,20},{5,21},{6,22},{7,23},{8,24},{9,... | collective-permute-start | bytes 2555912 | tf_op jit(solution)/shard_map/ppermute | solution.py:861
  85.1 40.4 %collective-permute-start.12 = (bf16[1,4,13,16,512]{4,3,2,1,0:T(8,128)(2,1)S(1)}, bf16[1,4,13,16,512]{4,3,2,1,0:T(8,128)(2,1)}, u32[]{:S(2)}, u32[]{:S(2)}) collective-permute-start(bf16[1,4,13,16,512]{4,3,2,1,0:T(8,128)(2,1)S(1)} %bitcast.107), channel_id=1, source_target_pairs={{0,18},{1,19},{2,16},{3,17},{4,22},{5,23},{6,20},{7,21},{8,26},{9,... | collective-permute-start | bytes 2555912 | tf_op jit(solution)/shard_map/ppermute | solution.py:861
  105.8 27.5 %copy-start.18 = (bf16[1,4,13,16,512]{4,3,2,1,0:T(8,128)(2,1)}, bf16[1,4,13,16,512]{4,3,2,1,0:T(8,128)(2,1)S(1)}, u32[]{:S(2)}) copy-start(bf16[1,4,13,16,512]{4,3,2,1,0:T(8,128)(2,1)S(1)} %collective-permute-done.10.refs_1_) | copy-start | bytes 2555908
  125.5 6.6 %collective-permute-start.17 = (bf16[1,4,13,16,512]{4,3,2,1,0:T(8,128)(2,1)S(1)}, bf16[1,4,13,16,512]{4,3,2,1,0:T(8,128)(2,1)S(1)}, u32[]{:S(2)}, u32[]{:S(2)}) collective-permute-start(bf16[1,4,13,16,512]{4,3,2,1,0:T(8,128)(2,1)S(1)} %bitcast.108), channel_id=1, source_target_pairs={{0,1},{1,0},{2,3},{3,2},{4,5},{5,4},{6,7},{7,6},{8,9},{9,8},{10,11... | collective-permute-start | bytes 2555912 | tf_op jit(solution)/shard_map/ppermute | solution.py:861
  125.5 6.6 %collective-permute-start.18 = (bf16[1,4,13,16,512]{4,3,2,1,0:T(8,128)(2,1)S(1)}, bf16[1,4,13,16,512]{4,3,2,1,0:T(8,128)(2,1)}, u32[]{:S(2)}, u32[]{:S(2)}) collective-permute-start(bf16[1,4,13,16,512]{4,3,2,1,0:T(8,128)(2,1)S(1)} %collective-permute-done.10.refs_1_), channel_id=1, source_target_pairs={{0,1},{1,0},{2,3},{3,2},{4,5},{5,4},{6,7},{7,6},{8,9},{9,8},{10,11... | collective-permute-start | bytes 2555912 | tf_op jit(solution)/shard_map/ppermute | solution.py:861
  126.0 6.1 %collective-permute-start.19 = (bf16[1,4,13,16,512]{4,3,2,1,0:T(8,128)(2,1)}, bf16[1,4,13,16,512]{4,3,2,1,0:T(8,128)(2,1)}, u32[]{:S(2)}, u32[]{:S(2)}) collective-permute-start(bf16[1,4,13,16,512]{4,3,2,1,0:T(8,128)(2,1)} %collective-permute-done.11.refs_2_), channel_id=1, source_target_pairs={{0,1},{1,0},{2,3},{3,2},{4,5},{5,4},{6,7},{7,6},{8,9},{9,8},{10,11... | collective-permute-start | bytes 2555912 | tf_op jit(solution)/shard_map/ppermute | solution.py:861
  126.0 6.6 %collective-permute-start.20 = (bf16[1,4,13,16,512]{4,3,2,1,0:T(8,128)(2,1)}, bf16[1,4,13,16,512]{4,3,2,1,0:T(8,128)(2,1)}, u32[]{:S(2)}, u32[]{:S(2)}) collective-permute-start(bf16[1,4,13,16,512]{4,3,2,1,0:T(8,128)(2,1)} %collective-permute-done.12.refs_3_), channel_id=1, source_target_pairs={{0,1},{1,0},{2,3},{3,2},{4,5},{5,4},{6,7},{7,6},{8,9},{9,8},{10,11... | collective-permute-start | bytes 2555912 | tf_op jit(solution)/shard_map/ppermute | solution.py:861
  289.3 15.9 %copy-start.21 = (s32[32]{0:T(128)S(1)}, s32[32]{0:T(128)}, u32[]{:S(2)}) copy-start(s32[32]{0:T(128)} %param.19) | copy-start | bytes 388
  289.3 17.2 %copy-start.8 = (f32[2,8,512]{2,1,0:T(8,128)S(1)}, f32[2,8,512]{2,1,0:T(8,128)}, u32[]{:S(2)}) copy-start(f32[2,8,512]{2,1,0:T(8,128)} %get-tuple-element.87) | copy-start | bytes 98308
  289.3 17.2 %copy-start.5 = (bf16[2,1024]{1,0:T(2,128)(2,1)S(1)}, bf16[2,1024]{1,0:T(2,128)(2,1)}, u32[]{:S(2)}) copy-start(bf16[2,1024]{1,0:T(2,128)(2,1)} %copy-done.4) | copy-start | bytes 12292
  289.3 17.2 %copy-start.13 = (f32[8,512]{1,0:T(8,128)S(1)}, f32[8,512]{1,0:T(8,128)}, u32[]{:S(2)}) copy-start(f32[8,512]{1,0:T(8,128)} %get-tuple-element.89) | copy-start | bytes 49156
  289.3 17.9 %copy-start.12 = (f32[8,512]{1,0:T(8,128)S(1)}, f32[8,512]{1,0:T(8,128)}, u32[]{:S(2)}) copy-start(f32[8,512]{1,0:T(8,128)} %get-tuple-element.90) | copy-start | bytes 49156
  305.1 4.7 %collective-permute-start.21 = (bf16[4,4,9,16,512]{4,3,2,1,0:T(8,128)(2,1)}, bf16[4,4,9,16,512]{4,3,2,1,0:T(8,128)(2,1)S(1)}, u32[]{:S(2)}, u32[]{:S(2)}) collective-permute-start(bf16[4,4,9,16,512]{4,3,2,1,0:T(8,128)(2,1)} %get-tuple-element.79), channel_id=1, source_target_pairs={{0,1},{1,0},{2,3},{3,2},{4,5},{5,4},{6,7},{7,6},{8,9},{9,8},{10,11... | collective-permute-start | bytes 7077896 | tf_op jit(solution)/shard_map/ppermute | solution.py:861
  313.5 28.4 %collective-permute-start.22 = (bf16[4,9,16,512]{3,2,1,0:T(8,128)(2,1)}, bf16[4,9,16,512]{3,2,1,0:T(8,128)(2,1)S(1)}, u32[]{:S(2)}, u32[]{:S(2)}) collective-permute-start(bf16[4,9,16,512]{3,2,1,0:T(8,128)(2,1)} %get-tuple-element.106), channel_id=1, source_target_pairs={{0,2},{1,3},{2,0},{3,1},{4,6},{5,7},{6,4},{7,5},{8,10},{9,11},{10,... | collective-permute-start | bytes 1769480 | tf_op jit(solution)/shard_map/ppermute | solution.py:861
  314.3 27.6 %collective-permute-start.23 = (bf16[4,9,16,512]{3,2,1,0:T(8,128)(2,1)}, bf16[4,9,16,512]{3,2,1,0:T(8,128)(2,1)S(1)}, u32[]{:S(2)}, u32[]{:S(2)}) collective-permute-start(bf16[4,9,16,512]{3,2,1,0:T(8,128)(2,1)} %get-tuple-element.105), channel_id=1, source_target_pairs={{0,16},{1,17},{2,18},{3,19},{4,20},{5,21},{6,22},{7,23},{8,24},{9,... | collective-permute-start | bytes 1769480 | tf_op jit(solution)/shard_map/ppermute | solution.py:861
  315.0 28.1 %collective-permute-start.24 = (bf16[4,9,16,512]{3,2,1,0:T(8,128)(2,1)S(1)}, bf16[4,9,16,512]{3,2,1,0:T(8,128)(2,1)S(1)}, u32[]{:S(2)}, u32[]{:S(2)}) collective-permute-start(bf16[4,9,16,512]{3,2,1,0:T(8,128)(2,1)S(1)} %get-tuple-element.104), channel_id=1, source_target_pairs={{0,18},{1,19},{2,16},{3,17},{4,22},{5,23},{6,20},{7,21},{8,26},{9,... | collective-permute-start | bytes 1769480 | tf_op jit(solution)/shard_map/ppermute | solution.py:861
  343.5 26.7 %collective-permute-start.25 = (bf16[9,16,512]{2,1,0:T(8,128)(2,1)S(1)}, bf16[9,16,512]{2,1,0:T(8,128)(2,1)S(1)}, u32[]{:S(2)}, u32[]{:S(2)}) collective-permute-start(bf16[9,16,512]{2,1,0:T(8,128)(2,1)S(1)} %get-tuple-element.84), channel_id=1, source_target_pairs={{0,4},{1,5},{2,6},{3,7},{4,0},{5,1},{6,2},{7,3},{8,12},{9,13},{10,... | collective-permute-start | bytes 442376 | tf_op jit(solution)/shard_map/ppermute | solution.py:861
  347.8 22.3 %collective-permute-start.26 = (bf16[9,16,512]{2,1,0:T(8,128)(2,1)S(1)}, bf16[9,16,512]{2,1,0:T(8,128)(2,1)S(1)}, u32[]{:S(2)}, u32[]{:S(2)}) collective-permute-start(bf16[9,16,512]{2,1,0:T(8,128)(2,1)S(1)} %get-tuple-element.85), channel_id=1, source_target_pairs={{0,8},{1,9},{2,10},{3,11},{4,12},{5,13},{6,14},{7,15},{8,0},{9,1},... | collective-permute-start | bytes 442376 | tf_op jit(solution)/shard_map/ppermute | solution.py:861
  347.8 22.3 %collective-permute-start.27 = (bf16[9,16,512]{2,1,0:T(8,128)(2,1)S(1)}, bf16[9,16,512]{2,1,0:T(8,128)(2,1)S(1)}, u32[]{:S(2)}, u32[]{:S(2)}) collective-permute-start(bf16[9,16,512]{2,1,0:T(8,128)(2,1)S(1)} %get-tuple-element.86), channel_id=1, source_target_pairs={{0,12},{1,13},{2,14},{3,15},{4,8},{5,9},{6,10},{7,11},{8,4},{9,5},... | collective-permute-start | bytes 442376 | tf_op jit(solution)/shard_map/ppermute | solution.py:861
  369.5 6.7 %collective-permute-start.28 = (bf16[13,16,512]{2,1,0:T(8,128)(2,1)S(1)}, bf16[13,16,512]{2,1,0:T(8,128)(2,1)S(1)}, u32[]{:S(2)}, u32[]{:S(2)}) collective-permute-start(bf16[13,16,512]{2,1,0:T(8,128)(2,1)S(1)} %dynamic-slice_bitcast_fusion), channel_id=1, source_target_pairs={{0,16},{1,17},{2,18},{3,19},{4,20},{5,21},{6,22},{7,23},{8,24},{9,... | collective-permute-start | bytes 638984 | tf_op jit(solution)/shard_map/ppermute | solution.py:861
  379.5 43.8 %copy-start.7 = (f32[13,32]{1,0:T(8,128)S(1)}, f32[13,32]{1,0:T(8,128)}, u32[]{:S(2)}) copy-start(f32[13,32]{1,0:T(8,128)} %param.25) | copy-start | bytes 4996
  379.5 43.8 %copy-start.10 = (f32[13,32]{1,0:T(8,128)S(1)}, f32[13,32]{1,0:T(8,128)}, u32[]{:S(2)}) copy-start(f32[13,32]{1,0:T(8,128)} %param.27) | copy-start | bytes 4996
  379.5 43.8 %copy-start.11 = (f32[13,32]{1,0:T(8,128)S(1)}, f32[13,32]{1,0:T(8,128)}, u32[]{:S(2)}) copy-start(f32[13,32]{1,0:T(8,128)} %param.26) | copy-start | bytes 4996
  379.5 42.6 %all-to-all-start.1 = ((bf16[32,41,512]{2,1,0:T(8,128)(2,1)}), bf16[32,41,512]{2,1,0:T(8,128)(2,1)S(1)}, u32[]{:S(2)}, u32[]{:S(2)}) async-start(bf16[32,41,512]{2,1,0:T(8,128)(2,1)} %maximum_maximum_fusion), calls=%async_computation.2 | async-start | bytes 3145728 | tf_op jit(solution)/shard_map/all_to_all | solution.py:968
  (7 other events, 28.9 us)
Sparse Core Ops, SparseCore 0:
  83.3 58.2 all-gather.2
  263.5 104.9 reduce-scatter.1

commit v4 on v3

--- a/solution.py
+++ b/solution.py
@@ -208,10 +208,10 @@
         copy.wait()
 
 
-def store_flat(out, block, grad):
+def store_flat(out, slot, grad):
     for n in range(PIECES):
         place = flat_place(n) * PIECE
-        out[n % 16, block, n // 16] = grad[place : place + PIECE]
+        out[slot, n % 16, n // 16] = grad[place : place + PIECE]
 
 
 def store_pieces(ids, keep, send, block, grad):
@@ -340,9 +340,12 @@
     parts = refs[:1]
     (
     r1, cot, vec, out, dr1, grads, sums, weights,
-    nhat, n3, n3t, q, k, v, da, dat, qt, kt, vt, att, dyb, dq, dk, dv, dn3, acc, sem,
+    nhat, n3, n3t, q, k, v, da, dat, qt, kt, vt, att, dyb, dq, dk, dv, dn3, acc, sem, flat, flat_sem,
     ) = refs[1:]
     step = pl.program_id(0)
+
+    def out_copy(n):
+        return pltpu.make_async_copy(flat.at[n], grads.at[:, 9 + n], flat_sem.at[n])
 
     @pl.when(step == 0)
     def _():
@@ -452,7 +455,8 @@
 
         @pl.when(step != 0)
         def _(n=n, term=term):
-            store_flat(grads, n, (acc[n] + term()).astype(BF16))
+            store_flat(flat, n, (acc[n] + term()).astype(BF16))
+            out_copy(n).start()
 
     def column_sums(c, totals):
         rows = rows_of(c, ROWS)
@@ -480,6 +484,11 @@
 
     chunks(HW // ROWS, back)
 
+    @pl.when(step != 0)
+    def _():
+        for n in range(4):
+            out_copy(n).wait()
+
 
 def split_three(value):
     high = value.astype(BF16)
@@ -614,19 +623,21 @@
             one(tap, 0)
 
 
-def two_taps(grad, act, others, out, slab, at):
+def two_taps(grad, act, others, out, slab, at, flat, sem):
     fill_taps(grad, act, slab, at)
 
+    def out_copy(tap):
+        return pltpu.make_async_copy(flat.at[tap % 2], out.at[:, tap], sem.at[tap % 2])
+
     @pl.when(pl.program_id(0) == pl.num_programs(0) - 1)
     def _():
-        out[:, pl.ds(9, 4)] = others[...]
-
-        def one(tap, _):
-            store_flat(out, tap, tap_grad(slab, at, tap))
-            return 0
-
         for tap in range(9):
-            one(tap, 0)
+            if tap > 1:
+                out_copy(tap - 2).wait()
+            store_flat(flat, tap % 2, tap_grad(slab, at, tap))
+            out_copy(tap).start()
+        out_copy(7).wait()
+        out_copy(8).wait()
 
 
 def bwd_one_data(ids, *refs):
@@ -703,7 +714,7 @@
     return jax.ShapeDtypeStruct(shape, kind)
 
 
-def call(body, images, in_specs, out_specs, out_shape, scratch, args, name, flops=20 * 10**9):
+def call(body, images, in_specs, out_specs, out_shape, scratch, args, name, flops=20 * 10**9, aliases=None):
     return pl.pallas_call(
         body,
         grid=(images,),
@@ -711,6 +722,7 @@
         out_specs=out_specs,
         out_shape=out_shape,
         scratch_shapes=scratch,
+        input_output_aliases=aliases or {},
         name=name,
         compiler_params=pltpu.CompilerParams(
             vmem_limit_bytes=VMEM_LIMIT, dimension_semantics=("arbitrary",)
@@ -725,7 +737,7 @@
 SEMS = pltpu.SemaphoreType.DMA((COPIES,))
 
 
-def layer(images, embeds, cotangent, weight, live, plan, gathered):
+def layer(images, emb, act, cotangent, weight, live, plan, gathered):
     chunk_one, planes_two, chunk_attn = gathered
     ids = plan.ids
     count = images.shape[0]
@@ -746,8 +758,6 @@
     )
     planes_two, h1 = lax.optimization_barrier((planes_two, h1))
     chunk_two = plan.gather_core(planes_two)
-    emb = embeds.astype(F32)
-    act = jax.nn.silu(emb).astype(BF16)
     act_rows = jnp.broadcast_to(act[:, None, :], (count, 16, EMB))
     a2, r1, nhat, stats = call(
         fwd_two, count, [SMEM] + PARTS + [IMAGE, IMAGE, per_image(16, EMB), VEC],
@@ -756,18 +766,20 @@
         [taps, maps, slab, SEMS, SEMS],
         (ids, *chunk_two, h1, images, act_rows, vectors), "second_conv",
     )
+    early = struct((16, 13, 2, PIECE, C), BF16)
     out, dr1, grads_attn, sums_attn = call(
         attention, count, [SMEM, SMEM, SMEM, ANY] + [IMAGE, IMAGE, VEC],
-        [IMAGE, IMAGE, whole(16, 4, 2, PIECE, C), whole(8, C)],
-        [big(BF16), big(F32), struct((16, 4, 2, PIECE, C), BF16), struct((8, C), F32)],
+        [IMAGE, IMAGE, ANY, whole(8, C)],
+        [big(BF16), big(F32), early, struct((8, C), F32)],
         [maps, full, low, lowt, low, low, low, low, lowt, lowt, lowt, lowt, lowt,
-         low, low, low, low, full, pltpu.VMEM((4, C, C), F32), SEMS],
+         low, low, low, low, full, pltpu.VMEM((4, C, C), F32), SEMS,
+         pltpu.VMEM((4, 16, 2, PIECE, C), BF16), pltpu.SemaphoreType.DMA((4,))],
         (ids, weight, live, chunk_attn, r1, cotangent, vectors), "attention", 80 * 10**9,
     )
     (early,) = call(
-        two_taps, count, [IMAGE, IMAGE, whole(16, 4, 2, PIECE, C)],
-        [whole(16, 13, 2, PIECE, C)], [struct((16, 13, 2, PIECE, C), BF16)],
-        [slabs, turned], (dr1, a2, grads_attn), "second_conv_taps",
+        two_taps, count, [IMAGE, IMAGE, ANY], [ANY], [early],
+        [slabs, turned, pltpu.VMEM((2, 16, 2, PIECE, C), BF16), pltpu.SemaphoreType.DMA((2,))],
+        (dr1, a2, grads_attn), "second_conv_taps", aliases={2: 0},
     )
     grads_early = plan.reduce_early(early)
     dr1, _ = lax.optimization_barrier((dr1, early))
@@ -795,7 +807,7 @@
     )
     grads_late = plan.reduce_late(planes, dx)
     grads = plan.finish_early(grads_late, grads_early)
-    map_terms = jnp.concatenate([act.astype(F32), dvec[:, 0], dvec[:, 1]], axis=1).astype(BF16)
+    map_terms = dvec[:, :2].astype(BF16)
     grad_vectors = jnp.concatenate([sums_one[:2], sums_two[:6], sums_attn[:5]], axis=0)
     return out, dx, demb[:, 0], grads, map_terms, grad_vectors
 
@@ -833,10 +845,8 @@
     new_first[0] = moment
     new_second[0] = square
     correction = 1.0 - MOMENT_DECAY**STEP
-    direction = split_two(
-        moment * (1.0 / correction) / (jnp.sqrt(square * (1.0 / correction)) + ADAM_EPS)
-    )
-    update = mm_two(mm, lefts, split_two(mm_two(mm_t, direction, rights)))
+    direction = moment * (1.0 / correction) / (jnp.sqrt(square * (1.0 / correction)) + ADAM_EPS)
+    update = mm(lefts[0], mm_t(direction.astype(BF16), rights[0]).astype(BF16))
     fresh = master[0] - rate[slot] * (update + WEIGHT_DECAY * master[0])
     new_master[0] = fresh
     low[0] = fresh.astype(BF16)
@@ -916,7 +926,7 @@
         shard = lax.axis_index("shard")
         self.ids = jnp.stack([shard % 2, self.rep * 2 + shard // 2 % 2, shard // 4])
 
-    def gather(self, master, vec_master, owner):
+    def gather(self, master, vec_master, owner, act):
         mat_dev = master.shape[0]
         rows = master.astype(BF16).reshape(mat_dev, 2, 2, 2, 4, PIECE, C)
         rows = lax.dynamic_index_in_dim(rows, self.rep, 2, keepdims=False)
@@ -927,14 +937,19 @@
         vec = jnp.pad(vec_master.astype(BF16), ((0, 16 - VECS), (0, C - width)))
         place = lax.axis_index("shard") * width
         vec = jnp.where(self.rep == 0, jnp.roll(vec, place, axis=1), jnp.zeros((), BF16))
+        rows = act.reshape(-1, C)
+        rows = jnp.pad(rows, ((0, PIECE - rows.shape[0]), (0, 0)))
+        attn = jnp.concatenate([blocks[22:26], rows[None]], axis=0)
         line_one = gather_line(jnp.concatenate([blocks[:9], vec[None]], axis=0))
         second, line_one = lax.optimization_barrier((blocks[9:22], line_one))
         first_one = gather_first(line_one)
         line_two = gather_line(second)
         planes_one = gather_second(first_one)
-        line_two, attn, planes_one = lax.optimization_barrier((line_two, blocks[22:26], planes_one))
+        line_two, attn, planes_one = lax.optimization_barrier((line_two, attn, planes_one))
         one = gather_core(planes_one)
-        return one, gather_plane(line_two), lax.all_gather(attn, AXES)
+        attn = lax.all_gather(attn, AXES)
+        acts = attn[:, 4, : act.size // C].reshape(-1, 2, C).transpose(1, 0, 2)
+        return one, gather_plane(line_two), attn, acts
 
     def gather_core(self, planes):
         return gather_core(planes)
@@ -967,7 +982,7 @@
         sent = jnp.concatenate([picked, terms, vec], axis=1)
         got = lax.all_to_all(jnp.concatenate([sent, sent]), AXES, 0, 0)
         split = mat_dev * PIECE
-        terms = got[:, split:-1].reshape(-1, 4, C).transpose(1, 0, 2)
+        terms = got[:, split:-1].reshape(-1, 2, C).transpose(1, 0, 2)
         vec = jnp.sum(got[:, -1, : VECS * width].astype(F32), axis=0)
         return got, terms, vec.reshape(VECS, width)
 
@@ -976,7 +991,7 @@
     def __init__(self):
         self.ids = jnp.zeros((3,), jnp.int32)
 
-    def gather(self, master, vec_master, owner):
+    def gather(self, master, vec_master, owner, act):
         slots = lax.all_gather(master.astype(BF16), "shard", axis=0, tiled=True)
         vec = lax.all_gather(vec_master.astype(BF16), "shard", axis=1, tiled=True)
         blocks = jnp.take(slots, owner[:BLOCKS], axis=0)
@@ -994,7 +1009,8 @@
         rows = jnp.zeros((C, C), BF16).at[:VECS].set(vec)
         one = parts(jnp.concatenate([blocks[:9], rows[None]], axis=0))
         flat = blocks[22:26].reshape(4, 2, 2, 2, 4, PIECE, C).transpose(2, 4, 3, 1, 0, 5, 6)
-        return one, parts(blocks[9:22]), flat.reshape(PIECES, 4, PIECE, C)
+        acts = lax.all_gather(act, AXES, axis=0, tiled=True).reshape(-1, 2, C).transpose(1, 0, 2)
+        return one, parts(blocks[9:22]), flat.reshape(PIECES, 4, PIECE, C), acts
 
     def gather_core(self, planes):
         return planes
@@ -1018,7 +1034,7 @@
         rows = lax.psum(mine, "rep").reshape(mat_dev, 2, 2, 2, 4, PIECE, C)
         got = rows.transpose(2, 4, 3, 1, 0, 5, 6).reshape(PIECES, mat_dev * PIECE, C)
         terms = lax.all_gather(map_terms, AXES, axis=0, tiled=True)
-        terms = terms.reshape(-1, 4, C).transpose(1, 0, 2)
+        terms = terms.transpose(1, 0, 2)
         vec = lax.psum_scatter(grad_vectors, "shard", scatter_dimension=1, tiled=True)
         return got, terms, lax.psum(vec, "rep")
 
@@ -1043,13 +1059,15 @@
     mats_all = mat_dev * lax.axis_size("shard")
     sizes = (lax.axis_size("rep"), lax.axis_size("shard"))
     plan = Split() if sizes == (2, 16) else Plain()
-    gathered = plan.gather(master, vec_master, owner)
+    emb = embeds.astype(F32)
+    act = jax.nn.silu(emb).astype(BF16)
+    *gathered, acts = plan.gather(master, vec_master, owner, act)
     slot_ids = jnp.arange(images.shape[0], dtype=jnp.int32)
     live = (slot_ids < counts[0, 0] + counts[0, 1]).astype(jnp.int32)
     weight = jnp.where(slot_ids < counts[0, 0], bucket_weight[0], bucket_weight[1])
     weight = jnp.where(live > 0, weight, 0.0)
     outputs, grad_images, grad_embeds, grads, map_terms, grad_vectors = layer(
-        images, embeds, cotangent, weight, live, plan, gathered
+        images, emb, act, cotangent, weight, live, plan, gathered
     )
     all_slots = block_slots(owner, mats_all)
     shard = lax.axis_index("shard")
@@ -1060,7 +1078,7 @@
         slot_block,
         step_rate,
         got,
-        terms,
+        jnp.concatenate([acts, terms], axis=0),
         (left_basis, right_basis, first_moment, second_moment, master),
     )
     correction = 1.0 - MOMENT_DECAY**STEP

time: 452 us -> 430 us (0.951)
  waiting for transfers between devices: 129 us -> 109 us
    reduce_scatter x1, waiting for transfers between devices: 17.3 us -> 0.02 us  [reduce_early(): return lax.psum_scatter(grads, 'shard', scatter_dimension=0, tiled=True)[0]]
    all_to_all x1, waiting for transfers between devices: 36.5 us -> 29.5 us  [own(): got = lax.all_to_all(jnp.concatenate([sent, sent]), AXES, 0, 0)]
  transfers between devices with their start and end apart: 33 -> 33, of which waited for: 14 -> 12; matrix products, arithmetic and copies ran while one was open for 4% -> 5% of each run, Pallas kernels for 24% -> 26%
where the time goes in v4:
time: 430 us; the launch traced here: 422 us
  Pallas kernels  225 us (52%)
  waiting for transfers between devices  109 us (25%)
  starting transfers between devices  42.7 us (10%)
  other arithmetic  16.5 us (4%)
  between operations  16.5 us (4%)
  local copies, waits for them, and re-layouts  12.6 us (3%)
    pallas_call x8, Pallas kernels, call(): pl.pallas_call(body, grid=(images,), in_specs=in_specs, out_specs=out_spe...  225 us
    ppermute x29, waiting for transfers between devices, swap(): return lax.ppermute(value, AXES, [(i, i ^ mask) for i in range(PIECES)])  65.4 us
    ppermute x29, starting transfers between devices, swap(): return lax.ppermute(value, AXES, [(i, i ^ mask) for i in range(PIECES)])  30.6 us
    all_to_all x1, waiting for transfers between devices, own(): got = lax.all_to_all(jnp.concatenate([sent, sent]), AXES, 0, 0)  29.5 us
    all_to_all x1, waiting for transfers between devices, gather(): slots = lax.all_to_all(rows, 'shard', 0, 0).reshape(16 * mat_dev, PIECE, C)  14.2 us
  transfers between devices with their start and end apart: 33, of which 12 were waited for; matrix products, arithmetic and copies ran while one was open for 5% of the time, Pallas kernels for 26%

profile of v4, /device:TPU:0, one launch (start us, length us, event | category | flops | bytes accessed | tf_op | source)
XLA Modules:
  0.0 422.2 jit_solution(17004764732607144552)
XLA Ops:
  7.2 1.7 convert_element_type.193
  9.0 0.8 copy.63
  9.8 7.4 %all-to-all-start = ((bf16[16,2,16,512]{3,2,1,0:T(8,128)(2,1)}), bf16[16,2,16,512]{3,2,1,0:T(8,128)(2,1)S(1)}, u32[]{:S(2)}, u32[]{:S(2)}) async-start(bf16[16,2,16,512]{3,2,1,0:T(8,128)(2,1)} %bitcast.10), calls=%async_computation | async-start | bytes 1048576 | tf_op jit(solution)/shard_map/all_to_all | solution.py:934
  17.5 14.2 %all-to-all-done = bf16[16,2,16,512]{3,2,1,0:T(8,128)(2,1)S(1)} async-done(((bf16[16,2,16,512]{3,2,1,0:T(8,128)(2,1)}), bf16[16,2,16,512]{3,2,1,0:T(8,128)(2,1)S(1)}, u32[]{:S(2)}, u32[]{:S(2)}) %all-to-all-start) | async-done | bytes 524320 | tf_op jit(solution)/shard_map/all_to_all | solution.py:934
  32.4 2.3 collective-permute-start.1
  34.8 2.1 collective-permute-start.2
  36.9 7.1 %collective-permute-done.1 = bf16[10,16,512]{2,1,0:T(8,128)(2,1)S(1)} collective-permute-done((bf16[10,16,512]{2,1,0:T(8,128)(2,1)S(1)}, bf16[10,16,512]{2,1,0:T(8,128)(2,1)S(1)}, u32[]{:S(2)}, u32[]{:S(2)}) %collective-permute-start.1) | collective-permute-done | bytes 163872 | tf_op jit(solution)/shard_map/ppermute | solution.py:871
  44.0 3.9 collective-permute-done.2
  48.1 1.6 collective-permute-start.6
  49.7 0.9 collective-permute-start.8
  50.6 6.9 %collective-permute-done.6 = bf16[4,5,16,512]{3,2,1,0:T(8,128)(2,1)S(1)} collective-permute-done((bf16[4,5,16,512]{3,2,1,0:T(8,128)(2,1)S(1)}, bf16[4,5,16,512]{3,2,1,0:T(8,128)(2,1)S(1)}, u32[]{:S(2)}, u32[]{:S(2)}) %collective-permute-start.6) | collective-permute-done | bytes 327712 | tf_op jit(solution)/shard_map/ppermute | solution.py:871
  58.8 1.1 collective-permute-start.9
  60.0 1.5 collective-permute-start.5
  61.4 3.5 collective-permute-start.4
  65.6 4.3 %collective-permute-done.5 = bf16[13,16,512]{2,1,0:T(8,128)(2,1)S(1)} collective-permute-done((bf16[13,16,512]{2,1,0:T(8,128)(2,1)S(1)}, bf16[13,16,512]{2,1,0:T(8,128)(2,1)S(1)}, u32[]{:S(2)}, u32[]{:S(2)}) %collective-permute-start.5) | collective-permute-done | bytes 213024 | tf_op jit(solution)/shard_map/ppermute | solution.py:871
  69.9 10.7 %collective-permute-done.4 = bf16[13,16,512]{2,1,0:T(8,128)(2,1)S(1)} collective-permute-done((bf16[13,16,512]{2,1,0:T(8,128)(2,1)S(1)}, bf16[13,16,512]{2,1,0:T(8,128)(2,1)S(1)}, u32[]{:S(2)}, u32[]{:S(2)}) %collective-permute-start.4) | collective-permute-done | bytes 213024 | tf_op jit(solution)/shard_map/ppermute | solution.py:871
  82.6 1.7 collective-permute-start.12
  84.3 1.5 collective-permute-start.11
  85.8 1.0 collective-permute-start.10
  86.8 19.6 %first_conv.1 = (f32[2,1024,512]{2,1,0:T(8,128)}, bf16[2,1024,512]{2,1,0:T(8,128)(2,1)}, f32[16,512]{1,0:T(8,128)}) custom-call(s32[3]{0:T(128)} %pad_add_fusion.ids, bf16[2,4,5,16,512]{4,3,2,1,0:T(8,128)(2,1)} %copy-done.2, bf16[2,4,5,16,512]{4,3,2,1,0:T(8,128)(2,1)} %collective-permute-done.7.refs_1_, bf16[2,4,5,16,512]{4,3,2,1,0:T(8,128)(2,1)} %copy-done.3, ...), custom_call_target="tpu_custom_call" | custom-call | flops 20000000000 | bytes 31457280 | tf_op jit(solution)/shard_map/first_conv/pallas_call | solution.py:718
  106.4 19.5 %collective-permute-done.11.refs_2_ = bf16[1,4,13,16,512]{4,3,2,1,0:T(8,128)(2,1)} collective-permute-done((bf16[1,4,13,16,512]{4,3,2,1,0:T(8,128)(2,1)S(1)}, bf16[1,4,13,16,512]{4,3,2,1,0:T(8,128)(2,1)}, u32[]{:S(2)}, u32[]{:S(2)}) %collective-permute-start.11) | collective-permute-done | bytes 852000 | tf_op jit(solution)/shard_map/ppermute | solution.py:871
  130.0 2.5 compare_select_fusion.10.weight
  132.5 0.7 broadcast_in_dim.132.refs_10_
  133.7 23.2 %second_conv.1 = (bf16[2,1024,512]{2,1,0:T(8,128)(2,1)}, f32[2,1024,512]{2,1,0:T(8,128)}, f32[2,1024,512]{2,1,0:T(8,128)}, f32[2,8,512]{2,1,0:T(8,128)}) custom-call(s32[3]{0:T(128)} %pad_add_fusion.ids, bf16[1,4,13,16,512]{4,3,2,1,0:T(8,128)(2,1)} %bitcast.110, bf16[1,4,13,16,512]{4,3,2,1,0:T(8,128)(2,1)} %collective-permute-done.10.refs_1_, ...), custom_call_target="tpu_custom_call" | custom-call | flops 20000000000 | bytes 31457280 | tf_op jit(solution)/shard_map/second_conv/pallas_call | solution.py:718
  157.0 89.3 %attention.1 = (bf16[2,1024,512]{2,1,0:T(8,128)(2,1)}, f32[2,1024,512]{2,1,0:T(8,128)}, bf16[16,13,2,16,512]{4,3,2,1,0:T(8,128)(2,1)}, f32[8,512]{1,0:T(8,128)}) custom-call(s32[3]{0:T(128)} %pad_add_fusion.ids, f32[2]{0:T(128)} %compare_select_fusion.10.weight, s32[2]{0:T(128)} %compare_convert_fusion.live, bf16[32,5,16,512]{3,2,1,0:T(8,128)(2,1)} %bitcast.126, ...), custom_call_target="tpu_custom_call" | custom-call | flops 80000000000 | bytes 31457280 | tf_op jit(solution)/shard_map/attention/pallas_call | solution.py:718
  246.3 15.5 %second_conv_taps.1 = bf16[16,13,2,16,512]{4,3,2,1,0:T(8,128)(2,1)} custom-call(f32[2,1024,512]{2,1,0:T(8,128)} %get-tuple-element.73.grad.refs_8_.refs_10_, bf16[2,1024,512]{2,1,0:T(8,128)(2,1)} %get-tuple-element.71.act, bf16[16,13,2,16,512]{4,3,2,1,0:T(8,128)(2,1)} %get-tuple-element.72.others), custom_call_target="tpu_custom_call", output_to_operand_aliasing={{}: (2, {})} | custom-call | flops 20000000000 | bytes 31457280 | tf_op jit(solution)/shard_map/second_conv_taps/pallas_call | solution.py:718
  262.5 25.9 %second_conv_back.1 = (bf16[2,1024,512]{2,1,0:T(8,128)(2,1)}, f32[2,8,512]{2,1,0:T(8,128)}, f32[2,8,1024]{2,1,0:T(8,128)}, f32[8,512]{1,0:T(8,128)}) custom-call(s32[3]{0:T(128)} %pad_add_fusion.ids, bf16[1,4,13,16,512]{4,3,2,1,0:T(8,128)(2,1)} %bitcast.111, bf16[1,4,13,16,512]{4,3,2,1,0:T(8,128)(2,1)} %collective-permute-done.10.refs_1_, ...), custom_call_target="tpu_custom_call" | custom-call | flops 20000000000 | bytes 31457280 | tf_op jit(solution)/shard_map/second_conv_back/pallas_call | solution.py:718
  288.5 16.4 %first_conv_taps.1 = (bf16[4,4,9,16,512]{4,3,2,1,0:T(8,128)(2,1)}, bf16[4,4,9,16,512]{4,3,2,1,0:T(8,128)(2,1)}) custom-call(s32[3]{0:T(128)} %pad_add_fusion.ids, bf16[2,1024,512]{2,1,0:T(8,128)(2,1)} %get-tuple-element.80.grad.refs_8_, bf16[2,1024,512]{2,1,0:T(8,128)(2,1)} %get-tuple-element.77.act), custom_call_target="tpu_custom_call" | custom-call | flops 20000000000 | bytes 31457280 | tf_op jit(solution)/shard_map/first_conv_taps/pallas_call | solution.py:718
  306.3 0.8 slice.255
  307.9 1.8 collective-permute-done.21
  309.6 3.7 add_convert_fusion
  314.0 2.9 collective-permute-start.22
  316.8 24.1 %first_conv_back.1 = (f32[2,1024,512]{2,1,0:T(8,128)}, f32[8,512]{1,0:T(8,128)}) custom-call(s32[3]{0:T(128)} %pad_add_fusion.ids, bf16[2,4,5,16,512]{4,3,2,1,0:T(8,128)(2,1)} %copy-done.2, bf16[2,4,5,16,512]{4,3,2,1,0:T(8,128)(2,1)} %collective-permute-done.7.refs_1_, bf16[2,4,5,16,512]{4,3,2,1,0:T(8,128)(2,1)} %copy-done.3, ...), custom_call_target="tpu_custom_call" | custom-call | flops 20000000000 | bytes 31457280 | tf_op jit(solution)/shard_map/first_conv_back/pallas_call | solution.py:718
  340.9 0.7 slice.256
  341.8 5.3 %collective-permute-done.22 = bf16[4,9,16,512]{3,2,1,0:T(8,128)(2,1)S(1)} collective-permute-done((bf16[4,9,16,512]{3,2,1,0:T(8,128)(2,1)S(1)}, bf16[4,9,16,512]{3,2,1,0:T(8,128)(2,1)S(1)}, u32[]{:S(2)}, u32[]{:S(2)}) %collective-permute-start.22) | collective-permute-done | bytes 589856 | tf_op jit(solution)/shard_map/ppermute | solution.py:871
  347.6 4.3 %collective-permute-start.27 = (bf16[9,16,512]{2,1,0:T(8,128)(2,1)S(1)}, bf16[9,16,512]{2,1,0:T(8,128)(2,1)S(1)}, u32[]{:S(2)}, u32[]{:S(2)}) collective-permute-start(bf16[9,16,512]{2,1,0:T(8,128)(2,1)S(1)} %get-tuple-element.86), channel_id=1, source_target_pairs={{0,12},{1,13},{2,14},{3,15},{4,8},{5,9},{6,10},{7,11},{8,4},{9,5},... | collective-permute-start | bytes 442376 | tf_op jit(solution)/shard_map/ppermute | solution.py:871
  351.9 0.8 maximum_bitcast_fusion
  352.9 1.0 dynamic-slice_bitcast_fusion
  353.9 2.7 collective-permute-start.28
  356.6 5.3 %collective-permute-done.26 = bf16[9,16,512]{2,1,0:T(8,128)(2,1)S(1)} collective-permute-done((bf16[9,16,512]{2,1,0:T(8,128)(2,1)S(1)}, bf16[9,16,512]{2,1,0:T(8,128)(2,1)S(1)}, u32[]{:S(2)}, u32[]{:S(2)}) %collective-permute-start.26) | collective-permute-done | bytes 147488 | tf_op jit(solution)/shard_map/ppermute | solution.py:871
  362.0 1.0 fusion.4
  363.9 1.2 maximum_maximum_fusion
  365.1 4.6 %all-to-all-start.1 = ((bf16[32,37,512]{2,1,0:T(8,128)(2,1)}), bf16[32,37,512]{2,1,0:T(8,128)(2,1)S(1)}, u32[]{:S(2)}, u32[]{:S(2)}) async-start(bf16[32,37,512]{2,1,0:T(8,128)(2,1)} %maximum_maximum_fusion), calls=%async_computation.2 | async-start | bytes 2621440 | tf_op jit(solution)/shard_map/all_to_all | solution.py:983
  370.4 1.0 slice.208
  371.5 0.8 slice.151
  372.9 29.5 %all-to-all-done.1.got = bf16[32,37,512]{2,1,0:T(8,128)(2,1)S(1)} async-done(((bf16[32,37,512]{2,1,0:T(8,128)(2,1)}), bf16[32,37,512]{2,1,0:T(8,128)(2,1)S(1)}, u32[]{:S(2)}, u32[]{:S(2)}) %all-to-all-start.1) | async-done | bytes 1212448 | tf_op jit(solution)/shard_map/all_to_all | solution.py:983
  402.8 0.9 pad_maximum_fusion.5.terms
  404.3 10.7 %rotated_adam.1 = (f32[2,512,512]{2,1,0:T(8,128)}, f32[2,512,512]{2,1,0:T(8,128)}, f32[2,512,512]{2,1,0:T(8,128)}, bf16[2,512,512]{2,1,0:T(8,128)(2,1)}) custom-call(s32[2]{0:T(128)} %get-tuple-element.100.block, f32[2]{0:T(128)} %get-tuple-element.99.rate, bf16[32,37,512]{2,1,0:T(8,128)(2,1)} %copy-done, bf16[4,64,512]{2,1,0:T(8,128)(2,1)} %pad_maximum_fusion.5.terms, ...), custom_call_target="tpu_custom_call" | custom-call | flops 20000000000 | bytes 31457280 | tf_op jit(solution)/shard_map/rotated_adam/pallas_call | solution.py:718
  (144 shorter events, 15.8 us)
Async XLA Ops:
  8.9 8.4 %copy-start.4 = (f32[13,32]{1,0:T(8,128)S(1)}, f32[13,32]{1,0:T(8,128)}, u32[]{:S(2)}) copy-start(f32[13,32]{1,0:T(8,128)} %param.25) | copy-start | bytes 4996
  8.9 8.4 %copy-start.17 = (s32[32]{0:T(128)S(1)}, s32[32]{0:T(128)}, u32[]{:S(2)}) copy-start(s32[32]{0:T(128)} %param.19) | copy-start | bytes 388
  9.8 21.9 %all-to-all-start = ((bf16[16,2,16,512]{3,2,1,0:T(8,128)(2,1)}), bf16[16,2,16,512]{3,2,1,0:T(8,128)(2,1)S(1)}, u32[]{:S(2)}, u32[]{:S(2)}) async-start(bf16[16,2,16,512]{3,2,1,0:T(8,128)(2,1)} %bitcast.10), calls=%async_computation | async-start | bytes 1048576 | tf_op jit(solution)/shard_map/all_to_all | solution.py:934
  17.2 139.7 %all-gather.3.cloned.1.call-start = ((), (), s32[]{:S(2)}) async-start(), calls=%async_computation.4 | async-start | bytes 2703360 | tf_op jit(solution)/shard_map/all_gather | solution.py:950
  32.4 11.6 %collective-permute-start.1 = (bf16[10,16,512]{2,1,0:T(8,128)(2,1)S(1)}, bf16[10,16,512]{2,1,0:T(8,128)(2,1)S(1)}, u32[]{:S(2)}, u32[]{:S(2)}) collective-permute-start(bf16[10,16,512]{2,1,0:T(8,128)(2,1)S(1)} %get-tuple-element.116), channel_id=1, source_target_pairs={{0,8},{1,9},{2,10},{3,11},{4,12},{5,13},{6,14},{7,15},{8,0},{9,1},... | collective-permute-start | bytes 491528 | tf_op jit(solution)/shard_map/ppermute | solution.py:871
  34.7 9.3 %collective-permute-start = (bf16[10,16,512]{2,1,0:T(8,128)(2,1)S(1)}, bf16[10,16,512]{2,1,0:T(8,128)(2,1)S(1)}, u32[]{:S(2)}, u32[]{:S(2)}) collective-permute-start(bf16[10,16,512]{2,1,0:T(8,128)(2,1)S(1)} %get-tuple-element.116), channel_id=1, source_target_pairs={{0,4},{1,5},{2,6},{3,7},{4,0},{5,1},{6,2},{7,3},{8,12},{9,13},{10,... | collective-permute-start | bytes 491528 | tf_op jit(solution)/shard_map/ppermute | solution.py:871
  34.8 13.1 %collective-permute-start.2 = (bf16[10,16,512]{2,1,0:T(8,128)(2,1)S(1)}, bf16[10,16,512]{2,1,0:T(8,128)(2,1)S(1)}, u32[]{:S(2)}, u32[]{:S(2)}) collective-permute-start(bf16[10,16,512]{2,1,0:T(8,128)(2,1)S(1)} %get-tuple-element.116), channel_id=1, source_target_pairs={{0,12},{1,13},{2,14},{3,15},{4,8},{5,9},{6,10},{7,11},{8,4},{9,5},... | collective-permute-start | bytes 491528 | tf_op jit(solution)/shard_map/ppermute | solution.py:871
  47.9 12.0 %copy-start.6 = (bf16[2,1024]{1,0:T(2,128)(2,1)S(1)}, bf16[2,1024]{1,0:T(2,128)(2,1)}, u32[]{:S(2)}) copy-start(bf16[2,1024]{1,0:T(2,128)(2,1)} %param.15) | copy-start | bytes 12292
  48.1 9.4 %collective-permute-start.6 = (bf16[4,5,16,512]{3,2,1,0:T(8,128)(2,1)S(1)}, bf16[4,5,16,512]{3,2,1,0:T(8,128)(2,1)S(1)}, u32[]{:S(2)}, u32[]{:S(2)}) collective-permute-start(bf16[4,5,16,512]{3,2,1,0:T(8,128)(2,1)S(1)} %get-tuple-element.114), channel_id=1, source_target_pairs={{0,16},{1,17},{2,18},{3,19},{4,20},{5,21},{6,22},{7,23},{8,24},{9,... | collective-permute-start | bytes 983048 | tf_op jit(solution)/shard_map/ppermute | solution.py:871
  49.7 9.1 %collective-permute-start.8 = (bf16[4,5,16,512]{3,2,1,0:T(8,128)(2,1)S(1)}, bf16[4,5,16,512]{3,2,1,0:T(8,128)(2,1)S(1)}, u32[]{:S(2)}, u32[]{:S(2)}) collective-permute-start(bf16[4,5,16,512]{3,2,1,0:T(8,128)(2,1)S(1)} %get-tuple-element.113), channel_id=1, source_target_pairs={{0,2},{1,3},{2,0},{3,1},{4,6},{5,7},{6,4},{7,5},{8,10},{9,11},{10,... | collective-permute-start | bytes 983048 | tf_op jit(solution)/shard_map/ppermute | solution.py:871
  57.6 29.2 %copy-start.2 = (bf16[2,4,5,16,512]{4,3,2,1,0:T(8,128)(2,1)}, bf16[2,4,5,16,512]{4,3,2,1,0:T(8,128)(2,1)S(1)}, u32[]{:S(2)}) copy-start(bf16[2,4,5,16,512]{4,3,2,1,0:T(8,128)(2,1)S(1)} %pad_maximum_fusion.2.refs_0_) | copy-start | bytes 1966084
  57.6 23.2 %collective-permute-start.7 = (bf16[2,4,5,16,512]{4,3,2,1,0:T(8,128)(2,1)S(1)}, bf16[2,4,5,16,512]{4,3,2,1,0:T(8,128)(2,1)}, u32[]{:S(2)}, u32[]{:S(2)}) collective-permute-start(bf16[2,4,5,16,512]{4,3,2,1,0:T(8,128)(2,1)S(1)} %pad_maximum_fusion.2.refs_0_), channel_id=1, source_target_pairs={{0,2},{1,3},{2,0},{3,1},{4,6},{5,7},{6,4},{7,5},{8,10},{9,11},{10,... | collective-permute-start | bytes 1966088 | tf_op jit(solution)/shard_map/ppermute | solution.py:871
  58.8 28.0 %copy-start.3 = (bf16[2,4,5,16,512]{4,3,2,1,0:T(8,128)(2,1)}, bf16[2,4,5,16,512]{4,3,2,1,0:T(8,128)(2,1)S(1)}, u32[]{:S(2)}) copy-start(bf16[2,4,5,16,512]{4,3,2,1,0:T(8,128)(2,1)S(1)} %pad_maximum_fusion.3.refs_2_) | copy-start | bytes 1966084
  58.8 22.0 %collective-permute-start.9 = (bf16[2,4,5,16,512]{4,3,2,1,0:T(8,128)(2,1)S(1)}, bf16[2,4,5,16,512]{4,3,2,1,0:T(8,128)(2,1)}, u32[]{:S(2)}, u32[]{:S(2)}) collective-permute-start(bf16[2,4,5,16,512]{4,3,2,1,0:T(8,128)(2,1)S(1)} %pad_maximum_fusion.3.refs_2_), channel_id=1, source_target_pairs={{0,16},{1,17},{2,18},{3,19},{4,20},{5,21},{6,22},{7,23},{8,24},{9,... | collective-permute-start | bytes 1966088 | tf_op jit(solution)/shard_map/ppermute | solution.py:871
  60.0 9.9 %collective-permute-start.5 = (bf16[13,16,512]{2,1,0:T(8,128)(2,1)S(1)}, bf16[13,16,512]{2,1,0:T(8,128)(2,1)S(1)}, u32[]{:S(2)}, u32[]{:S(2)}) collective-permute-start(bf16[13,16,512]{2,1,0:T(8,128)(2,1)S(1)} %slice.181), channel_id=1, source_target_pairs={{0,12},{1,13},{2,14},{3,15},{4,8},{5,9},{6,10},{7,11},{8,4},{9,5},... | collective-permute-start | bytes 638984 | tf_op jit(solution)/shard_map/ppermute | solution.py:871
  61.4 19.2 %collective-permute-start.4 = (bf16[13,16,512]{2,1,0:T(8,128)(2,1)S(1)}, bf16[13,16,512]{2,1,0:T(8,128)(2,1)S(1)}, u32[]{:S(2)}, u32[]{:S(2)}) collective-permute-start(bf16[13,16,512]{2,1,0:T(8,128)(2,1)S(1)} %slice.181), channel_id=1, source_target_pairs={{0,8},{1,9},{2,10},{3,11},{4,12},{5,13},{6,14},{7,15},{8,0},{9,1},... | collective-permute-start | bytes 638984 | tf_op jit(solution)/shard_map/ppermute | solution.py:871
  65.0 15.7 %collective-permute-start.3 = (bf16[13,16,512]{2,1,0:T(8,128)(2,1)S(1)}, bf16[13,16,512]{2,1,0:T(8,128)(2,1)S(1)}, u32[]{:S(2)}, u32[]{:S(2)}) collective-permute-start(bf16[13,16,512]{2,1,0:T(8,128)(2,1)S(1)} %slice.181), channel_id=1, source_target_pairs={{0,4},{1,5},{2,6},{3,7},{4,0},{5,1},{6,2},{7,3},{8,12},{9,13},{10,... | collective-permute-start | bytes 638984 | tf_op jit(solution)/shard_map/ppermute | solution.py:871
  80.8 45.2 %copy-start.1 = (bf16[4,13,16,512]{3,2,1,0:T(8,128)(2,1)}, bf16[4,13,16,512]{3,2,1,0:T(8,128)(2,1)S(1)}, u32[]{:S(2)}) copy-start(bf16[4,13,16,512]{3,2,1,0:T(8,128)(2,1)S(1)} %pad_maximum_fusion) | copy-start | bytes 2555908
  80.8 3.5 collective-permute-start.13
  80.9 4.9 %collective-permute-start.14 = (bf16[2,4,5,16,512]{4,3,2,1,0:T(8,128)(2,1)}, bf16[2,4,5,16,512]{4,3,2,1,0:T(8,128)(2,1)}, u32[]{:S(2)}, u32[]{:S(2)}) collective-permute-start(bf16[2,4,5,16,512]{4,3,2,1,0:T(8,128)(2,1)} %collective-permute-done.7.refs_1_), channel_id=1, source_target_pairs={{0,1},{1,0},{2,3},{3,2},{4,5},{5,4},{6,7},{7,6},{8,9},{9,8},{10,11... | collective-permute-start | bytes 1966088 | tf_op jit(solution)/shard_map/ppermute | solution.py:871
  81.4 5.4 %collective-permute-start.15 = (bf16[2,4,5,16,512]{4,3,2,1,0:T(8,128)(2,1)S(1)}, bf16[2,4,5,16,512]{4,3,2,1,0:T(8,128)(2,1)}, u32[]{:S(2)}, u32[]{:S(2)}) collective-permute-start(bf16[2,4,5,16,512]{4,3,2,1,0:T(8,128)(2,1)S(1)} %pad_maximum_fusion.3.refs_2_), channel_id=1, source_target_pairs={{0,1},{1,0},{2,3},{3,2},{4,5},{5,4},{6,7},{7,6},{8,9},{9,8},{10,11... | collective-permute-start | bytes 1966088 | tf_op jit(solution)/shard_map/ppermute | solution.py:871
  81.5 5.3 %collective-permute-start.16 = (bf16[2,4,5,16,512]{4,3,2,1,0:T(8,128)(2,1)}, bf16[2,4,5,16,512]{4,3,2,1,0:T(8,128)(2,1)}, u32[]{:S(2)}, u32[]{:S(2)}) collective-permute-start(bf16[2,4,5,16,512]{4,3,2,1,0:T(8,128)(2,1)} %collective-permute-done.9.refs_3_), channel_id=1, source_target_pairs={{0,1},{1,0},{2,3},{3,2},{4,5},{5,4},{6,7},{7,6},{8,9},{9,8},{10,11... | collective-permute-start | bytes 1966088 | tf_op jit(solution)/shard_map/ppermute | solution.py:871
  81.9 271.0 %reduce-scatter.2.cloned.1.call-start = ((), (), s32[]{:S(2)}) async-start(), calls=%async_computation.3 | async-start | bytes 7241728 | tf_op jit(solution)/shard_map/reduce_scatter | solution.py:958
  82.6 44.4 %copy-start.11 = (s32[1,2]{1,0:T(1,128)S(1)}, s32[1,2]{1,0:T(1,128)}, u32[]{:S(2)}) copy-start(s32[1,2]{1,0:T(1,128)} %param.17) | copy-start | bytes 28
  82.6 46.9 %copy-start.12 = (f32[2]{0:T(128)S(1)}, f32[2]{0:T(128)}, u32[]{:S(2)}) copy-start(f32[2]{0:T(128)} %param.18) | copy-start | bytes 28
  82.6 23.8 %collective-permute-start.12 = (bf16[1,4,13,16,512]{4,3,2,1,0:T(8,128)(2,1)S(1)}, bf16[1,4,13,16,512]{4,3,2,1,0:T(8,128)(2,1)}, u32[]{:S(2)}, u32[]{:S(2)}) collective-permute-start(bf16[1,4,13,16,512]{4,3,2,1,0:T(8,128)(2,1)S(1)} %bitcast.106), channel_id=1, source_target_pairs={{0,18},{1,19},{2,16},{3,17},{4,22},{5,23},{6,20},{7,21},{8,26},{9,... | collective-permute-start | bytes 2555912 | tf_op jit(solution)/shard_map/ppermute | solution.py:871
  84.3 41.7 %collective-permute-start.11 = (bf16[1,4,13,16,512]{4,3,2,1,0:T(8,128)(2,1)S(1)}, bf16[1,4,13,16,512]{4,3,2,1,0:T(8,128)(2,1)}, u32[]{:S(2)}, u32[]{:S(2)}) collective-permute-start(bf16[1,4,13,16,512]{4,3,2,1,0:T(8,128)(2,1)S(1)} %bitcast.107), channel_id=1, source_target_pairs={{0,16},{1,17},{2,18},{3,19},{4,20},{5,21},{6,22},{7,23},{8,24},{9,... | collective-permute-start | bytes 2555912 | tf_op jit(solution)/shard_map/ppermute | solution.py:871
  85.8 40.2 %collective-permute-start.10 = (bf16[1,4,13,16,512]{4,3,2,1,0:T(8,128)(2,1)S(1)}, bf16[1,4,13,16,512]{4,3,2,1,0:T(8,128)(2,1)}, u32[]{:S(2)}, u32[]{:S(2)}) collective-permute-start(bf16[1,4,13,16,512]{4,3,2,1,0:T(8,128)(2,1)S(1)} %bitcast.108), channel_id=1, source_target_pairs={{0,2},{1,3},{2,0},{3,1},{4,6},{5,7},{6,4},{7,5},{8,10},{9,11},{10,... | collective-permute-start | bytes 2555912 | tf_op jit(solution)/shard_map/ppermute | solution.py:871
  126.0 6.5 %collective-permute-start.17 = (bf16[1,4,13,16,512]{4,3,2,1,0:T(8,128)(2,1)S(1)}, bf16[1,4,13,16,512]{4,3,2,1,0:T(8,128)(2,1)S(1)}, u32[]{:S(2)}, u32[]{:S(2)}) collective-permute-start(bf16[1,4,13,16,512]{4,3,2,1,0:T(8,128)(2,1)S(1)} %bitcast.109), channel_id=1, source_target_pairs={{0,1},{1,0},{2,3},{3,2},{4,5},{5,4},{6,7},{7,6},{8,9},{9,8},{10,11... | collective-permute-start | bytes 2555912 | tf_op jit(solution)/shard_map/ppermute | solution.py:871
  126.0 6.5 %collective-permute-start.18 = (bf16[1,4,13,16,512]{4,3,2,1,0:T(8,128)(2,1)}, bf16[1,4,13,16,512]{4,3,2,1,0:T(8,128)(2,1)S(1)}, u32[]{:S(2)}, u32[]{:S(2)}) collective-permute-start(bf16[1,4,13,16,512]{4,3,2,1,0:T(8,128)(2,1)} %collective-permute-done.10.refs_1_), channel_id=1, source_target_pairs={{0,1},{1,0},{2,3},{3,2},{4,5},{5,4},{6,7},{7,6},{8,9},{9,8},{10,11... | collective-permute-start | bytes 2555912 | tf_op jit(solution)/shard_map/ppermute | solution.py:871
  126.5 6.0 %collective-permute-start.19 = (bf16[1,4,13,16,512]{4,3,2,1,0:T(8,128)(2,1)}, bf16[1,4,13,16,512]{4,3,2,1,0:T(8,128)(2,1)}, u32[]{:S(2)}, u32[]{:S(2)}) collective-permute-start(bf16[1,4,13,16,512]{4,3,2,1,0:T(8,128)(2,1)} %collective-permute-done.11.refs_2_), channel_id=1, source_target_pairs={{0,1},{1,0},{2,3},{3,2},{4,5},{5,4},{6,7},{7,6},{8,9},{9,8},{10,11... | collective-permute-start | bytes 2555912 | tf_op jit(solution)/shard_map/ppermute | solution.py:871
  126.6 6.0 %collective-permute-start.20 = (bf16[1,4,13,16,512]{4,3,2,1,0:T(8,128)(2,1)}, bf16[1,4,13,16,512]{4,3,2,1,0:T(8,128)(2,1)}, u32[]{:S(2)}, u32[]{:S(2)}) collective-permute-start(bf16[1,4,13,16,512]{4,3,2,1,0:T(8,128)(2,1)} %collective-permute-done.12.refs_3_), channel_id=1, source_target_pairs={{0,1},{1,0},{2,3},{3,2},{4,5},{5,4},{6,7},{7,6},{8,9},{9,8},{10,11... | collective-permute-start | bytes 2555912 | tf_op jit(solution)/shard_map/ppermute | solution.py:871
  288.4 16.5 %copy-start.18 = (s32[32]{0:T(128)S(1)}, s32[32]{0:T(128)}, u32[]{:S(2)}) copy-start(s32[32]{0:T(128)} %param.19) | copy-start | bytes 388
  288.5 17.1 %copy-start.9 = (f32[8,512]{1,0:T(8,128)S(1)}, f32[8,512]{1,0:T(8,128)}, u32[]{:S(2)}) copy-start(f32[8,512]{1,0:T(8,128)} %get-tuple-element.90) | copy-start | bytes 49156
  288.5 18.7 %copy-start.10 = (f32[8,512]{1,0:T(8,128)S(1)}, f32[8,512]{1,0:T(8,128)}, u32[]{:S(2)}) copy-start(f32[8,512]{1,0:T(8,128)} %get-tuple-element.89) | copy-start | bytes 49156
  304.9 4.7 %collective-permute-start.21 = (bf16[4,4,9,16,512]{4,3,2,1,0:T(8,128)(2,1)}, bf16[4,4,9,16,512]{4,3,2,1,0:T(8,128)(2,1)S(1)}, u32[]{:S(2)}, u32[]{:S(2)}) collective-permute-start(bf16[4,4,9,16,512]{4,3,2,1,0:T(8,128)(2,1)} %get-tuple-element.79), channel_id=1, source_target_pairs={{0,1},{1,0},{2,3},{3,2},{4,5},{5,4},{6,7},{7,6},{8,9},{9,8},{10,11... | collective-permute-start | bytes 7077896 | tf_op jit(solution)/shard_map/ppermute | solution.py:871
  313.4 28.4 %collective-permute-start.24 = (bf16[4,9,16,512]{3,2,1,0:T(8,128)(2,1)}, bf16[4,9,16,512]{3,2,1,0:T(8,128)(2,1)S(1)}, u32[]{:S(2)}, u32[]{:S(2)}) collective-permute-start(bf16[4,9,16,512]{3,2,1,0:T(8,128)(2,1)} %get-tuple-element.104), channel_id=1, source_target_pairs={{0,18},{1,19},{2,16},{3,17},{4,22},{5,23},{6,20},{7,21},{8,26},{9,... | collective-permute-start | bytes 1769480 | tf_op jit(solution)/shard_map/ppermute | solution.py:871
  313.4 28.4 %collective-permute-start.23 = (bf16[4,9,16,512]{3,2,1,0:T(8,128)(2,1)}, bf16[4,9,16,512]{3,2,1,0:T(8,128)(2,1)S(1)}, u32[]{:S(2)}, u32[]{:S(2)}) collective-permute-start(bf16[4,9,16,512]{3,2,1,0:T(8,128)(2,1)} %get-tuple-element.105), channel_id=1, source_target_pairs={{0,16},{1,17},{2,18},{3,19},{4,20},{5,21},{6,22},{7,23},{8,24},{9,... | collective-permute-start | bytes 1769480 | tf_op jit(solution)/shard_map/ppermute | solution.py:871
  314.0 33.1 %collective-permute-start.22 = (bf16[4,9,16,512]{3,2,1,0:T(8,128)(2,1)S(1)}, bf16[4,9,16,512]{3,2,1,0:T(8,128)(2,1)S(1)}, u32[]{:S(2)}, u32[]{:S(2)}) collective-permute-start(bf16[4,9,16,512]{3,2,1,0:T(8,128)(2,1)S(1)} %get-tuple-element.106), channel_id=1, source_target_pairs={{0,2},{1,3},{2,0},{3,1},{4,6},{5,7},{6,4},{7,5},{8,10},{9,11},{10,... | collective-permute-start | bytes 1769480 | tf_op jit(solution)/shard_map/ppermute | solution.py:871
  347.5 9.1 %collective-permute-start.25 = (bf16[9,16,512]{2,1,0:T(8,128)(2,1)S(1)}, bf16[9,16,512]{2,1,0:T(8,128)(2,1)S(1)}, u32[]{:S(2)}, u32[]{:S(2)}) collective-permute-start(bf16[9,16,512]{2,1,0:T(8,128)(2,1)S(1)} %get-tuple-element.84), channel_id=1, source_target_pairs={{0,4},{1,5},{2,6},{3,7},{4,0},{5,1},{6,2},{7,3},{8,12},{9,13},{10,... | collective-permute-start | bytes 442376 | tf_op jit(solution)/shard_map/ppermute | solution.py:871
  347.5 14.4 %collective-permute-start.26 = (bf16[9,16,512]{2,1,0:T(8,128)(2,1)S(1)}, bf16[9,16,512]{2,1,0:T(8,128)(2,1)S(1)}, u32[]{:S(2)}, u32[]{:S(2)}) collective-permute-start(bf16[9,16,512]{2,1,0:T(8,128)(2,1)S(1)} %get-tuple-element.85), channel_id=1, source_target_pairs={{0,8},{1,9},{2,10},{3,11},{4,12},{5,13},{6,14},{7,15},{8,0},{9,1},... | collective-permute-start | bytes 442376 | tf_op jit(solution)/shard_map/ppermute | solution.py:871
  347.6 14.3 %collective-permute-start.27 = (bf16[9,16,512]{2,1,0:T(8,128)(2,1)S(1)}, bf16[9,16,512]{2,1,0:T(8,128)(2,1)S(1)}, u32[]{:S(2)}, u32[]{:S(2)}) collective-permute-start(bf16[9,16,512]{2,1,0:T(8,128)(2,1)S(1)} %get-tuple-element.86), channel_id=1, source_target_pairs={{0,12},{1,13},{2,14},{3,15},{4,8},{5,9},{6,10},{7,11},{8,4},{9,5},... | collective-permute-start | bytes 442376 | tf_op jit(solution)/shard_map/ppermute | solution.py:871
  353.9 8.1 %collective-permute-start.28 = (bf16[13,16,512]{2,1,0:T(8,128)(2,1)S(1)}, bf16[13,16,512]{2,1,0:T(8,128)(2,1)S(1)}, u32[]{:S(2)}, u32[]{:S(2)}) collective-permute-start(bf16[13,16,512]{2,1,0:T(8,128)(2,1)S(1)} %dynamic-slice_bitcast_fusion), channel_id=1, source_target_pairs={{0,16},{1,17},{2,18},{3,19},{4,20},{5,21},{6,22},{7,23},{8,24},{9,... | collective-permute-start | bytes 638984 | tf_op jit(solution)/shard_map/ppermute | solution.py:871
  363.9 5.8 %copy-start.14 = (s32[32]{0:T(128)S(1)}, s32[32]{0:T(128)}, u32[]{:S(2)}) copy-start(s32[32]{0:T(128)} %copy-done.13) | copy-start | bytes 388
  365.1 38.5 %copy-start.5 = (f32[13,32]{1,0:T(8,128)S(1)}, f32[13,32]{1,0:T(8,128)}, u32[]{:S(2)}) copy-start(f32[13,32]{1,0:T(8,128)} %param.25) | copy-start | bytes 4996
  365.1 38.5 %copy-start.7 = (f32[13,32]{1,0:T(8,128)S(1)}, f32[13,32]{1,0:T(8,128)}, u32[]{:S(2)}) copy-start(f32[13,32]{1,0:T(8,128)} %param.27) | copy-start | bytes 4996
  365.1 38.5 %copy-start.8 = (f32[13,32]{1,0:T(8,128)S(1)}, f32[13,32]{1,0:T(8,128)}, u32[]{:S(2)}) copy-start(f32[13,32]{1,0:T(8,128)} %param.26) | copy-start | bytes 4996
  365.1 37.3 %all-to-all-start.1 = ((bf16[32,37,512]{2,1,0:T(8,128)(2,1)}), bf16[32,37,512]{2,1,0:T(8,128)(2,1)S(1)}, u32[]{:S(2)}, u32[]{:S(2)}) async-start(bf16[32,37,512]{2,1,0:T(8,128)(2,1)} %maximum_maximum_fusion), calls=%async_computation.2 | async-start | bytes 2621440 | tf_op jit(solution)/shard_map/all_to_all | solution.py:983
  (4 other events, 4.5 us)
Sparse Core Ops, SparseCore 0:
  82.0 68.4 all-gather.2
  262.0 89.1 reduce-scatter.1

commit v5 on v4

--- a/solution.py
+++ b/solution.py
@@ -227,7 +227,8 @@
 
 
 def fwd_one(ids, *refs):
-    parts, (x, h1, a1, vec, weights, slab, held, sem, vec_sem) = refs[:8], refs[8:]
+    parts = refs[:8]
+    x, nhat, a1, stats, vec, weights, slab, hidden, held, sem, vec_sem = refs[8:]
     step = pl.program_id(0)
 
     def vec_copies():
@@ -276,17 +277,26 @@
         wait_all(ids, parts, weights, sem, 0, 9)
 
     def conv(c, _):
-        h1[0, rows_of(c, CONV_ROWS), :] = (
+        hidden[rows_of(c, CONV_ROWS), :] = (
             conv_rows(slab, (), weights, c * CONV_ROWS, CONV_ROWS, False) + vec[2:3]
         )
         return 0
 
     chunks(HW // CONV_ROWS, conv)
+    mean_two, inv_two = norm_stats(lambda rows: hidden[rows, :])
+    stats[0] = jnp.concatenate([mean, inv, inv_two, jnp.zeros((5, C), F32)], axis=0)
+
+    def normalize(c, _):
+        rows = rows_of(c, ROWS)
+        nhat[0, rows, :] = (hidden[rows, :] - mean_two) * inv_two
+        return 0
+
+    chunks(HW // ROWS, normalize)
 
 
 def fwd_two(ids, *refs):
     parts = refs[:8]
-    h1, x, act, vec, a2, r1, nhat, stats, weights, maps, slab, sem, map_sem = refs[8:]
+    nhat, x, act, vec, a2, r1, stats, weights, maps, slab, sem, map_sem = refs[8:]
     step = pl.program_id(0)
 
     @pl.when(step == 0)
@@ -295,8 +305,6 @@
         start_all(ids, parts, weights, sem, 0, 9)
         clear_pads(slab)
 
-    mean, inv = norm_stats(lambda rows: h1[0, rows, :])
-
     @pl.when(step == 0)
     def _():
         wait_all(ids, parts, maps, map_sem, 9, 4)
@@ -304,15 +312,13 @@
     row = act[0]
     scale = (mm(row[:, :C], maps[0]) + mm(row[:, C:], maps[1]))[0:1] + vec[3:4]
     shift = (mm(row[:, :C], maps[2]) + mm(row[:, C:], maps[3]))[0:1] + vec[4:5]
-    stats[0] = jnp.concatenate([scale, shift, inv, jnp.zeros((5, C), F32)], axis=0)
+    stats[0] = jnp.concatenate([scale, shift, jnp.zeros((6, C), F32)], axis=0)
     gain = vec[5:6]
     bias = vec[6:7]
 
     def activate(c, _):
         rows = rows_of(c, ROWS)
-        normed = (h1[0, rows, :] - mean) * inv
-        nhat[0, rows, :] = normed
-        pre = (normed * gain + bias) * (1.0 + scale) + shift
+        pre = (nhat[0, rows, :] * gain + bias) * (1.0 + scale) + shift
         act_two = pre * sigmoid(pre)
         a2[0, rows, :] = act_two.astype(BF16)
         store_slab(slab, (), c, act_two)
@@ -336,7 +342,7 @@
 MM_ROWS = 512
 
 
-def attention(ids, weight, live, *refs):
+def attention(ids, counts, bucket_weight, *refs):
     parts = refs[:1]
     (
     r1, cot, vec, out, dr1, grads, sums, weights,
@@ -355,7 +361,9 @@
     mean, inv = norm_stats(lambda rows: r1[0, rows, :])
     gain = vec[8:9]
     bias = vec[9:10]
-    image_weight = weight[step]
+    is_live = step < counts[0, 0] + counts[0, 1]
+    image_weight = jnp.where(step < counts[0, 0], bucket_weight[0], bucket_weight[1])
+    image_weight = jnp.where(is_live, image_weight, 0.0)
 
     def normalize(c, total):
         rows = rows_of(c, ROWS)
@@ -427,7 +435,6 @@
     dq[...] = dat[...].T
     q[...] = att[...].T
 
-    is_live = live[step] > 0
 
     def result(c, _):
         rows = rows_of(c, MM_ROWS)
@@ -499,8 +506,8 @@
 
 def bwd_two_data(ids, *refs):
     parts = refs[:8]
-    dr1, nhat, stats, vec, emb, dh1, dvec, demb, sums = refs[8:17]
-    weights, maps, slab, dz, sem, map_sem = refs[17:]
+    dr1, nhat, stats, norms, vec, emb, dh1, dvec, demb, sums = refs[8:18]
+    weights, maps, slab, dz, sem, map_sem = refs[18:]
     step = pl.program_id(0)
 
     @pl.when(step == 0)
@@ -526,7 +533,7 @@
 
     scale = 1.0 + stats[0, 0:1]
     shift = stats[0, 1:2]
-    inv = stats[0, 2:3]
+    inv = norms[0, 2:3]
     gain = vec[5:6]
     bias = vec[6:7]
 
@@ -641,7 +648,7 @@
 
 
 def bwd_one_data(ids, *refs):
-    parts, (dh1, x, dr1, vec, dx, sums, weights, slab, dp, sem) = refs[:8], refs[8:]
+    parts, (dh1, x, dr1, norms, vec, dx, sums, weights, slab, dp, sem) = refs[:8], refs[8:]
     step = pl.program_id(0)
 
     @pl.when(step == 0)
@@ -659,7 +666,7 @@
     def read(rows):
         return x[0, rows, :].astype(F32)
 
-    mean, inv = norm_stats(read)
+    mean, inv = norms[0, 0:1], norms[0, 1:2]
     gain = vec[0:1]
     bias = vec[1:2]
 
@@ -737,8 +744,8 @@
 SEMS = pltpu.SemaphoreType.DMA((COPIES,))
 
 
-def layer(images, emb, act, cotangent, weight, live, plan, gathered):
-    chunk_one, planes_two, chunk_attn = gathered
+def layer(images, emb_rows, act_rows, cotangent, counts, bucket_weight, plan, gathered):
+    images_one, chunk_one, planes_two, chunk_attn = gathered
     ids = plan.ids
     count = images.shape[0]
     big = lambda kind: struct((count, HW, C), kind)
@@ -750,21 +757,20 @@
     low = pltpu.VMEM((HW, C), BF16)
     lowt = pltpu.VMEM((C, HW), BF16)
     full = pltpu.VMEM((HW, C), F32)
-    h1, a1, vectors = call(
-        fwd_one, count, [SMEM] + PARTS + [IMAGE], [IMAGE, IMAGE, VEC],
-        [big(F32), big(BF16), struct((16, C), F32)],
-        [taps, slab, pltpu.VMEM((4, 2, 4, PIECE, C), BF16), SEMS, pltpu.SemaphoreType.DMA((4,))],
-        (ids, *chunk_one, images), "first_conv",
-    )
-    planes_two, h1 = lax.optimization_barrier((planes_two, h1))
+    nhat, a1, norms, vectors = call(
+        fwd_one, count, [SMEM] + PARTS + [IMAGE], [IMAGE, IMAGE, per_image(8, C), VEC],
+        [big(F32), big(BF16), struct((count, 8, C), F32), struct((16, C), F32)],
+        [taps, slab, full, pltpu.VMEM((4, 2, 4, PIECE, C), BF16), SEMS, pltpu.SemaphoreType.DMA((4,))],
+        (ids, *chunk_one, images_one), "first_conv",
+    )
+    planes_two, nhat = lax.optimization_barrier((planes_two, nhat))
     chunk_two = plan.gather_core(planes_two)
-    act_rows = jnp.broadcast_to(act[:, None, :], (count, 16, EMB))
-    a2, r1, nhat, stats = call(
+    a2, r1, stats = call(
         fwd_two, count, [SMEM] + PARTS + [IMAGE, IMAGE, per_image(16, EMB), VEC],
-        [IMAGE, IMAGE, IMAGE, per_image(8, C)],
-        [big(BF16), big(F32), big(F32), struct((count, 8, C), F32)],
+        [IMAGE, IMAGE, per_image(8, C)],
+        [big(BF16), big(F32), struct((count, 8, C), F32)],
         [taps, maps, slab, SEMS, SEMS],
-        (ids, *chunk_two, h1, images, act_rows, vectors), "second_conv",
+        (plan.ids_two, *chunk_two, nhat, images, act_rows, vectors), "second_conv",
     )
     early = struct((16, 13, 2, PIECE, C), BF16)
     out, dr1, grads_attn, sums_attn = call(
@@ -774,7 +780,7 @@
         [maps, full, low, lowt, low, low, low, low, lowt, lowt, lowt, lowt, lowt,
          low, low, low, low, full, pltpu.VMEM((4, C, C), F32), SEMS,
          pltpu.VMEM((4, 16, 2, PIECE, C), BF16), pltpu.SemaphoreType.DMA((4,))],
-        (ids, weight, live, chunk_attn, r1, cotangent, vectors), "attention", 80 * 10**9,
+        (ids, counts, bucket_weight, chunk_attn, r1, cotangent, vectors), "attention", 80 * 10**9,
     )
     (early,) = call(
         two_taps, count, [IMAGE, IMAGE, ANY], [ANY], [early],
@@ -783,14 +789,13 @@
     )
     grads_early = plan.reduce_early(early)
     dr1, _ = lax.optimization_barrier((dr1, early))
-    emb_rows = jnp.broadcast_to(emb[:, None, :], (count, 8, EMB))
     dh1, dvec, demb, sums_two = call(
         bwd_two_data, count,
-        [SMEM] + PARTS + [IMAGE, IMAGE, per_image(8, C), VEC, per_image(8, EMB)],
+        [SMEM] + PARTS + [IMAGE, IMAGE, per_image(8, C), per_image(8, C), VEC, per_image(8, EMB)],
         [IMAGE, per_image(8, C), per_image(8, EMB), whole(8, C)],
         [big(BF16), struct((count, 8, C), F32), struct((count, 8, EMB), F32), struct((8, C), F32)],
         [taps, maps, slab, full, SEMS, SEMS],
-        (ids, *chunk_two, dr1, nhat, stats, vectors, emb_rows), "second_conv_back",
+        (plan.ids_two, *chunk_two, dr1, nhat, stats, norms, vectors, emb_rows), "second_conv_back",
     )
     late = call(
         one_taps, count, [SMEM, IMAGE, IMAGE], [whole(4, 4, 9, PIECE, C)] * 2,
@@ -800,10 +805,11 @@
     planes = plan.reduce_core(*late)
     dh1, _ = lax.optimization_barrier((dh1, planes))
     dx, sums_one = call(
-        bwd_one_data, count, [SMEM] + PARTS + [IMAGE, IMAGE, IMAGE, VEC], [IMAGE, whole(8, C)],
+        bwd_one_data, count, [SMEM] + PARTS + [IMAGE, IMAGE, IMAGE, per_image(8, C), VEC],
+        [IMAGE, whole(8, C)],
         [big(F32), struct((8, C), F32)],
         [taps, slab, full, SEMS],
-        (ids, *chunk_one, dh1, images, dr1, vectors), "first_conv_back",
+        (ids, *chunk_one, dh1, images, dr1, norms, vectors), "first_conv_back",
     )
     grads_late = plan.reduce_late(planes, dx)
     grads = plan.finish_early(grads_late, grads_early)
@@ -895,8 +901,8 @@
     return [line] + [swap(line, mask) for mask in (2, 16, 18)]
 
 
-def gather_core(plane):
-    return plane + [swap(part, 1) for part in plane]
+def gather_core(planes, core):
+    return planes + [core[0], swap(planes[1], 1), core[1], swap(planes[3], 1)]
 
 
 def add_up(*terms):
@@ -925,14 +931,17 @@
         self.rep = lax.axis_index("rep")
         shard = lax.axis_index("shard")
         self.ids = jnp.stack([shard % 2, self.rep * 2 + shard // 2 % 2, shard // 4])
-
-    def gather(self, master, vec_master, owner, act):
+        self.ids_two = self.ids * jnp.array([1, 1, 0])
+
+    def gather(self, images, master, vec_master, owner, early):
         mat_dev = master.shape[0]
         rows = master.astype(BF16).reshape(mat_dev, 2, 2, 2, 4, PIECE, C)
         rows = lax.dynamic_index_in_dim(rows, self.rep, 2, keepdims=False)
         rows = rows.transpose(3, 2, 1, 0, 4, 5).reshape(16, mat_dev, PIECE, C)
         slots = lax.all_to_all(rows, "shard", 0, 0).reshape(16 * mat_dev, PIECE, C)
         blocks = jnp.take(slots, owner[:BLOCKS], axis=0)
+        early, blocks = lax.optimization_barrier((early, blocks))
+        act = early[0]
         width = vec_master.shape[1]
         vec = jnp.pad(vec_master.astype(BF16), ((0, 16 - VECS), (0, C - width)))
         place = lax.axis_index("shard") * width
@@ -943,16 +952,25 @@
         line_one = gather_line(jnp.concatenate([blocks[:9], vec[None]], axis=0))
         second, line_one = lax.optimization_barrier((blocks[9:22], line_one))
         first_one = gather_first(line_one)
-        line_two = gather_line(second)
+        groups = [[line * 4 + place for line in range(4)] for place in range(4)]
+        line_two = lax.all_to_all(
+            jnp.broadcast_to(second[None], (4,) + second.shape), "shard", 0, 0, axis_index_groups=groups
+        )
+        core_one = [swap(part, 1) for part in first_one]
         planes_one = gather_second(first_one)
-        line_two, attn, planes_one = lax.optimization_barrier((line_two, attn, planes_one))
-        one = gather_core(planes_one)
+        line_two, attn, planes_one, core_one = lax.optimization_barrier(
+            (line_two, attn, planes_one, core_one)
+        )
+        first_two = gather_first(line_two)
+        one = gather_core(planes_one, core_one)
+        images, first_two = lax.optimization_barrier((images, first_two))
+        core_two = [swap(part, 1) for part in first_two]
         attn = lax.all_gather(attn, AXES)
         acts = attn[:, 4, : act.size // C].reshape(-1, 2, C).transpose(1, 0, 2)
-        return one, gather_plane(line_two), attn, acts
+        return (*early, images, one, (gather_second(first_two), core_two), attn), acts
 
     def gather_core(self, planes):
-        return gather_core(planes)
+        return gather_core(*planes)
 
     def reduce_early(self, grads):
         return lax.psum_scatter(grads, "shard", scatter_dimension=0, tiled=True)[0]
@@ -989,9 +1007,10 @@
 
 class Plain:
     def __init__(self):
-        self.ids = jnp.zeros((3,), jnp.int32)
-
-    def gather(self, master, vec_master, owner, act):
+        self.ids = self.ids_two = jnp.zeros((3,), jnp.int32)
+
+    def gather(self, images, master, vec_master, owner, early):
+        act = early[0]
         slots = lax.all_gather(master.astype(BF16), "shard", axis=0, tiled=True)
         vec = lax.all_gather(vec_master.astype(BF16), "shard", axis=1, tiled=True)
         blocks = jnp.take(slots, owner[:BLOCKS], axis=0)
@@ -1010,7 +1029,8 @@
         one = parts(jnp.concatenate([blocks[:9], rows[None]], axis=0))
         flat = blocks[22:26].reshape(4, 2, 2, 2, 4, PIECE, C).transpose(2, 4, 3, 1, 0, 5, 6)
         acts = lax.all_gather(act, AXES, axis=0, tiled=True).reshape(-1, 2, C).transpose(1, 0, 2)
-        return one, parts(blocks[9:22]), flat.reshape(PIECES, 4, PIECE, C), acts
+        two, attn = parts(blocks[9:22]), flat.reshape(PIECES, 4, PIECE, C)
+        return (*early, images, one, two, attn), acts
 
     def gather_core(self, planes):
         return planes
@@ -1061,13 +1081,13 @@
     plan = Split() if sizes == (2, 16) else Plain()
     emb = embeds.astype(F32)
     act = jax.nn.silu(emb).astype(BF16)
-    *gathered, acts = plan.gather(master, vec_master, owner, act)
-    slot_ids = jnp.arange(images.shape[0], dtype=jnp.int32)
-    live = (slot_ids < counts[0, 0] + counts[0, 1]).astype(jnp.int32)
-    weight = jnp.where(slot_ids < counts[0, 0], bucket_weight[0], bucket_weight[1])
-    weight = jnp.where(live > 0, weight, 0.0)
+    act_rows = jnp.broadcast_to(act[:, None, :], act.shape[:1] + (16, EMB))
+    emb_rows = jnp.broadcast_to(emb[:, None, :], emb.shape[:1] + (8, EMB))
+    (act, act_rows, emb_rows, *gathered), acts = plan.gather(
+        images, master, vec_master, owner, (act, act_rows, emb_rows)
+    )
     outputs, grad_images, grad_embeds, grads, map_terms, grad_vectors = layer(
-        images, emb, act, cotangent, weight, live, plan, gathered
+        images, emb_rows, act_rows, cotangent, counts, bucket_weight, plan, gathered
     )
     all_slots = block_slots(owner, mats_all)
     shard = lax.axis_index("shard")

time: 430 us -> 427 us (level)
    reduce_scatter x1, waiting for transfers between devices: 0.02 us -> 7.43 us  [reduce_early(): return lax.psum_scatter(grads, 'shard', scatter_dimension=0, tiled=True)[0]]
    ppermute x29 -> x27, waiting for transfers between devices: 65.4 us -> 58.4 us  [swap(): return lax.ppermute(value, AXES, [(i, i ^ mask) for i in range(PIECES)])]
    all_to_all x0 -> x1, starting transfers between devices: none -> 4.54 us  [gather(): lax.all_to_all(jnp.broadcast_to(second[None], (4,) + second.shape), 'shar...]
    ppermute x29 -> x27, starting transfers between devices: 30.6 us -> 26.7 us  [swap(): return lax.ppermute(value, AXES, [(i, i ^ mask) for i in range(PIECES)])]
  transfers between devices with their start and end apart: 33 -> 32, of which waited for: 12 -> 18; matrix products, arithmetic and copies ran while one was open for 5% -> 4% of each run, Pallas kernels for 26% -> 26%
where the time goes in v5:
time: 427 us; the launch traced here: 419 us
  Pallas kernels  223 us (52%)
  waiting for transfers between devices  110 us (26%)
  starting transfers between devices  42.1 us (10%)
  between operations  15.2 us (4%)
  other arithmetic  14.4 us (3%)
  local copies, waits for them, and re-layouts  14 us (3%)
    pallas_call x8, Pallas kernels, call(): pl.pallas_call(body, grid=(images,), in_specs=in_specs, out_specs=out_spe...  223 us
    ppermute x27, waiting for transfers between devices, swap(): return lax.ppermute(value, AXES, [(i, i ^ mask) for i in range(PIECES)])  58.4 us
    all_to_all x1, waiting for transfers between devices, own(): got = lax.all_to_all(jnp.concatenate([sent, sent]), AXES, 0, 0)  29.6 us
    ppermute x27, starting transfers between devices, swap(): return lax.ppermute(value, AXES, [(i, i ^ mask) for i in range(PIECES)])  26.7 us
    all_to_all x1, waiting for transfers between devices, gather(): slots = lax.all_to_all(rows, 'shard', 0, 0).reshape(16 * mat_dev, PIECE, C)  14.2 us
  transfers between devices with their start and end apart: 32, of which 18 were waited for; matrix products, arithmetic and copies ran while one was open for 4% of the time, Pallas kernels for 26%

profile of v5, /device:TPU:0, one launch (start us, length us, event | category | flops | bytes accessed | tf_op | source)
XLA Modules:
  0.0 418.7 jit_solution(15050571785966899075)
XLA Ops:
  7.2 1.7 convert_element_type.191
  9.8 7.4 %all-to-all-start = ((bf16[16,2,16,512]{3,2,1,0:T(8,128)(2,1)}), bf16[16,2,16,512]{3,2,1,0:T(8,128)(2,1)S(1)}, u32[]{:S(2)}, u32[]{:S(2)}) async-start(bf16[16,2,16,512]{3,2,1,0:T(8,128)(2,1)} %bitcast.6), calls=%async_computation | async-start | bytes 1048576 | tf_op jit(solution)/shard_map/all_to_all | solution.py:941
  17.5 14.2 %all-to-all-done = bf16[16,2,16,512]{3,2,1,0:T(8,128)(2,1)S(1)} async-done(((bf16[16,2,16,512]{3,2,1,0:T(8,128)(2,1)}), bf16[16,2,16,512]{3,2,1,0:T(8,128)(2,1)S(1)}, u32[]{:S(2)}, u32[]{:S(2)}) %all-to-all-start) | async-done | bytes 524320 | tf_op jit(solution)/shard_map/all_to_all | solution.py:941
  33.7 2.3 collective-permute-start.1
  36.0 2.1 collective-permute-start.2
  38.2 7.1 %collective-permute-done.1 = bf16[10,16,512]{2,1,0:T(8,128)(2,1)S(1)} collective-permute-done((bf16[10,16,512]{2,1,0:T(8,128)(2,1)S(1)}, bf16[10,16,512]{2,1,0:T(8,128)(2,1)S(1)}, u32[]{:S(2)}, u32[]{:S(2)}) %collective-permute-start.1) | collective-permute-done | bytes 163872 | tf_op jit(solution)/shard_map/ppermute | solution.py:877
  45.3 3.9 collective-permute-done.2
  49.2 1.0 broadcast_in_dim.122
  50.2 4.5 %all-to-all-start.1 = ((bf16[4,13,16,512]{3,2,1,0:T(8,128)(2,1)}), bf16[4,13,16,512]{3,2,1,0:T(8,128)(2,1)S(1)}, u32[]{:S(2)}, u32[]{:S(2)}) async-start(bf16[4,13,16,512]{3,2,1,0:T(8,128)(2,1)} %broadcast_in_dim.122), calls=%async_computation.1 | async-start | bytes 1703936 | tf_op jit(solution)/shard_map/all_to_all | solution.py:956
  54.9 1.6 collective-permute-start.3
  57.2 7.0 %collective-permute-done.3 = bf16[4,5,16,512]{3,2,1,0:T(8,128)(2,1)S(1)} collective-permute-done((bf16[4,5,16,512]{3,2,1,0:T(8,128)(2,1)S(1)}, bf16[4,5,16,512]{3,2,1,0:T(8,128)(2,1)S(1)}, u32[]{:S(2)}, u32[]{:S(2)}) %collective-permute-start.3) | collective-permute-done | bytes 327712 | tf_op jit(solution)/shard_map/ppermute | solution.py:877
  64.3 1.0 collective-permute-start.4
  65.6 1.5 collective-permute-start.6
  67.8 13.8 %collective-permute-done.4.refs_1_ = bf16[2,4,5,16,512]{4,3,2,1,0:T(8,128)(2,1)} collective-permute-done((bf16[2,4,5,16,512]{4,3,2,1,0:T(8,128)(2,1)S(1)}, bf16[2,4,5,16,512]{4,3,2,1,0:T(8,128)(2,1)}, u32[]{:S(2)}, u32[]{:S(2)}) %collective-permute-start.4) | collective-permute-done | bytes 655392 | tf_op jit(solution)/shard_map/ppermute | solution.py:877
  81.6 1.2 collective-permute-done.6.refs_3_
  84.1 1.0 collective-permute-start.10
  85.3 1.6 collective-permute-start.9
  87.5 8.0 %collective-permute-done.10 = bf16[4,6,16,512]{3,2,1,0:T(8,128)(2,1)} collective-permute-done((bf16[4,6,16,512]{3,2,1,0:T(8,128)(2,1)}, bf16[4,6,16,512]{3,2,1,0:T(8,128)(2,1)}, u32[]{:S(2)}, u32[]{:S(2)}) %collective-permute-start.10) | collective-permute-done | bytes 393248 | tf_op jit(solution)/shard_map/ppermute | solution.py:877
  95.5 1.1 pad_maximum_fusion.1.refs_2_
  96.6 0.9 collective-permute-done.9
  97.7 2.1 collective-permute-start.12
  100.5 22.6 %first_conv.1 = (f32[2,1024,512]{2,1,0:T(8,128)}, bf16[2,1024,512]{2,1,0:T(8,128)(2,1)}, f32[2,8,512]{2,1,0:T(8,128)}, f32[16,512]{1,0:T(8,128)}) custom-call(s32[3]{0:T(128)} %get-tuple-element.124.ids, bf16[2,4,5,16,512]{4,3,2,1,0:T(8,128)(2,1)} %copy-done.3, bf16[2,4,5,16,512]{4,3,2,1,0:T(8,128)(2,1)} %collective-permute-done.4.refs_1_, ...), custom_call_target="tpu_custom_call" | custom-call | flops 20000000000 | bytes 31457280 | tf_op jit(solution)/shard_map/first_conv/pallas_call | solution.py:725
  124.4 3.1 collective-permute-done.18.refs_7_
  128.6 21.2 %second_conv.1 = (bf16[2,1024,512]{2,1,0:T(8,128)(2,1)}, f32[2,1024,512]{2,1,0:T(8,128)}, f32[2,8,512]{2,1,0:T(8,128)}) custom-call(s32[3]{0:T(128)} %get-tuple-element.123.ids, bf16[2,4,7,16,512]{4,3,2,1,0:T(8,128)(2,1)} %copy-done.1, bf16[2,4,7,16,512]{4,3,2,1,0:T(8,128)(2,1)} %copy-done.16, bf16[2,4,6,16,512]{4,3,2,1,0:T(8,128)(2,1)} %copy-done.2, ...), custom_call_target="tpu_custom_call" | custom-call | flops 20000000000 | bytes 31457280 | tf_op jit(solution)/shard_map/second_conv/pallas_call | solution.py:725
  149.9 89.3 %attention.1 = (bf16[2,1024,512]{2,1,0:T(8,128)(2,1)}, f32[2,1024,512]{2,1,0:T(8,128)}, bf16[16,13,2,16,512]{4,3,2,1,0:T(8,128)(2,1)}, f32[8,512]{1,0:T(8,128)}) custom-call(s32[3]{0:T(128)} %get-tuple-element.124.ids, s32[1,2]{1,0:T(1,128)} %counts.1, f32[2]{0:T(128)} %bucket_weight.1, bf16[32,5,16,512]{3,2,1,0:T(8,128)(2,1)} %bitcast.114, ...), custom_call_target="tpu_custom_call" | custom-call | flops 80000000000 | bytes 31457280 | tf_op jit(solution)/shard_map/attention/pallas_call | solution.py:725
  239.2 15.6 %second_conv_taps.1 = bf16[16,13,2,16,512]{4,3,2,1,0:T(8,128)(2,1)} custom-call(f32[2,1024,512]{2,1,0:T(8,128)} %get-tuple-element.94.grad.refs_8_.refs_10_, bf16[2,1024,512]{2,1,0:T(8,128)(2,1)} %get-tuple-element.92.act, bf16[16,13,2,16,512]{4,3,2,1,0:T(8,128)(2,1)} %get-tuple-element.93.others), custom_call_target="tpu_custom_call", output_to_operand_aliasing={{}: (2, {})} | custom-call | flops 20000000000 | bytes 31457280 | tf_op jit(solution)/shard_map/second_conv_taps/pallas_call | solution.py:725
  254.8 25.2 %second_conv_back.1 = (bf16[2,1024,512]{2,1,0:T(8,128)(2,1)}, f32[2,8,512]{2,1,0:T(8,128)}, f32[2,8,1024]{2,1,0:T(8,128)}, f32[8,512]{1,0:T(8,128)}) custom-call(s32[3]{0:T(128)} %get-tuple-element.123.ids, bf16[2,4,7,16,512]{4,3,2,1,0:T(8,128)(2,1)} %copy-done.1, bf16[2,4,7,16,512]{4,3,2,1,0:T(8,128)(2,1)} %copy-done.16, ...), custom_call_target="tpu_custom_call" | custom-call | flops 20000000000 | bytes 31457280 | tf_op jit(solution)/shard_map/second_conv_back/pallas_call | solution.py:725
  280.0 15.8 %first_conv_taps.1 = (bf16[4,4,9,16,512]{4,3,2,1,0:T(8,128)(2,1)}, bf16[4,4,9,16,512]{4,3,2,1,0:T(8,128)(2,1)}) custom-call(s32[3]{0:T(128)} %get-tuple-element.124.ids, bf16[2,1024,512]{2,1,0:T(8,128)(2,1)} %get-tuple-element.102.grad.refs_8_, bf16[2,1024,512]{2,1,0:T(8,128)(2,1)} %get-tuple-element.99.act), custom_call_target="tpu_custom_call" | custom-call | flops 20000000000 | bytes 31457280 | tf_op jit(solution)/shard_map/first_conv_taps/pallas_call | solution.py:725
  298.7 1.8 collective-permute-done.19
  300.5 3.7 add_convert_fusion
  304.7 1.7 collective-permute-start.21
  306.4 1.3 collective-permute-start.20
  307.7 22.9 %first_conv_back.1 = (f32[2,1024,512]{2,1,0:T(8,128)}, f32[8,512]{1,0:T(8,128)}) custom-call(s32[3]{0:T(128)} %get-tuple-element.124.ids, bf16[2,4,5,16,512]{4,3,2,1,0:T(8,128)(2,1)} %copy-done.3, bf16[2,4,5,16,512]{4,3,2,1,0:T(8,128)(2,1)} %collective-permute-done.4.refs_1_, bf16[2,4,5,16,512]{4,3,2,1,0:T(8,128)(2,1)} %copy-done.4, ...), custom_call_target="tpu_custom_call" | custom-call | flops 20000000000 | bytes 31457280 | tf_op jit(solution)/shard_map/first_conv_back/pallas_call | solution.py:725
  331.5 1.2 collective-permute-done.21
  332.7 5.3 %collective-permute-done.20 = bf16[4,9,16,512]{3,2,1,0:T(8,128)(2,1)S(1)} collective-permute-done((bf16[4,9,16,512]{3,2,1,0:T(8,128)(2,1)S(1)}, bf16[4,9,16,512]{3,2,1,0:T(8,128)(2,1)S(1)}, u32[]{:S(2)}, u32[]{:S(2)}) %collective-permute-start.20) | collective-permute-done | bytes 589856 | tf_op jit(solution)/shard_map/ppermute | solution.py:877
  338.3 2.5 collective-permute-start.23
  340.8 1.6 collective-permute-start.24
  344.2 7.4 %reduce-scatter.2.cloned.1.call-done = bf16[1,13,2,16,512]{4,3,2,1,0:T(8,128)(2,1)} async-done(((bf16[16,13,2,16,512]{4,3,2,1,0:T(8,128)(2,1)}), bf16[1,13,2,16,512]{4,3,2,1,0:T(8,128)(2,1)}) %reduce-scatter.2.cloned.1.call-update) | async-done | bytes 426000 | tf_op jit(solution)/shard_map/reduce_scatter | solution.py:976
  351.7 0.9 dynamic-slice_bitcast_fusion
  352.6 2.4 collective-permute-start.26
  355.1 1.7 collective-permute-done.25
  356.8 2.7 collective-permute-done.26
  359.6 1.0 fusion.4
  361.5 1.2 maximum_maximum_fusion
  362.7 3.5 all-to-all-start.2
  366.8 1.0 slice.196
  369.3 29.6 %all-to-all-done.2.got = bf16[32,37,512]{2,1,0:T(8,128)(2,1)S(1)} async-done(((bf16[32,37,512]{2,1,0:T(8,128)(2,1)}), bf16[32,37,512]{2,1,0:T(8,128)(2,1)S(1)}, u32[]{:S(2)}, u32[]{:S(2)}) %all-to-all-start.2) | async-done | bytes 1212448 | tf_op jit(solution)/shard_map/all_to_all | solution.py:1001
  400.8 10.7 %rotated_adam.1 = (f32[2,512,512]{2,1,0:T(8,128)}, f32[2,512,512]{2,1,0:T(8,128)}, f32[2,512,512]{2,1,0:T(8,128)}, bf16[2,512,512]{2,1,0:T(8,128)(2,1)}) custom-call(s32[2]{0:T(128)} %get-tuple-element.122.block, f32[2]{0:T(128)} %get-tuple-element.121.rate, bf16[32,37,512]{2,1,0:T(8,128)(2,1)} %copy-done, bf16[4,64,512]{2,1,0:T(8,128)(2,1)} %pad_maximum_fusion.6.terms, ...), custom_call_target="tpu_custom_call" | custom-call | flops 20000000000 | bytes 31457280 | tf_op jit(solution)/shard_map/rotated_adam/pallas_call | solution.py:725
  (152 shorter events, 21.6 us)
Async XLA Ops:
  8.9 8.3 %copy-start.5 = (f32[13,32]{1,0:T(8,128)S(1)}, f32[13,32]{1,0:T(8,128)}, u32[]{:S(2)}) copy-start(f32[13,32]{1,0:T(8,128)} %param.26) | copy-start | bytes 4996
  8.9 8.4 %copy-start.22 = (s32[32]{0:T(128)S(1)}, s32[32]{0:T(128)}, u32[]{:S(2)}) copy-start(s32[32]{0:T(128)} %param.20) | copy-start | bytes 388
  8.9 8.5 %copy-start.7 = (bf16[2,1024]{1,0:T(2,128)(2,1)S(1)}, bf16[2,1024]{1,0:T(2,128)(2,1)}, u32[]{:S(2)}) copy-start(bf16[2,1024]{1,0:T(2,128)(2,1)} %param.16) | copy-start | bytes 12292
  9.8 21.9 %all-to-all-start = ((bf16[16,2,16,512]{3,2,1,0:T(8,128)(2,1)}), bf16[16,2,16,512]{3,2,1,0:T(8,128)(2,1)S(1)}, u32[]{:S(2)}, u32[]{:S(2)}) async-start(bf16[16,2,16,512]{3,2,1,0:T(8,128)(2,1)} %bitcast.6), calls=%async_computation | async-start | bytes 1048576 | tf_op jit(solution)/shard_map/all_to_all | solution.py:941
  33.7 11.6 %collective-permute-start.1 = (bf16[10,16,512]{2,1,0:T(8,128)(2,1)S(1)}, bf16[10,16,512]{2,1,0:T(8,128)(2,1)S(1)}, u32[]{:S(2)}, u32[]{:S(2)}) collective-permute-start(bf16[10,16,512]{2,1,0:T(8,128)(2,1)S(1)} %get-tuple-element.144), channel_id=1, source_target_pairs={{0,8},{1,9},{2,10},{3,11},{4,12},{5,13},{6,14},{7,15},{8,0},{9,1},... | collective-permute-start | bytes 491528 | tf_op jit(solution)/shard_map/ppermute | solution.py:877
  36.0 9.3 %collective-permute-start = (bf16[10,16,512]{2,1,0:T(8,128)(2,1)S(1)}, bf16[10,16,512]{2,1,0:T(8,128)(2,1)S(1)}, u32[]{:S(2)}, u32[]{:S(2)}) collective-permute-start(bf16[10,16,512]{2,1,0:T(8,128)(2,1)S(1)} %get-tuple-element.144), channel_id=1, source_target_pairs={{0,4},{1,5},{2,6},{3,7},{4,0},{5,1},{6,2},{7,3},{8,12},{9,13},{10,... | collective-permute-start | bytes 491528 | tf_op jit(solution)/shard_map/ppermute | solution.py:877
  36.0 13.1 %collective-permute-start.2 = (bf16[10,16,512]{2,1,0:T(8,128)(2,1)S(1)}, bf16[10,16,512]{2,1,0:T(8,128)(2,1)S(1)}, u32[]{:S(2)}, u32[]{:S(2)}) collective-permute-start(bf16[10,16,512]{2,1,0:T(8,128)(2,1)S(1)} %get-tuple-element.144), channel_id=1, source_target_pairs={{0,12},{1,13},{2,14},{3,15},{4,8},{5,9},{6,10},{7,11},{8,4},{9,5},... | collective-permute-start | bytes 491528 | tf_op jit(solution)/shard_map/ppermute | solution.py:877
  50.2 32.6 %all-to-all-start.1 = ((bf16[4,13,16,512]{3,2,1,0:T(8,128)(2,1)}), bf16[4,13,16,512]{3,2,1,0:T(8,128)(2,1)S(1)}, u32[]{:S(2)}, u32[]{:S(2)}) async-start(bf16[4,13,16,512]{3,2,1,0:T(8,128)(2,1)} %broadcast_in_dim.122), calls=%async_computation.1 | async-start | bytes 1703936 | tf_op jit(solution)/shard_map/all_to_all | solution.py:956
  54.8 95.1 %all-gather.3.cloned.1.call-start = ((), (), s32[]{:S(2)}) async-start(), calls=%async_computation.5 | async-start | bytes 2703360 | tf_op jit(solution)/shard_map/all_gather | solution.py:968
  54.9 9.2 %collective-permute-start.3 = (bf16[4,5,16,512]{3,2,1,0:T(8,128)(2,1)S(1)}, bf16[4,5,16,512]{3,2,1,0:T(8,128)(2,1)S(1)}, u32[]{:S(2)}, u32[]{:S(2)}) collective-permute-start(bf16[4,5,16,512]{3,2,1,0:T(8,128)(2,1)S(1)} %get-tuple-element.142), channel_id=1, source_target_pairs={{0,16},{1,17},{2,18},{3,19},{4,20},{5,21},{6,22},{7,23},{8,24},{9,... | collective-permute-start | bytes 983048 | tf_op jit(solution)/shard_map/ppermute | solution.py:877
  56.5 8.9 %collective-permute-start.5 = (bf16[4,5,16,512]{3,2,1,0:T(8,128)(2,1)S(1)}, bf16[4,5,16,512]{3,2,1,0:T(8,128)(2,1)S(1)}, u32[]{:S(2)}, u32[]{:S(2)}) collective-permute-start(bf16[4,5,16,512]{3,2,1,0:T(8,128)(2,1)S(1)} %get-tuple-element.141), channel_id=1, source_target_pairs={{0,2},{1,3},{2,0},{3,1},{4,6},{5,7},{6,4},{7,5},{8,10},{9,11},{10,... | collective-permute-start | bytes 983048 | tf_op jit(solution)/shard_map/ppermute | solution.py:877
  64.2 21.1 %copy-start.3 = (bf16[2,4,5,16,512]{4,3,2,1,0:T(8,128)(2,1)}, bf16[2,4,5,16,512]{4,3,2,1,0:T(8,128)(2,1)S(1)}, u32[]{:S(2)}) copy-start(bf16[2,4,5,16,512]{4,3,2,1,0:T(8,128)(2,1)S(1)} %pad_maximum_fusion.3.refs_0_) | copy-start | bytes 1966084
  64.2 3.6 collective-permute-start.7
  64.3 17.3 %collective-permute-start.4 = (bf16[2,4,5,16,512]{4,3,2,1,0:T(8,128)(2,1)S(1)}, bf16[2,4,5,16,512]{4,3,2,1,0:T(8,128)(2,1)}, u32[]{:S(2)}, u32[]{:S(2)}) collective-permute-start(bf16[2,4,5,16,512]{4,3,2,1,0:T(8,128)(2,1)S(1)} %pad_maximum_fusion.3.refs_0_), channel_id=1, source_target_pairs={{0,2},{1,3},{2,0},{3,1},{4,6},{5,7},{6,4},{7,5},{8,10},{9,11},{10,... | collective-permute-start | bytes 1966088 | tf_op jit(solution)/shard_map/ppermute | solution.py:877
  65.4 21.6 %copy-start.14 = (s32[3]{0:T(128)S(1)}, s32[3]{0:T(128)}, u32[]{:S(2)}) copy-start(s32[3]{0:T(128)} %constant.162.clone) | copy-start | bytes 40
  65.4 31.2 %copy-start.4 = (bf16[2,4,5,16,512]{4,3,2,1,0:T(8,128)(2,1)}, bf16[2,4,5,16,512]{4,3,2,1,0:T(8,128)(2,1)S(1)}, u32[]{:S(2)}) copy-start(bf16[2,4,5,16,512]{4,3,2,1,0:T(8,128)(2,1)S(1)} %pad_maximum_fusion.4.refs_2_) | copy-start | bytes 1966084
  65.4 16.1 %collective-permute-start.8 = (bf16[2,4,5,16,512]{4,3,2,1,0:T(8,128)(2,1)S(1)}, bf16[2,4,5,16,512]{4,3,2,1,0:T(8,128)(2,1)S(1)}, u32[]{:S(2)}, u32[]{:S(2)}) collective-permute-start(bf16[2,4,5,16,512]{4,3,2,1,0:T(8,128)(2,1)S(1)} %pad_maximum_fusion.4.refs_2_), channel_id=1, source_target_pairs={{0,1},{1,0},{2,3},{3,2},{4,5},{5,4},{6,7},{7,6},{8,9},{9,8},{10,11... | collective-permute-start | bytes 1966088 | tf_op jit(solution)/shard_map/ppermute | solution.py:877
  65.6 17.2 %collective-permute-start.6 = (bf16[2,4,5,16,512]{4,3,2,1,0:T(8,128)(2,1)S(1)}, bf16[2,4,5,16,512]{4,3,2,1,0:T(8,128)(2,1)}, u32[]{:S(2)}, u32[]{:S(2)}) collective-permute-start(bf16[2,4,5,16,512]{4,3,2,1,0:T(8,128)(2,1)S(1)} %pad_maximum_fusion.4.refs_2_), channel_id=1, source_target_pairs={{0,16},{1,17},{2,18},{3,19},{4,20},{5,21},{6,22},{7,23},{8,24},{9,... | collective-permute-start | bytes 1966088 | tf_op jit(solution)/shard_map/ppermute | solution.py:877
  82.8 17.3 %collective-permute-start.15 = (bf16[2,4,5,16,512]{4,3,2,1,0:T(8,128)(2,1)}, bf16[2,4,5,16,512]{4,3,2,1,0:T(8,128)(2,1)}, u32[]{:S(2)}, u32[]{:S(2)}) collective-permute-start(bf16[2,4,5,16,512]{4,3,2,1,0:T(8,128)(2,1)} %collective-permute-done.4.refs_1_), channel_id=1, source_target_pairs={{0,1},{1,0},{2,3},{3,2},{4,5},{5,4},{6,7},{7,6},{8,9},{9,8},{10,11... | collective-permute-start | bytes 1966088 | tf_op jit(solution)/shard_map/ppermute | solution.py:877
  82.8 17.7 %collective-permute-start.16 = (bf16[2,4,5,16,512]{4,3,2,1,0:T(8,128)(2,1)}, bf16[2,4,5,16,512]{4,3,2,1,0:T(8,128)(2,1)}, u32[]{:S(2)}, u32[]{:S(2)}) collective-permute-start(bf16[2,4,5,16,512]{4,3,2,1,0:T(8,128)(2,1)} %collective-permute-done.6.refs_3_), channel_id=1, source_target_pairs={{0,1},{1,0},{2,3},{3,2},{4,5},{5,4},{6,7},{7,6},{8,9},{9,8},{10,11... | collective-permute-start | bytes 1966088 | tf_op jit(solution)/shard_map/ppermute | solution.py:877
  84.1 11.4 %collective-permute-start.10 = (bf16[4,6,16,512]{3,2,1,0:T(8,128)(2,1)}, bf16[4,6,16,512]{3,2,1,0:T(8,128)(2,1)}, u32[]{:S(2)}, u32[]{:S(2)}) collective-permute-start(bf16[4,6,16,512]{3,2,1,0:T(8,128)(2,1)} %get-tuple-element.136), channel_id=1, source_target_pairs={{0,2},{1,3},{2,0},{3,1},{4,6},{5,7},{6,4},{7,5},{8,10},{9,11},{10,... | collective-permute-start | bytes 1179656 | tf_op jit(solution)/shard_map/ppermute | solution.py:877
  85.3 12.3 %collective-permute-start.9 = (bf16[4,7,16,512]{3,2,1,0:T(8,128)(2,1)S(1)}, bf16[4,7,16,512]{3,2,1,0:T(8,128)(2,1)S(1)}, u32[]{:S(2)}, u32[]{:S(2)}) collective-permute-start(bf16[4,7,16,512]{3,2,1,0:T(8,128)(2,1)S(1)} %get-tuple-element.138), channel_id=1, source_target_pairs={{0,16},{1,17},{2,18},{3,19},{4,20},{5,21},{6,22},{7,23},{8,24},{9,... | collective-permute-start | bytes 1376264 | tf_op jit(solution)/shard_map/ppermute | solution.py:877
  86.9 264.8 %reduce-scatter.2.cloned.1.call-start = ((), (), s32[]{:S(2)}) async-start(), calls=%async_computation.4 | async-start | bytes 7241728 | tf_op jit(solution)/shard_map/reduce_scatter | solution.py:976
  96.6 26.4 %copy-start.2 = (bf16[2,4,6,16,512]{4,3,2,1,0:T(8,128)(2,1)}, bf16[2,4,6,16,512]{4,3,2,1,0:T(8,128)(2,1)S(1)}, u32[]{:S(2)}) copy-start(bf16[2,4,6,16,512]{4,3,2,1,0:T(8,128)(2,1)S(1)} %pad_maximum_fusion.1.refs_2_) | copy-start | bytes 2359300
  97.6 25.4 %copy-start.1 = (bf16[2,4,7,16,512]{4,3,2,1,0:T(8,128)(2,1)}, bf16[2,4,7,16,512]{4,3,2,1,0:T(8,128)(2,1)S(1)}, u32[]{:S(2)}) copy-start(bf16[2,4,7,16,512]{4,3,2,1,0:T(8,128)(2,1)S(1)} %pad_maximum_fusion.refs_0_) | copy-start | bytes 2752516
  97.7 25.4 %collective-permute-start.14 = (bf16[2,4,6,16,512]{4,3,2,1,0:T(8,128)(2,1)S(1)}, bf16[2,4,6,16,512]{4,3,2,1,0:T(8,128)(2,1)S(1)}, u32[]{:S(2)}, u32[]{:S(2)}) collective-permute-start(bf16[2,4,6,16,512]{4,3,2,1,0:T(8,128)(2,1)S(1)} %pad_maximum_fusion.1.refs_2_), channel_id=1, source_target_pairs={{0,1},{1,0},{2,3},{3,2},{4,5},{5,4},{6,7},{7,6},{8,9},{9,8},{10,11... | collective-permute-start | bytes 2359304 | tf_op jit(solution)/shard_map/ppermute | solution.py:877
  97.7 25.4 %collective-permute-start.12 = (bf16[2,4,6,16,512]{4,3,2,1,0:T(8,128)(2,1)S(1)}, bf16[2,4,6,16,512]{4,3,2,1,0:T(8,128)(2,1)S(1)}, u32[]{:S(2)}, u32[]{:S(2)}) collective-permute-start(bf16[2,4,6,16,512]{4,3,2,1,0:T(8,128)(2,1)S(1)} %pad_maximum_fusion.1.refs_2_), channel_id=1, source_target_pairs={{0,16},{1,17},{2,18},{3,19},{4,20},{5,21},{6,22},{7,23},{8,24},{9,... | collective-permute-start | bytes 2359304 | tf_op jit(solution)/shard_map/ppermute | solution.py:877
  99.9 23.3 %collective-permute-start.13 = (bf16[2,4,7,16,512]{4,3,2,1,0:T(8,128)(2,1)S(1)}, bf16[2,4,7,16,512]{4,3,2,1,0:T(8,128)(2,1)S(1)}, u32[]{:S(2)}, u32[]{:S(2)}) collective-permute-start(bf16[2,4,7,16,512]{4,3,2,1,0:T(8,128)(2,1)S(1)} %pad_maximum_fusion.refs_0_), channel_id=1, source_target_pairs={{0,1},{1,0},{2,3},{3,2},{4,5},{5,4},{6,7},{7,6},{8,9},{9,8},{10,11... | collective-permute-start | bytes 2752520 | tf_op jit(solution)/shard_map/ppermute | solution.py:877
  100.1 23.8 %collective-permute-start.11 = (bf16[2,4,7,16,512]{4,3,2,1,0:T(8,128)(2,1)S(1)}, bf16[2,4,7,16,512]{4,3,2,1,0:T(8,128)(2,1)S(1)}, u32[]{:S(2)}, u32[]{:S(2)}) collective-permute-start(bf16[2,4,7,16,512]{4,3,2,1,0:T(8,128)(2,1)S(1)} %pad_maximum_fusion.refs_0_), channel_id=1, source_target_pairs={{0,2},{1,3},{2,0},{3,1},{4,6},{5,7},{6,4},{7,5},{8,10},{9,11},{10,... | collective-permute-start | bytes 2752520 | tf_op jit(solution)/shard_map/ppermute | solution.py:877
  123.1 4.3 %copy-start.18 = (bf16[2,4,6,16,512]{4,3,2,1,0:T(8,128)(2,1)}, bf16[2,4,6,16,512]{4,3,2,1,0:T(8,128)(2,1)S(1)}, u32[]{:S(2)}) copy-start(bf16[2,4,6,16,512]{4,3,2,1,0:T(8,128)(2,1)S(1)} %collective-permute-done.14.refs_6_) | copy-start | bytes 2359300
  123.8 3.6 collective-permute-start.17
  123.8 3.6 collective-permute-start.18
  280.0 15.8 %copy-start.23 = (s32[32]{0:T(128)S(1)}, s32[32]{0:T(128)}, u32[]{:S(2)}) copy-start(s32[32]{0:T(128)} %param.20) | copy-start | bytes 388
  280.0 16.5 %copy-start.10 = (f32[8,512]{1,0:T(8,128)S(1)}, f32[8,512]{1,0:T(8,128)}, u32[]{:S(2)}) copy-start(f32[8,512]{1,0:T(8,128)} %get-tuple-element.112) | copy-start | bytes 49156
  280.0 18.0 %copy-start.11 = (f32[8,512]{1,0:T(8,128)S(1)}, f32[8,512]{1,0:T(8,128)}, u32[]{:S(2)}) copy-start(f32[8,512]{1,0:T(8,128)} %get-tuple-element.111) | copy-start | bytes 49156
  295.8 4.7 %collective-permute-start.19 = (bf16[4,4,9,16,512]{4,3,2,1,0:T(8,128)(2,1)}, bf16[4,4,9,16,512]{4,3,2,1,0:T(8,128)(2,1)S(1)}, u32[]{:S(2)}, u32[]{:S(2)}) collective-permute-start(bf16[4,4,9,16,512]{4,3,2,1,0:T(8,128)(2,1)} %get-tuple-element.101), channel_id=1, source_target_pairs={{0,1},{1,0},{2,3},{3,2},{4,5},{5,4},{6,7},{7,6},{8,9},{9,8},{10,11... | collective-permute-start | bytes 7077896 | tf_op jit(solution)/shard_map/ppermute | solution.py:877
  304.3 27.2 %collective-permute-start.22 = (bf16[4,9,16,512]{3,2,1,0:T(8,128)(2,1)}, bf16[4,9,16,512]{3,2,1,0:T(8,128)(2,1)S(1)}, u32[]{:S(2)}, u32[]{:S(2)}) collective-permute-start(bf16[4,9,16,512]{3,2,1,0:T(8,128)(2,1)} %get-tuple-element.128), channel_id=1, source_target_pairs={{0,18},{1,19},{2,16},{3,17},{4,22},{5,23},{6,20},{7,21},{8,26},{9,... | collective-permute-start | bytes 1769480 | tf_op jit(solution)/shard_map/ppermute | solution.py:877
  304.7 27.9 %collective-permute-start.21 = (bf16[4,9,16,512]{3,2,1,0:T(8,128)(2,1)}, bf16[4,9,16,512]{3,2,1,0:T(8,128)(2,1)S(1)}, u32[]{:S(2)}, u32[]{:S(2)}) collective-permute-start(bf16[4,9,16,512]{3,2,1,0:T(8,128)(2,1)} %get-tuple-element.129), channel_id=1, source_target_pairs={{0,16},{1,17},{2,18},{3,19},{4,20},{5,21},{6,22},{7,23},{8,24},{9,... | collective-permute-start | bytes 1769480 | tf_op jit(solution)/shard_map/ppermute | solution.py:877
  306.4 31.5 %collective-permute-start.20 = (bf16[4,9,16,512]{3,2,1,0:T(8,128)(2,1)S(1)}, bf16[4,9,16,512]{3,2,1,0:T(8,128)(2,1)S(1)}, u32[]{:S(2)}, u32[]{:S(2)}) collective-permute-start(bf16[4,9,16,512]{3,2,1,0:T(8,128)(2,1)S(1)} %get-tuple-element.130), channel_id=1, source_target_pairs={{0,2},{1,3},{2,0},{3,1},{4,6},{5,7},{6,4},{7,5},{8,10},{9,11},{10,... | collective-permute-start | bytes 1769480 | tf_op jit(solution)/shard_map/ppermute | solution.py:877
  338.3 16.7 %collective-permute-start.23 = (bf16[9,16,512]{2,1,0:T(8,128)(2,1)S(1)}, bf16[9,16,512]{2,1,0:T(8,128)(2,1)S(1)}, u32[]{:S(2)}, u32[]{:S(2)}) collective-permute-start(bf16[9,16,512]{2,1,0:T(8,128)(2,1)S(1)} %get-tuple-element.106), channel_id=1, source_target_pairs={{0,4},{1,5},{2,6},{3,7},{4,0},{5,1},{6,2},{7,3},{8,12},{9,13},{10,... | collective-permute-start | bytes 442376 | tf_op jit(solution)/shard_map/ppermute | solution.py:877
  340.8 14.2 %collective-permute-start.24 = (bf16[9,16,512]{2,1,0:T(8,128)(2,1)S(1)}, bf16[9,16,512]{2,1,0:T(8,128)(2,1)S(1)}, u32[]{:S(2)}, u32[]{:S(2)}) collective-permute-start(bf16[9,16,512]{2,1,0:T(8,128)(2,1)S(1)} %get-tuple-element.107), channel_id=1, source_target_pairs={{0,8},{1,9},{2,10},{3,11},{4,12},{5,13},{6,14},{7,15},{8,0},{9,1},... | collective-permute-start | bytes 442376 | tf_op jit(solution)/shard_map/ppermute | solution.py:877
  342.4 14.3 %collective-permute-start.25 = (bf16[9,16,512]{2,1,0:T(8,128)(2,1)S(1)}, bf16[9,16,512]{2,1,0:T(8,128)(2,1)S(1)}, u32[]{:S(2)}, u32[]{:S(2)}) collective-permute-start(bf16[9,16,512]{2,1,0:T(8,128)(2,1)S(1)} %get-tuple-element.108), channel_id=1, source_target_pairs={{0,12},{1,13},{2,14},{3,15},{4,8},{5,9},{6,10},{7,11},{8,4},{9,5},... | collective-permute-start | bytes 442376 | tf_op jit(solution)/shard_map/ppermute | solution.py:877
  352.6 7.0 %collective-permute-start.26 = (bf16[13,16,512]{2,1,0:T(8,128)(2,1)S(1)}, bf16[13,16,512]{2,1,0:T(8,128)(2,1)S(1)}, u32[]{:S(2)}, u32[]{:S(2)}) collective-permute-start(bf16[13,16,512]{2,1,0:T(8,128)(2,1)S(1)} %dynamic-slice_bitcast_fusion), channel_id=1, source_target_pairs={{0,16},{1,17},{2,18},{3,19},{4,20},{5,21},{6,22},{7,23},{8,24},{9,... | collective-permute-start | bytes 638984 | tf_op jit(solution)/shard_map/ppermute | solution.py:877
  361.5 4.7 %copy-start.13 = (s32[32]{0:T(128)S(1)}, s32[32]{0:T(128)}, u32[]{:S(2)}) copy-start(s32[32]{0:T(128)} %copy-done.12) | copy-start | bytes 388
  362.7 37.4 %copy-start.6 = (f32[13,32]{1,0:T(8,128)S(1)}, f32[13,32]{1,0:T(8,128)}, u32[]{:S(2)}) copy-start(f32[13,32]{1,0:T(8,128)} %param.26) | copy-start | bytes 4996
  362.7 37.4 %copy-start.8 = (f32[13,32]{1,0:T(8,128)S(1)}, f32[13,32]{1,0:T(8,128)}, u32[]{:S(2)}) copy-start(f32[13,32]{1,0:T(8,128)} %param.28) | copy-start | bytes 4996
  362.7 37.4 %copy-start.9 = (f32[13,32]{1,0:T(8,128)S(1)}, f32[13,32]{1,0:T(8,128)}, u32[]{:S(2)}) copy-start(f32[13,32]{1,0:T(8,128)} %param.27) | copy-start | bytes 4996
  362.7 36.3 %all-to-all-start.2 = ((bf16[32,37,512]{2,1,0:T(8,128)(2,1)}), bf16[32,37,512]{2,1,0:T(8,128)(2,1)S(1)}, u32[]{:S(2)}, u32[]{:S(2)}) async-start(bf16[32,37,512]{2,1,0:T(8,128)(2,1)} %maximum_maximum_fusion), calls=%async_computation.3 | async-start | bytes 2621440 | tf_op jit(solution)/shard_map/all_to_all | solution.py:1001
  (8 other events, 18.0 us)
Sparse Core Ops, SparseCore 0:
  87.0 59.4 all-gather.2
  254.9 96.7 reduce-scatter.1
